TPU v7x, 32 devices: a whole 2x2x4 slice. The times are simulated.
32 devices in a mesh: op: 2 (over core), sec: 16 (over z, y, x).
Axes of the slice: x: 2, y: 2, z: 4, core: 2. Of those that a mesh axis runs over, the one named last changes fastest.
Arguments:
- psi: bfloat16 [3, 128, 256, 256], P(None, 'sec'), may hold values from -6 to 6
- left_ops: bfloat16 [8, 128, 256, 256], P('op', 'sec'), may hold values from -0.125 to 0.125
- right_ops: bfloat16 [8, 128, 256, 256], P('op', 'sec'), may hold values from -0.375 to 0.375
- shifts: int32 [8], P('op'), may hold values from -1 to 1
- active: int32 [8, 128], P('op', 'sec'), may hold values 0 or 1
Outputs:
- right_view: bfloat16 [3, 256, 128, 256], P(None, 'sec', None, 'op')
All inputs are finite; a program needn't handle non-finite values. No bound on the sum of `active` on one device may be relied on, other than what follows from the above.
Results may differ from a plain program's by a relative error of at most 0.0049.
Values may be sent and summed in bfloat16 or wider, within the bound.
No kernel may reach another device: no remote copies, remote signals or barrier semaphores. Data moves between devices by JAX's collectives and lax.ppermute only.
A program may use at most 64 MiB of HBM per device.

v0:
```python
import jax
import jax.numpy as jnp
from jax import lax
from jax.sharding import PartitionSpec as P

QMAX = 1


def extended(value, sides, width):
    for axis, dim in sides:
        size, length = (lax.axis_size(axis), value.shape[dim])
        up = [(i, (i + 1) % size) for i in range(size - 1)]
        down = [(j, i) for i, j in up]
        last = lax.slice_in_dim(value, length - width, length, axis=dim)
        leading = lax.slice_in_dim(value, 0, width, axis=dim)
        before = lax.ppermute(last, axis, up)
        after = lax.ppermute(leading, axis, down)
        value = jnp.concatenate([before, value, after], axis=dim)
    return value


def per_device(psi, left_ops, right_ops, shifts, active):
    padded = extended(psi, (("sec", 1),), QMAX)
    count = left_ops.shape[0]
    sectors = psi.shape[1]
    nvec = psi.shape[0]
    blk = psi.shape[2]

    def add_term(index, total):
        start = QMAX - shifts[index]
        source = lax.dynamic_slice_in_dim(padded, start, sectors, 1)
        middle = jnp.einsum(
            "tij,vtjk->vtik", left_ops[index], source, preferred_element_type=jnp.float32
        ).astype(jnp.bfloat16)
        term = jnp.einsum(
            "vtik,tlk->vlti", middle, right_ops[index], preferred_element_type=jnp.float32
        )
        weight = active[index].astype(jnp.float32)
        return total + term * weight[None, None, :, None]

    total = lax.fori_loop(0, count, add_term, jnp.zeros((nvec, blk, sectors, blk), jnp.float32))
    summed = lax.psum(total, "op")
    share = blk // lax.axis_size("op")
    owned = lax.dynamic_slice_in_dim(summed, lax.axis_index("op") * share, share, 3)
    return lax.all_to_all(
        owned.astype(jnp.bfloat16), "sec", split_axis=1, concat_axis=2, tiled=True
    )


def solution(mesh):
    placed = (
        P(None, "sec", None, None),
        P("op", "sec", None, None),
        P("op", "sec", None, None),
        P("op"),
        P("op", "sec"),
    )
    return jax.shard_map(
        per_device,
        mesh=mesh,
        in_specs=placed,
        out_specs=P(None, "sec", None, "op"),
        check_vma=False,
    )
```

profile of v0, /device:TPU:0, one launch (start us, length us, event | category | flops | bytes accessed | tf_op | source)
XLA Modules:
  0.0 150.0 jit_solution(6220508223610330525)
XLA Ops:
  0.0 3.2 %copy.10 = bf16[3,8,256,256]{2,3,0,1:T(8,128)(2,1)S(1)} copy(bf16[3,8,256,256]{3,2,1,0:T(8,128)(2,1)} %param.7) | data formatting | bytes 6291456 | tf_op args[0]
  3.2 0.8 fusion.23
  4.0 5.6 %collective-permute-start = (bf16[3,1,256,256]{2,3,0,1:T(8,128)(2,1)}, bf16[3,1,256,256]{2,3,0,1:T(8,128)(2,1)}, u32[]{:S(2)}, u32[]{:S(2)}) collective-permute-start(bf16[3,1,256,256]{2,3,0,1:T(8,128)(2,1)} %get-tuple-element.220), channel_id=1, source_target_pairs={{0,1},{1,2},{2,3},{3,4},{4,5},{5,6},{6,7},{7,8},{8,9},{9,10},{10,1... | collective-permute-start | bytes 1179656 | tf_op jit(solution)/shard_map/ppermute | solution.py:16
  9.6 1.3 collective-permute-start.1
  10.9 0.0 copy-start
  10.9 15.0 %collective-permute-done = bf16[3,1,256,256]{2,3,0,1:T(8,128)(2,1)} collective-permute-done((bf16[3,1,256,256]{2,3,0,1:T(8,128)(2,1)}, bf16[3,1,256,256]{2,3,0,1:T(8,128)(2,1)}, u32[]{:S(2)}, u32[]{:S(2)}) %collective-permute-start) | collective-permute-done | bytes 393248 | tf_op jit(solution)/shard_map/ppermute | solution.py:16
  25.9 1.9 %collective-permute-done.1 = bf16[3,1,256,256]{2,3,0,1:T(8,128)(2,1)} collective-permute-done((bf16[3,1,256,256]{2,3,0,1:T(8,128)(2,1)S(1)}, bf16[3,1,256,256]{2,3,0,1:T(8,128)(2,1)}, u32[]{:S(2)}, u32[]{:S(2)}) %collective-permute-start.1) | collective-permute-done | bytes 393248 | tf_op jit(solution)/shard_map/ppermute | solution.py:17
  27.9 3.2 %pad_maximum_fusion = bf16[3,10,256,256]{2,3,0,1:T(8,128)(2,1)} fusion(bf16[3,1,256,256]{2,3,0,1:T(8,128)(2,1)} %collective-permute-done.1, bf16[3,8,256,256]{2,3,0,1:T(8,128)(2,1)S(1)} %copy.10, bf16[3,1,256,256]{2,3,0,1:T(8,128)(2,1)} %collective-permute-done), kind=kLoop, calls=%fused_computation.14 | loop fusion | flops 3932160 | bytes 7864320 | tf_op jit(solution)/shard_map/concatenate | solution.py:18
  31.1 0.0 copy-done
  31.1 44.0 %while.16 = (s32[]{:T(128)}, f32[3,256,8,256]{3,1,0,2:T(8,128)}, bf16[4,8,256,256]{3,2,1,0:T(8,128)(2,1)}, s32[4]{0:T(128)S(1)}, bf16[3,10,256,256]{2,3,0,1:T(8,...) while((s32[]{:T(128)}, f32[3,256,8,256]{3,1,0,2:T(8,128)}, ...), condition=%wide.region_1.0_spmd.clone, body=%wide.region_0.0_spmd.clone.sunk | while | flops 1616904192 | bytes 17827096 | solution.py:41
  31.1 0.6 dynamic_slice.91
  33.0 0.7 fusion.33
  33.7 7.0 %bitcast_add_fusion.2 = f32[3,256,8,256]{3,1,0,2:T(8,128)} fusion(f32[3,256,8,256]{3,1,0,2:T(8,128)} %get-tuple-element.277, f32[8]{0:T(128)S(1)} %fusion.33, pred[]{:T(512)S(6)} %compare.3, bf16[3,10,256,256]{2,3,0,1:T(8,128)(2,1)} %get-tuple-element.291, s32[]{:T(128)S(6)} %select_n.27, bf16[4,8,256,256]{3,2,1,0:T(8,128)(2,1)} %get-tuple-element.292, ...), kind=kOutput, calls=%fused_computation.clone.1 | convolution fusion | flops 1616904192 | bytes 17826852 | tf_op jit(solution)/shard_map/while/body/eval_jaxpr/vtik,tlk->vlti/dot_general | solution.py:35
  40.7 0.6 dynamic_slice.91
  42.6 0.7 fusion.33
  43.3 8.9 %bitcast_add_fusion.2 = f32[3,256,8,256]{3,1,0,2:T(8,128)} fusion(f32[3,256,8,256]{3,1,0,2:T(8,128)} %get-tuple-element.277, f32[8]{0:T(128)S(1)} %fusion.33, pred[]{:T(512)S(6)} %compare.3, bf16[3,10,256,256]{2,3,0,1:T(8,128)(2,1)} %get-tuple-element.291, s32[]{:T(128)S(6)} %select_n.27, bf16[4,8,256,256]{3,2,1,0:T(8,128)(2,1)} %get-tuple-element.292, ...), kind=kOutput, calls=%fused_computation.clone.1 | convolution fusion | flops 1616904192 | bytes 17826852 | tf_op jit(solution)/shard_map/while/body/eval_jaxpr/vtik,tlk->vlti/dot_general | solution.py:35
  52.2 0.6 dynamic_slice.91
  54.0 0.7 fusion.33
  54.7 8.9 %bitcast_add_fusion.2 = f32[3,256,8,256]{3,1,0,2:T(8,128)} fusion(f32[3,256,8,256]{3,1,0,2:T(8,128)} %get-tuple-element.277, f32[8]{0:T(128)S(1)} %fusion.33, pred[]{:T(512)S(6)} %compare.3, bf16[3,10,256,256]{2,3,0,1:T(8,128)(2,1)} %get-tuple-element.291, s32[]{:T(128)S(6)} %select_n.27, bf16[4,8,256,256]{3,2,1,0:T(8,128)(2,1)} %get-tuple-element.292, ...), kind=kOutput, calls=%fused_computation.clone.1 | convolution fusion | flops 1616904192 | bytes 17826852 | tf_op jit(solution)/shard_map/while/body/eval_jaxpr/vtik,tlk->vlti/dot_general | solution.py:35
  63.6 0.6 dynamic_slice.91
  65.5 0.7 fusion.33
  66.2 8.9 %bitcast_add_fusion.2 = f32[3,256,8,256]{3,1,0,2:T(8,128)} fusion(f32[3,256,8,256]{3,1,0,2:T(8,128)} %get-tuple-element.277, f32[8]{0:T(128)S(1)} %fusion.33, pred[]{:T(512)S(6)} %compare.3, bf16[3,10,256,256]{2,3,0,1:T(8,128)(2,1)} %get-tuple-element.291, s32[]{:T(128)S(6)} %select_n.27, bf16[4,8,256,256]{3,2,1,0:T(8,128)(2,1)} %get-tuple-element.292, ...), kind=kOutput, calls=%fused_computation.clone.1 | convolution fusion | flops 1616904192 | bytes 17826852 | tf_op jit(solution)/shard_map/while/body/eval_jaxpr/vtik,tlk->vlti/dot_general | solution.py:35
  75.1 9.1 %copy.13 = f32[3,256,8,256]{3,2,0,1:T(8,128)} copy(f32[3,256,8,256]{3,1,0,2:T(8,128)} %get-tuple-element.181) | data formatting | bytes 12582912 | tf_op jit(solution)/shard_map/while | solution.py:41
  84.2 20.3 %all-reduce.1 = bf16[3,256,8,256]{3,2,0,1:T(8,128)(2,1)S(1)} all-reduce(f32[3,256,8,256]{3,2,0,1:T(8,128)} %copy.13), channel_id=1, replica_groups=mesh['op'=2,'sec'=16] {'op'}, use_global_device_ids=true, to_apply=%region_2.0 | all-reduce | flops 1572864 | bytes 9437184 | tf_op jit(solution)/shard_map/psum | solution.py:42
  104.4 0.3 dynamic-slice_convert_fusion
  104.7 43.7 %all_to_all.18 = bf16[3,256,8,128]{3,2,0,1:T(8,128)(2,1)S(1)} all-to-all(bf16[3,256,8,128]{3,2,0,1:T(8,128)(2,1)S(1)} %dynamic-slice_convert_fusion), channel_id=1, replica_groups=mesh['op'=2,'sec'=16] {'sec'}, dimensions={1} | all-to-all | bytes 3145728 | tf_op jit(solution)/shard_map/all_to_all | solution.py:45
  148.4 1.6 %copy.19 = bf16[3,16,16,8,128]{4,3,2,1,0:T(8,128)(2,1)} copy(bf16[3,16,16,8,128]{4,3,0,1,2:T(8,128)(2,1)S(1)} %bitcast.44) | data formatting | bytes 3145728 | tf_op jit(solution)/shard_map/all_to_all | solution.py:45
  (1 shorter events, 0.0 us)
Async XLA Ops:
  4.0 21.9 %collective-permute-start = (bf16[3,1,256,256]{2,3,0,1:T(8,128)(2,1)}, bf16[3,1,256,256]{2,3,0,1:T(8,128)(2,1)}, u32[]{:S(2)}, u32[]{:S(2)}) collective-permute-start(bf16[3,1,256,256]{2,3,0,1:T(8,128)(2,1)} %get-tuple-element.220), channel_id=1, source_target_pairs={{0,1},{1,2},{2,3},{3,4},{4,5},{5,6},{6,7},{7,8},{8,9},{9,10},{10,1... | collective-permute-start | bytes 1179656 | tf_op jit(solution)/shard_map/ppermute | solution.py:16
  9.6 18.3 %collective-permute-start.1 = (bf16[3,1,256,256]{2,3,0,1:T(8,128)(2,1)S(1)}, bf16[3,1,256,256]{2,3,0,1:T(8,128)(2,1)}, u32[]{:S(2)}, u32[]{:S(2)}) collective-permute-start(bf16[3,1,256,256]{2,3,0,1:T(8,128)(2,1)S(1)} %get-tuple-element.221), channel_id=1, source_target_pairs={{1,0},{2,1},{3,2},{4,3},{5,4},{6,5},{7,6},{8,7},{9,8},{10,9},{11,1... | collective-permute-start | bytes 1179656 | tf_op jit(solution)/shard_map/ppermute | solution.py:17
  10.9 20.2 %copy-start = (s32[4]{0:T(128)S(1)}, s32[4]{0:T(128)}, u32[]{:S(2)}) copy-start(s32[4]{0:T(128)} %param.10) | copy-start | bytes 52
where the time goes:
time: 150 us
  blocking collectives  63.9 us (43%)
  matrix products  33.7 us (22%)
  local copies, waits for them, and re-layouts  17.3 us (12%)
  waiting for transfers between devices  16.9 us (11%)
  starting transfers between devices  6.9 us (5%)
  other arithmetic  6 us (4%)
  loops' own time  5.21 us (3%)
    all_to_all x1, blocking collectives, per_device(): lax.all_to_all(owned.astype(jnp.bfloat16), 'sec', split_axis=1, concat_ax...  43.7 us
    dot_general x4, matrix products, add_term(): jnp.einsum('vtik,tlk->vlti', middle, right_ops[index], preferred_element_...  33.7 us
    psum x1, blocking collectives, per_device(): summed = lax.psum(total, 'op')  20.3 us
    ppermute x1, waiting for transfers between devices, extended(): before = lax.ppermute(last, axis, up)  15 us
    while x1, local copies, waits for them, and re-layouts, per_device(): lax.fori_loop(0, count, add_term, jnp.zeros((nvec, blk, sectors, blk), jn...  9.08 us
    ppermute x1, starting transfers between devices, extended(): before = lax.ppermute(last, axis, up)  5.62 us
    another operation x1, loops' own time, per_device(): lax.fori_loop(0, count, add_term, jnp.zeros((nvec, blk, sectors, blk), jn...  5.21 us
    concatenate x1, other arithmetic, extended(): value = jnp.concatenate([before, value, after], axis=dim)  3.22 us
  transfers between devices with their start and end apart: 2, of which 2 were waited for; matrix products, arithmetic and copies ran while one was open for 0% of the time, Pallas kernels for 0%

commit v1 on v0

v1 whole, which is shorter than its diff:
```python
import functools

import jax
import jax.numpy as jnp
from jax import lax
from jax.experimental import pallas as pl
from jax.experimental.pallas import tpu as pltpu
from jax.sharding import PartitionSpec as P

QMAX = 1
F32, B16 = jnp.float32, jnp.bfloat16


def neighbours(value):
    size, length = lax.axis_size("sec"), value.shape[1]
    up = [(i, i + 1) for i in range(size - 1)]
    down = [(j, i) for i, j in up]
    before = lax.ppermute(lax.slice_in_dim(value, length - QMAX, length, axis=1), "sec", up)
    after = lax.ppermute(lax.slice_in_dim(value, 0, QMAX, axis=1), "sec", down)
    return before, after


def products_kernel(me_ref, shifts_ref, active_ref, psi, before, after, left, right, mine, theirs,
                    ext, lbuf, rbuf, acc, mbuf, tbuf, sem_p, sem_l, sem_r, sem_o):
    nvec = psi.shape[0]
    count, sectors, blk, _ = left.shape
    half = blk // 2

    def load_psi():
        return [
            pltpu.make_async_copy(psi, ext.at[:, pl.ds(QMAX, sectors)], sem_p.at[0]),
            pltpu.make_async_copy(before, ext.at[:, pl.ds(0, QMAX)], sem_p.at[1]),
            pltpu.make_async_copy(after, ext.at[:, pl.ds(sectors + QMAX, QMAX)], sem_p.at[2]),
        ]

    def load_left(t):
        return pltpu.make_async_copy(left.at[:, pl.ds(t, 1)], lbuf.at[:, pl.ds(t, 1)], sem_l.at[t])

    def load_right(t):
        return pltpu.make_async_copy(right.at[:, pl.ds(t, 1)], rbuf.at[:, pl.ds(t, 1)], sem_r.at[t])

    for copy in load_psi():
        copy.start()
    for t in range(sectors):
        load_left(t).start()
        load_right(t).start()
    for copy in load_psi():
        copy.wait()

    def sector(t, carry):
        load_left(t).wait()
        load_right(t).wait()
        for v in range(nvec):
            middles = []
            for k in range(count):
                source = ext[v, t + QMAX - shifts_ref[k]]
                middle = jnp.dot(lbuf[k, t], source, preferred_element_type=F32)
                middles.append((middle * active_ref[k, t].astype(F32)).astype(B16))
            rights = jnp.concatenate([rbuf[k, t] for k in range(count)], axis=1)
            total = lax.dot_general(
                rights, jnp.concatenate(middles, axis=1), (((1,), (1,)), ((), ())), preferred_element_type=F32
            )
            for h in range(2):
                acc[v, h, pl.ds(t, blk, stride=sectors), :] = total[:, h * half : (h + 1) * half]
        return carry

    lax.fori_loop(0, sectors, sector, 0)
    me = me_ref[0]
    stores = []
    for v in range(nvec):
        tbuf[v] = acc[v, 1 - me].astype(B16)
        stores.append(pltpu.make_async_copy(tbuf.at[v], theirs.at[v], sem_o.at[0, v]))
        stores[-1].start()
        mbuf[v] = acc[v, me].astype(B16)
        stores.append(pltpu.make_async_copy(mbuf.at[v], mine.at[v], sem_o.at[1, v]))
        stores[-1].start()
    for copy in stores:
        copy.wait()


def products(me, shifts, active, psi, before, after, left, right):
    nvec = psi.shape[0]
    count, sectors, blk, _ = left.shape
    rows, half = blk * sectors, blk // 2
    smem = pl.BlockSpec(memory_space=pltpu.SMEM)
    hbm = pl.BlockSpec(memory_space=pl.ANY)
    out = jax.ShapeDtypeStruct((nvec, rows, half), B16)
    return pl.pallas_call(
        products_kernel,
        out_shape=(out, out),
        in_specs=[smem] * 3 + [hbm] * 5,
        out_specs=(hbm, hbm),
        scratch_shapes=[
            pltpu.VMEM((nvec, sectors + 2 * QMAX, blk, blk), B16),
            pltpu.VMEM((count, sectors, blk, blk), B16),
            pltpu.VMEM((count, sectors, blk, blk), B16),
            pltpu.VMEM((nvec, 2, rows, half), F32),
            pltpu.VMEM((nvec, rows, half), B16),
            pltpu.VMEM((nvec, rows, half), B16),
            pltpu.SemaphoreType.DMA((3,)),
            pltpu.SemaphoreType.DMA((sectors,)),
            pltpu.SemaphoreType.DMA((sectors,)),
            pltpu.SemaphoreType.DMA((2, nvec)),
        ],
        compiler_params=pltpu.CompilerParams(vmem_limit_bytes=48 * 2**20),
        cost_estimate=pl.CostEstimate(
            flops=4 * count * sectors * nvec * blk**3, bytes_accessed=16 * 2**20, transcendentals=0
        ),
        name="products",
    )(me, shifts, active, psi, before, after, left, right)


def general(psi, left_ops, right_ops, shifts, active):
    before, after = neighbours(psi)
    padded = jnp.concatenate([before, psi, after], axis=1)
    count = left_ops.shape[0]
    nvec, sectors, blk, _ = psi.shape

    def add_term(index, total):
        source = lax.dynamic_slice_in_dim(padded, QMAX - shifts[index], sectors, 1)
        middle = jnp.einsum("tij,vtjk->vtik", left_ops[index], source, preferred_element_type=F32).astype(B16)
        term = jnp.einsum("vtik,tlk->vlti", middle, right_ops[index], preferred_element_type=F32)
        weight = active[index].astype(F32)
        return total + term * weight[None, None, :, None]

    total = lax.fori_loop(0, count, add_term, jnp.zeros((nvec, blk, sectors, blk), F32))
    summed = lax.psum(total, "op")
    share = blk // lax.axis_size("op")
    owned = lax.dynamic_slice_in_dim(summed, lax.axis_index("op") * share, share, 3)
    return lax.all_to_all(owned.astype(B16), "sec", split_axis=1, concat_axis=2, tiled=True)


def per_device(psi, left_ops, right_ops, shifts, active):
    if lax.axis_size("op") != 2:
        return general(psi, left_ops, right_ops, shifts, active)
    nvec, sectors, blk, _ = psi.shape
    before, after = neighbours(psi)
    me = lax.axis_index("op").reshape(1)
    mine, theirs = products(me, shifts, active, psi, before, after, left_ops, right_ops)
    other = lax.ppermute(theirs, "op", [(0, 1), (1, 0)])
    owned = (mine.astype(F32) + other.astype(F32)).astype(B16)
    owned = owned.reshape(nvec, blk, sectors, blk // 2)
    return lax.all_to_all(owned, "sec", split_axis=1, concat_axis=2, tiled=True)


def solution(mesh):
    placed = (
        P(None, "sec", None, None),
        P("op", "sec", None, None),
        P("op", "sec", None, None),
        P("op"),
        P("op", "sec"),
    )
    return jax.shard_map(
        per_device,
        mesh=mesh,
        in_specs=placed,
        out_specs=P(None, "sec", None, "op"),
        check_vma=False,
    )
```

time: 150 us -> 87.3 us (0.58)
  matrix products: 33.7 us -> 0 us
  blocking collectives: 63.9 us -> 43.6 us
  local copies, waits for them, and re-layouts: 17.3 us -> 3.06 us
  Pallas kernels: 0 us -> 13 us
  other arithmetic: 6 us -> 0.41 us
  loops' own time: 5.21 us -> 0 us
  waiting for transfers between devices: 16.9 us -> 20.1 us
    dot_general x4 -> x0, matrix products: 33.7 us -> none  [add_term(): jnp.einsum('vtik,tlk->vlti', middle, right_ops[index], preferred_element_...]
    psum x1 -> x0, blocking collectives: 20.3 us -> none  [per_device(): summed = lax.psum(total, 'op')]
    pallas_call x0 -> x1, Pallas kernels: none -> 13 us  [products(): pl.pallas_call(products_kernel, out_shape=(out, out), in_specs=[smem] * 3...]
    while x1 -> x0, local copies, waits for them, and re-layouts: 9.08 us -> none  [per_device(): lax.fori_loop(0, count, add_term, jnp.zeros((nvec, blk, sectors, blk), jn...]
    another operation x1 -> x0, loops' own time: 5.21 us -> none  [per_device(): lax.fori_loop(0, count, add_term, jnp.zeros((nvec, blk, sectors, blk), jn...]
    concatenate x1 -> x0, other arithmetic: 3.22 us -> none  [extended(): value = jnp.concatenate([before, value, after], axis=dim)]
    unnamed x3 -> x4, local copies, waits for them, and re-layouts: 3.19 us -> 0.01 us
    ppermute x2 -> x3, waiting for transfers between devices: 16.9 us -> 20.1 us  [the longest x1 8.7 us: neighbours(): lax.ppermute(lax.slice_in_dim(value, length - QMAX, length, axis=1), 'sec...]
  transfers between devices with their start and end apart: 2 -> 3, of which waited for: 2 -> 3; matrix products, arithmetic and copies ran while one was open for 0% -> 0% of each run, Pallas kernels for 0% -> 0%
where the time goes in v1:
time: 87.3 us; the launch traced here: 87.1 us
  blocking collectives  43.6 us (50%)
  waiting for transfers between devices  20.1 us (23%)
  Pallas kernels  13 us (15%)
  starting transfers between devices  6.87 us (8%)
  local copies, waits for them, and re-layouts  3.06 us (4%)
    all_to_all x1, blocking collectives, per_device(): return lax.all_to_all(owned, 'sec', split_axis=1, concat_axis=2, tiled=True)  43.6 us
    pallas_call x1, Pallas kernels, products(): pl.pallas_call(products_kernel, out_shape=(out, out), in_specs=[smem] * 3...  13 us
    ppermute x1, waiting for transfers between devices, neighbours(): lax.ppermute(lax.slice_in_dim(value, length - QMAX, length, axis=1), 'sec...  8.7 us
    ppermute x1, waiting for transfers between devices, neighbours(): after = lax.ppermute(lax.slice_in_dim(value, 0, QMAX, axis=1), 'sec', down)  7.97 us
    ppermute x1, starting transfers between devices, neighbours(): lax.ppermute(lax.slice_in_dim(value, length - QMAX, length, axis=1), 'sec...  5.5 us
    ppermute x1, waiting for transfers between devices, per_device(): other = lax.ppermute(theirs, 'op', [(0, 1), (1, 0)])  3.39 us
  transfers between devices with their start and end apart: 3, of which 3 were waited for; matrix products, arithmetic and copies ran while one was open for 0% of the time, Pallas kernels for 0%

profile of v1, /device:TPU:0, one launch (start us, length us, event | category | flops | bytes accessed | tf_op | source)
XLA Modules:
  0.0 87.1 jit_solution(12588821943847498656)
XLA Ops:
  0.0 0.0 copy-start
  0.0 0.0 copy-start.1
  0.0 1.2 %fusion.1 = (bf16[3,1,256,256]{3,2,1,0:T(8,128)(2,1)S(1)}, bf16[3,1,256,256]{3,2,1,0:T(8,128)(2,1)S(1)}) fusion(bf16[3,8,256,256]{3,2,1,0:T(8,128)(2,1)} %psi.1), kind=kLoop, calls=%fused_computation.3 | loop fusion | bytes 1572864 | tf_op jit(solution)/shard_map/slice | solution.py:19
  1.2 1.3 %collective-permute-start.1 = (bf16[3,1,256,256]{3,2,1,0:T(8,128)(2,1)S(1)}, bf16[3,1,256,256]{3,2,1,0:T(8,128)(2,1)S(1)}, u32[]{:S(2)}, u32[]{:S(2)}) collective-permute-start(bf16[3,1,256,256]{3,2,1,0:T(8,128)(2,1)S(1)} %get-tuple-element.9), channel_id=1, source_target_pairs={{1,0},{2,1},{3,2},{4,3},{5,4},{6,5},{7,6},{8,7},{9,8},{10,9},{11,1... | collective-permute-start | bytes 1179656 | tf_op jit(solution)/shard_map/ppermute | solution.py:19
  2.5 5.5 %collective-permute-start = (bf16[3,1,256,256]{3,2,1,0:T(8,128)(2,1)S(1)}, bf16[3,1,256,256]{3,2,1,0:T(8,128)(2,1)S(1)}, u32[]{:S(2)}, u32[]{:S(2)}) collective-permute-start(bf16[3,1,256,256]{3,2,1,0:T(8,128)(2,1)S(1)} %get-tuple-element.10), channel_id=1, source_target_pairs={{0,1},{1,2},{2,3},{3,4},{4,5},{5,6},{6,7},{7,8},{8,9},{9,10},{10,1... | collective-permute-start | bytes 1179656 | tf_op jit(solution)/shard_map/ppermute | solution.py:18
  8.0 8.0 %collective-permute-done.1.after = bf16[3,1,256,256]{3,2,1,0:T(8,128)(2,1)S(1)} collective-permute-done((bf16[3,1,256,256]{3,2,1,0:T(8,128)(2,1)S(1)}, bf16[3,1,256,256]{3,2,1,0:T(8,128)(2,1)S(1)}, u32[]{:S(2)}, u32[]{:S(2)}) %collective-permute-start.1) | collective-permute-done | bytes 393248 | tf_op jit(solution)/shard_map/ppermute | solution.py:19
  16.0 8.7 %collective-permute-done.before = bf16[3,1,256,256]{3,2,1,0:T(8,128)(2,1)S(1)} collective-permute-done((bf16[3,1,256,256]{3,2,1,0:T(8,128)(2,1)S(1)}, bf16[3,1,256,256]{3,2,1,0:T(8,128)(2,1)S(1)}, u32[]{:S(2)}, u32[]{:S(2)}) %collective-permute-start) | collective-permute-done | bytes 393248 | tf_op jit(solution)/shard_map/ppermute | solution.py:18
  24.7 0.0 copy-done
  24.7 0.0 copy-done.1
  24.7 13.0 %products.1 = (bf16[3,2048,128]{2,1,0:T(8,128)(2,1)S(1)}, bf16[3,2048,128]{2,1,0:T(8,128)(2,1)S(1)}) custom-call(s32[1]{0:T(128)} %bitcast.me_ref, s32[4]{0:T(128)S(1)} %copy-done.1, s32[4,8]{1,0:T(4,128)S(1)} %copy-done, bf16[3,8,256,256]{3,2,1,0:T(8,128)(2,1)} %psi.1, bf16[3,1,256,256]{3,2,1,0:T(8,128)(2,1)S(1)} %collective-permute-done.before, ...), custom_call_target="tpu_custom_call" | custom-call | flops 6442450944 | bytes 16777216 | tf_op jit(solution)/shard_map/products/pallas_call | solution.py:88
  37.7 0.1 collective-permute-start.2
  37.8 3.4 %collective-permute-done.2 = bf16[3,2048,128]{2,1,0:T(8,128)(2,1)S(1)} collective-permute-done((bf16[3,2048,128]{2,1,0:T(8,128)(2,1)S(1)}, bf16[3,2048,128]{2,1,0:T(8,128)(2,1)S(1)}, u32[]{:S(2)}, u32[]{:S(2)}) %collective-permute-start.2) | collective-permute-done | bytes 1572896 | tf_op jit(solution)/shard_map/ppermute | solution.py:140
  41.2 0.4 fusion
  41.6 0.3 copy.7
  41.9 43.6 %all_to_all.18 = bf16[3,256,8,128]{3,2,0,1:T(8,128)(2,1)S(1)} all-to-all(bf16[3,256,8,128]{3,2,0,1:T(8,128)(2,1)S(1)} %copy.7), channel_id=1, replica_groups=mesh['op'=2,'sec'=16] {'sec'}, dimensions={1} | all-to-all | bytes 3145728 | tf_op jit(solution)/shard_map/all_to_all | solution.py:143
  85.5 1.6 %copy.10 = bf16[3,16,16,8,128]{4,3,2,1,0:T(8,128)(2,1)} copy(bf16[3,16,16,8,128]{4,3,0,1,2:T(8,128)(2,1)S(1)} %bitcast.9) | data formatting | bytes 3145728 | tf_op jit(solution)/shard_map/all_to_all | solution.py:143
Async XLA Ops:
  0.0 24.7 %copy-start = (s32[4,8]{1,0:T(4,128)S(1)}, s32[4,8]{1,0:T(4,128)}, u32[]{:S(2)}) copy-start(s32[4,8]{1,0:T(4,128)} %active_ref.1) | copy-start | bytes 388
  0.0 24.7 %copy-start.1 = (s32[4]{0:T(128)S(1)}, s32[4]{0:T(128)}, u32[]{:S(2)}) copy-start(s32[4]{0:T(128)} %shifts_ref.1) | copy-start | bytes 52
  1.2 14.8 %collective-permute-start.1 = (bf16[3,1,256,256]{3,2,1,0:T(8,128)(2,1)S(1)}, bf16[3,1,256,256]{3,2,1,0:T(8,128)(2,1)S(1)}, u32[]{:S(2)}, u32[]{:S(2)}) collective-permute-start(bf16[3,1,256,256]{3,2,1,0:T(8,128)(2,1)S(1)} %get-tuple-element.9), channel_id=1, source_target_pairs={{1,0},{2,1},{3,2},{4,3},{5,4},{6,5},{7,6},{8,7},{9,8},{10,9},{11,1... | collective-permute-start | bytes 1179656 | tf_op jit(solution)/shard_map/ppermute | solution.py:19
  2.5 22.2 %collective-permute-start = (bf16[3,1,256,256]{3,2,1,0:T(8,128)(2,1)S(1)}, bf16[3,1,256,256]{3,2,1,0:T(8,128)(2,1)S(1)}, u32[]{:S(2)}, u32[]{:S(2)}) collective-permute-start(bf16[3,1,256,256]{3,2,1,0:T(8,128)(2,1)S(1)} %get-tuple-element.10), channel_id=1, source_target_pairs={{0,1},{1,2},{2,3},{3,4},{4,5},{5,6},{6,7},{7,8},{8,9},{9,10},{10,1... | collective-permute-start | bytes 1179656 | tf_op jit(solution)/shard_map/ppermute | solution.py:18
  37.7 3.5 %collective-permute-start.2 = (bf16[3,2048,128]{2,1,0:T(8,128)(2,1)S(1)}, bf16[3,2048,128]{2,1,0:T(8,128)(2,1)S(1)}, u32[]{:S(2)}, u32[]{:S(2)}) collective-permute-start(bf16[3,2048,128]{2,1,0:T(8,128)(2,1)S(1)} %get-tuple-element.8), channel_id=1, source_target_pairs={{0,16},{16,0},{1,17},{17,1},{2,18},{18,2},{3,19},{19,3},{4,20},{20... | collective-permute-start | bytes 4718600 | tf_op jit(solution)/shard_map/ppermute | solution.py:140

commit v2 on v0

v2 whole, which is shorter than its diff:
```python
import functools

import jax
import jax.numpy as jnp
from jax import lax
from jax.experimental import pallas as pl
from jax.experimental.pallas import tpu as pltpu
from jax.sharding import PartitionSpec as P

QMAX = 1
F32, B16 = jnp.float32, jnp.bfloat16


def neighbours(value, width):
    size, length = lax.axis_size("sec"), value.shape[1]
    up = [(i, i + 1) for i in range(size - 1)]
    down = [(j, i) for i, j in up]
    before = lax.ppermute(lax.slice_in_dim(value, length - width, length, axis=1), "sec", up)
    after = lax.ppermute(lax.slice_in_dim(value, 0, width, axis=1), "sec", down)
    return before, after


def fetch(psi, me):
    size, sectors = lax.axis_size("sec"), psi.shape[1]
    ahead = [(i, i + 1) for i in range(size - 1)]
    back = [(size + j, size + i) for i, j in ahead]
    part = lax.dynamic_slice_in_dim(psi, (1 - me) * (sectors - QMAX), QMAX, axis=1)
    return lax.ppermute(part, ("op", "sec"), ahead + back)


def swap(value):
    return lax.ppermute(value, "op", [(0, 1), (1, 0)])


def plan(nvec, sectors, early):
    inner = range(QMAX, sectors - QMAX)
    edge = [*range(QMAX), *range(sectors - QMAX, sectors)]
    first = [(v, t) for t in inner for v in range(early)]
    inside = [(v, t) for t in inner for v in range(early, nvec)]
    border = [(v, t) for t in edge for v in range(nvec)]
    return first, inside, border


class Work:
    def __init__(self, refs, psi, left, right, shifts, active, me, vectors):
        self.ext, self.lbuf, self.rbuf, self.obuf, self.sem_p, self.sem_l, self.sem_r, self.sem_o = refs
        self.psi, self.left, self.right, self.shifts, self.active, self.me = psi, left, right, shifts, active, me
        self.vectors = pl.ds(vectors[0], len(vectors)) if vectors else None
        self.sectors = left.shape[1]

    def operators(self, t):
        one = pl.ds(t, 1)
        return [
            pltpu.make_async_copy(self.left.at[:, one], self.lbuf.at[:, one], self.sem_l.at[t]),
            pltpu.make_async_copy(self.right.at[:, one], self.rbuf.at[:, one], self.sem_r.at[t]),
        ]

    def source(self, s):
        return [
            pltpu.make_async_copy(
                self.psi.at[self.vectors, pl.ds(s, 1)], self.ext.at[self.vectors, pl.ds(s + QMAX, 1)], self.sem_p.at[s]
            )
        ]

    def stores(self, job, mine, theirs):
        return [
            pltpu.make_async_copy(self.obuf.at[self.me, job], mine.at[job], self.sem_o.at[0, job]),
            pltpu.make_async_copy(self.obuf.at[1 - self.me, job], theirs.at[job], self.sem_o.at[1, job]),
        ]

    def product(self, v, t, job):
        count, _, _, blk = self.left.shape
        half = blk // 2
        middles = []
        for k in range(count):
            source = self.ext[v, t + QMAX - self.shifts[k]]
            middle = jnp.dot(self.lbuf[k, t], source, preferred_element_type=F32)
            middles.append((middle * self.active[k, t].astype(F32)).astype(B16))
        rights = jnp.concatenate([self.rbuf[k, t] for k in range(count)], axis=1)
        total = lax.dot_general(
            rights, jnp.concatenate(middles, axis=1), (((1,), (1,)), ((), ())), preferred_element_type=F32
        )
        for h in range(2):
            self.obuf[h, job] = total[:, h * half : (h + 1) * half].astype(B16)

    def start_inner(self):
        for s in range(2 * QMAX):
            for copy in self.source(s):
                copy.start()
        for t in range(QMAX, self.sectors - QMAX):
            for copy in self.source(t + QMAX) + self.operators(t):
                copy.start()

    def inner(self, vectors, group, mine, theirs):
        for s in range(2 * QMAX):
            for copy in self.source(s):
                copy.wait()

        def body(index, carry):
            at = [QMAX + index * group + place for place in range(group)]
            for t in at:
                for copy in self.source(t + QMAX) + self.operators(t):
                    copy.wait()
            self.several([(v, t) for t in at for v in vectors], index * group * len(vectors), mine, theirs)
            return carry

        lax.fori_loop(0, (self.sectors - 2 * QMAX) // group, body, 0)

    def several(self, jobs, base, mine, theirs):
        for place, (v, t) in enumerate(jobs):
            self.product(v, t, base + place)
        for place in range(len(jobs)):
            for copy in self.stores(base + place, mine, theirs):
                copy.start()

    def finish(self, jobs, mine, theirs):
        def body(job, carry):
            for copy in self.stores(job, mine, theirs):
                copy.wait()
            return carry

        lax.fori_loop(0, jobs, body, 0)


def first_kernel(early, me_ref, shifts, active, psi, left, right, mine, theirs, *refs):
    work = Work(refs, psi, left, right, shifts, active, me_ref[0], range(early))
    work.start_inner()
    work.inner(range(early), 2, mine, theirs)
    work.finish(mine.shape[0], mine, theirs)


def second_kernel(early, me_ref, shifts, active, psi, left, right, halo, other, mine, theirs, *refs):
    nvec, sectors = psi.shape[:2]
    me = me_ref[0]
    late = range(early, nvec)
    *refs, sem_h = refs
    work = Work(refs, psi, left, right, shifts, active, me, late)
    sides = []
    for index, at in enumerate((0, sectors - 2 * QMAX)):
        sides.append(
            pltpu.make_async_copy(
                psi.at[pl.ds(0, early), pl.ds(at, 2 * QMAX)],
                work.ext.at[pl.ds(0, early), pl.ds(at + QMAX, 2 * QMAX)],
                sem_h.at[index],
            )
        )
    for index, (source, core) in enumerate(((halo, me), (other, 1 - me))):
        at = core * (sectors + QMAX)
        sides.append(pltpu.make_async_copy(source, work.ext.at[:, pl.ds(at, QMAX)], sem_h.at[2 + index]))
    edge = [*range(QMAX), *range(sectors - QMAX, sectors)]
    if late:
        work.start_inner()
    for copy in sides:
        copy.start()
    for t in edge:
        for copy in work.operators(t):
            copy.start()
    if late:
        work.inner(late, 3, mine, theirs)
    for copy in sides:
        copy.wait()
    base = len(late) * (sectors - 2 * QMAX)
    for t in edge:
        for copy in work.operators(t):
            copy.wait()
        work.several([(v, t) for v in range(nvec)], base, mine, theirs)
        base += nvec
    work.finish(mine.shape[0], mine, theirs)


def products(kernel, early, jobs, vectors, me, shifts, active, psi, left, right, *more):
    count, sectors, blk, _ = left.shape
    half = blk // 2
    smem = pl.BlockSpec(memory_space=pltpu.SMEM)
    hbm = pl.BlockSpec(memory_space=pl.ANY)
    out = jax.ShapeDtypeStruct((jobs, blk, half), B16)
    return pl.pallas_call(
        functools.partial(kernel, early),
        out_shape=(out, out),
        in_specs=[smem] * 3 + [hbm] * 3 + [hbm] * len(more),
        out_specs=(hbm, hbm),
        scratch_shapes=[
            pltpu.VMEM((vectors, sectors + 2 * QMAX, blk, blk), B16),
            pltpu.VMEM((count, sectors, blk, blk), B16),
            pltpu.VMEM((count, sectors, blk, blk), B16),
            pltpu.VMEM((2, jobs, blk, half), B16),
            pltpu.SemaphoreType.DMA((sectors,)),
            pltpu.SemaphoreType.DMA((sectors,)),
            pltpu.SemaphoreType.DMA((sectors,)),
            pltpu.SemaphoreType.DMA((2, jobs)),
        ]
        + ([pltpu.SemaphoreType.DMA((4,))] if more else []),
        compiler_params=pltpu.CompilerParams(vmem_limit_bytes=60 * 2**20),
        cost_estimate=pl.CostEstimate(flops=2 * jobs * 2 * count * blk**3, bytes_accessed=12 * 2**20, transcendentals=0),
        name=kernel.__name__,
    )(me, shifts, active, psi, left, right, *more)


def combine_kernel(parts, behind, *refs):
    pairs, refs = refs[: 2 * parts], refs[2 * parts + behind :]
    owned, bufs, (obuf, sem) = refs[0], refs[1:-2], refs[-2:]
    size, _, share, half = obuf.shape
    loads = [pltpu.make_async_copy(ref, buf, sem.at[index]) for index, (ref, buf) in enumerate(zip(pairs, bufs))]
    for copy in loads:
        copy.start()
    base = 0
    for part in range(parts):
        loads[2 * part].wait()
        loads[2 * part + 1].wait()
        abuf, bbuf = bufs[2 * part], bufs[2 * part + 1]
        for job in range(abuf.shape[0]):
            total = (abuf[job].astype(F32) + bbuf[job].astype(F32)).astype(B16)
            obuf[:, base + job] = total.reshape(size, share, half)
        base += abuf.shape[0]
    store = pltpu.make_async_copy(obuf, owned, sem.at[0])
    store.start()
    store.wait()


def combine(pairs, size, *behind):
    refs = [ref for pair in pairs for ref in pair]
    jobs = sum(mine.shape[0] for mine, _ in pairs)
    _, blk, half = refs[0].shape
    hbm = pl.BlockSpec(memory_space=pl.ANY)
    block = (size, jobs, blk // size, half)
    return pl.pallas_call(
        functools.partial(combine_kernel, len(pairs), len(behind)),
        out_shape=jax.ShapeDtypeStruct(block, B16),
        in_specs=[hbm] * (len(refs) + len(behind)),
        out_specs=hbm,
        scratch_shapes=[pltpu.VMEM(ref.shape, B16) for ref in refs]
        + [pltpu.VMEM(block, B16), pltpu.SemaphoreType.DMA((len(refs),))],
        compiler_params=pltpu.CompilerParams(vmem_limit_bytes=16 * 2**20),
        cost_estimate=pl.CostEstimate(flops=0, bytes_accessed=0, transcendentals=0),
        name="combine",
    )(*refs, *behind)


def arrange_kernel(plans, sectors, *refs):
    count = len(plans)
    views, out, bufs, (acc, obuf, sem) = refs[:count], refs[count], refs[count + 1 : 2 * count + 1], refs[2 * count + 1 :]
    size, _, share, _ = bufs[0].shape
    loads = [pltpu.make_async_copy(view, buf, sem.at[index]) for index, (view, buf) in enumerate(zip(views, bufs))]
    for copy in loads:
        copy.start()
    for copy in loads:
        copy.wait()

    def body(source, carry):
        for buf, jobs in zip(bufs, plans):
            for job, (v, t) in enumerate(jobs):
                acc[v, pl.ds(source * sectors + t, share, stride=size * sectors), :] = buf[source, job].astype(F32)
        return carry

    lax.fori_loop(0, size, body, 0)
    stores = []
    for v in range(obuf.shape[0]):
        obuf[v] = acc[v].astype(B16)
        stores.append(pltpu.make_async_copy(obuf.at[v], out.at[v], sem.at[count + v]))
        stores[-1].start()
    for copy in stores:
        copy.wait()


def arrange(plans, views, nvec, sectors):
    size, _, share, half = views[0].shape
    rows = share * size * sectors
    hbm = pl.BlockSpec(memory_space=pl.ANY)
    out = pl.pallas_call(
        functools.partial(arrange_kernel, plans, sectors),
        out_shape=jax.ShapeDtypeStruct((nvec, rows, half), B16),
        in_specs=[hbm] * len(views),
        out_specs=hbm,
        scratch_shapes=[pltpu.VMEM(view.shape, B16) for view in views]
        + [
            pltpu.VMEM((nvec, rows, half), F32),
            pltpu.VMEM((nvec, rows, half), B16),
            pltpu.SemaphoreType.DMA((len(views) + nvec,)),
        ],
        compiler_params=pltpu.CompilerParams(vmem_limit_bytes=24 * 2**20),
        name="arrange",
    )(*views)
    return out.reshape(nvec, share, size * sectors, half)


def general(psi, left_ops, right_ops, shifts, active):
    before, after = neighbours(psi, QMAX)
    padded = jnp.concatenate([before, psi, after], axis=1)
    count = left_ops.shape[0]
    nvec, sectors, blk, _ = psi.shape

    def add_term(index, total):
        source = lax.dynamic_slice_in_dim(padded, QMAX - shifts[index], sectors, 1)
        middle = jnp.einsum("tij,vtjk->vtik", left_ops[index], source, preferred_element_type=F32).astype(B16)
        term = jnp.einsum("vtik,tlk->vlti", middle, right_ops[index], preferred_element_type=F32)
        weight = active[index].astype(F32)
        return total + term * weight[None, None, :, None]

    total = lax.fori_loop(0, count, add_term, jnp.zeros((nvec, blk, sectors, blk), F32))
    summed = lax.psum(total, "op")
    share = blk // lax.axis_size("op")
    owned = lax.dynamic_slice_in_dim(summed, lax.axis_index("op") * share, share, 3)
    return lax.all_to_all(owned.astype(B16), "sec", split_axis=1, concat_axis=2, tiled=True)


def per_device(psi, left_ops, right_ops, shifts, active):
    nvec, sectors, blk, _ = psi.shape
    size, half = lax.axis_size("sec"), blk // 2
    if lax.axis_size("op") != 2 or sectors <= 2 * QMAX or blk % (16 * size):
        return general(psi, left_ops, right_ops, shifts, active)
    me = lax.axis_index("op")
    state = (me.reshape(1), shifts, active, psi, left_ops, right_ops)
    early = 2
    first, inside, border = plan(nvec, sectors, early)
    rest = inside + border

    def fence(make, jobs, *operands):
        zeros = lambda *_: (jnp.zeros((len(jobs), blk, half), B16),) * 2
        return lax.cond(shifts[0] <= QMAX, make, zeros, *operands)

    def begin(*state):
        mine, theirs = products(first_kernel, early, len(first), early, *state)
        return mine, swap(theirs)

    def go_on(*state):
        mine, theirs = products(second_kernel, early, len(rest), nvec, *state)
        return mine, swap(theirs)

    halo = fetch(psi, me)
    owned = combine([fence(begin, first, *state)], size, halo)
    views = [lax.all_to_all(owned, "sec", split_axis=0, concat_axis=0, tiled=True)]
    pair = fence(go_on, rest, *state, halo, swap(halo))
    owned = combine([pair], size, views[0])
    views.append(lax.all_to_all(owned, "sec", split_axis=0, concat_axis=0, tiled=True))
    return arrange([first, rest], views, nvec, sectors)


def solution(mesh):
    placed = (
        P(None, "sec", None, None),
        P("op", "sec", None, None),
        P("op", "sec", None, None),
        P("op"),
        P("op", "sec"),
    )
    return jax.shard_map(
        per_device,
        mesh=mesh,
        in_specs=placed,
        out_specs=P(None, "sec", None, "op"),
        check_vma=False,
    )
```

time: 150 us -> 77.5 us (0.52)
  blocking collectives: 63.9 us -> 25 us
  matrix products: 33.7 us -> 0 us
  Pallas kernels: 0 us -> 26.4 us
  local copies, waits for them, and re-layouts: 17.3 us -> 1.03 us
  other arithmetic: 6 us -> 0 us
  loops' own time: 5.21 us -> 0.04 us
  starting transfers between devices: 6.9 us -> 11.1 us
  waiting for transfers between devices: 16.9 us -> 12.8 us
    dot_general x4 -> x0, matrix products: 33.7 us -> none  [add_term(): jnp.einsum('vtik,tlk->vlti', middle, right_ops[index], preferred_element_...]
    pallas_call x0 -> x5, Pallas kernels: none -> 26.4 us  [the longest x2 18.5 us: products(): pl.pallas_call(functools.partial(kernel, early), out_shape=(out, out), in...]
    psum x1 -> x0, blocking collectives: 20.3 us -> none  [per_device(): summed = lax.psum(total, 'op')]
    all_to_all x1, blocking collectives: 43.7 us -> 25 us  [per_device(): lax.all_to_all(owned, 'sec', split_axis=0, concat_axis=0, tiled=True)]
    ppermute x2 -> x4, waiting for transfers between devices: 16.9 us -> 6.81 us  [the longest x3 6.81 us: swap(): return lax.ppermute(value, 'op', [(0, 1), (1, 0)])]
    while x1 -> x0, local copies, waits for them, and re-layouts: 9.08 us -> none  [per_device(): lax.fori_loop(0, count, add_term, jnp.zeros((nvec, blk, sectors, blk), jn...]
    all_to_all x0 -> x1, waiting for transfers between devices: none -> 5.98 us  [per_device(): lax.all_to_all(owned, 'sec', split_axis=0, concat_axis=0, tiled=True)]
    all_to_all x0 -> x1, starting transfers between devices: none -> 5.93 us  [per_device(): lax.all_to_all(owned, 'sec', split_axis=0, concat_axis=0, tiled=True)]
  transfers between devices with their start and end apart: 2 -> 5, of which waited for: 2 -> 4; matrix products, arithmetic and copies ran while one was open for 0% -> 0% of each run, Pallas kernels for 0% -> 24%
where the time goes in v2:
time: 77.5 us; the launch traced here: 77.1 us
  Pallas kernels  26.4 us (34%)
  blocking collectives  25 us (32%)
  waiting for transfers between devices  12.8 us (17%)
  starting transfers between devices  11.1 us (14%)
  local copies, waits for them, and re-layouts  1.03 us (1%)
    all_to_all x1, blocking collectives, per_device(): lax.all_to_all(owned, 'sec', split_axis=0, concat_axis=0, tiled=True)  25 us
    pallas_call x2, Pallas kernels, products(): pl.pallas_call(functools.partial(kernel, early), out_shape=(out, out), in...  18.5 us
    ppermute x3, waiting for transfers between devices, swap(): return lax.ppermute(value, 'op', [(0, 1), (1, 0)])  6.81 us
    all_to_all x1, waiting for transfers between devices, per_device(): lax.all_to_all(owned, 'sec', split_axis=0, concat_axis=0, tiled=True)  5.98 us
    all_to_all x1, starting transfers between devices, per_device(): lax.all_to_all(owned, 'sec', split_axis=0, concat_axis=0, tiled=True)  5.93 us
    ppermute x1, starting transfers between devices, fetch(): return lax.ppermute(part, ('op', 'sec'), ahead + back)  4.87 us
    pallas_call x1, Pallas kernels, arrange(): pl.pallas_call(functools.partial(arrange_kernel, plans, sectors), out_sha...  4.25 us
    pallas_call x2, Pallas kernels, combine(): pl.pallas_call(functools.partial(combine_kernel, len(pairs), len(behind))...  3.7 us
  transfers between devices with their start and end apart: 5, of which 4 were waited for; matrix products, arithmetic and copies ran while one was open for 0% of the time, Pallas kernels for 24%

profile of v2, /device:TPU:0, one launch (start us, length us, event | category | flops | bytes accessed | tf_op | source)
XLA Modules:
  0.0 77.1 jit_solution(6182952464118900641)
XLA Ops:
  0.0 1.0 %constant_dynamic-slice_fusion = bf16[3,1,256,256]{3,2,1,0:T(8,128)(2,1)S(1)} fusion(bf16[3,8,256,256]{3,2,1,0:T(8,128)(2,1)} %param.9, s32[]{:T(128)S(6)} %select_n.3), kind=kLoop, calls=%fused_computation | loop fusion | bytes 786436 | tf_op jit(solution)/shard_map/dynamic_slice | solution.py:27
  1.0 4.9 %collective-permute-start.2 = (bf16[3,1,256,256]{3,2,1,0:T(8,128)(2,1)S(1)}, bf16[3,1,256,256]{3,2,1,0:T(8,128)(2,1)S(1)}, u32[]{:S(2)}, u32[]{:S(2)}) collective-permute-start(bf16[3,1,256,256]{3,2,1,0:T(8,128)(2,1)S(1)} %constant_dynamic-slice_fusion), channel_id=1, source_target_pairs={{0,1},{1,2},{2,3},{3,4},{4,5},{5,6},{6,7},{7,8},{8,9},{9,10},{10,1... | collective-permute-start | bytes 1179656 | tf_op jit(solution)/shard_map/ppermute | solution.py:28
  6.5 11.7 %conditional.2 = (bf16[12,256,128]{2,1,0:T(8,128)(2,1)S(1)}, bf16[12,256,128]{2,1,0:T(8,128)(2,1)}) conditional(s32[]{:T(128)} %bitcast, () %tuple.21, (s32[1]{0:T(128)}, s32[4]{0:T(128)}, s32[4,8]{1,0:T(4,128)}, bf16[3,8,256,256]{3,2,1,0:T(8,128)(2,1)}, bf16[4,8,256,256]{3,2,1,0:T(8,128)(2,1)}, /*index=5*/bf16[4,8,256,256]{3,2,1,0:T(8,128)(2,1)}) %tuple.22), branch_computations={%region_0.0_spmd, %region_1.0_spmd} | conditional | flops 3221225472 | bytes 15728696 | solution.py:319
  6.6 9.0 %first_kernel.1 = (bf16[12,256,128]{2,1,0:T(8,128)(2,1)S(1)}, bf16[12,256,128]{2,1,0:T(8,128)(2,1)}) custom-call(s32[1]{0:T(128)} %get-tuple-element.33.me_ref, s32[4]{0:T(128)} %get-tuple-element.34.shifts, s32[4,8]{1,0:T(4,128)} %get-tuple-element.35.active, bf16[3,8,256,256]{3,2,1,0:T(8,128)(2,1)} %get-tuple-element.36.psi, ...), custom_call_target="tpu_custom_call" | custom-call | flops 3221225472 | bytes 12582912 | tf_op jit(solution)/shard_map/cond/branch_1_fun/first_kernel/pallas_call | solution.py:177
  15.5 0.1 collective-permute-start
  15.6 2.6 %collective-permute-done = bf16[12,256,128]{2,1,0:T(8,128)(2,1)} collective-permute-done((bf16[12,256,128]{2,1,0:T(8,128)(2,1)}, bf16[12,256,128]{2,1,0:T(8,128)(2,1)}, u32[]{:S(2)}, u32[]{:S(2)}) %collective-permute-start) | collective-permute-done | bytes 786464 | tf_op jit(solution)/shard_map/cond/branch_1_fun/ppermute | solution.py:32
  18.2 0.0 copy-start
  18.2 0.0 copy-start.1
  18.2 0.0 collective-permute-done.2.refs_2_
  18.2 2.3 %combine.2 = bf16[16,12,16,128]{3,2,1,0:T(8,128)(2,1)} custom-call(bf16[12,256,128]{2,1,0:T(8,128)(2,1)S(1)} %get-tuple-element.55.refs_0_, bf16[12,256,128]{2,1,0:T(8,128)(2,1)} %get-tuple-element.56.refs_1_, bf16[3,1,256,256]{3,2,1,0:T(8,128)(2,1)S(1)} %collective-permute-done.2.refs_2_), custom_call_target="tpu_custom_call" | custom-call | tf_op jit(solution)/shard_map/combine/pallas_call | solution.py:226
  20.5 5.9 %all-to-all-start = ((bf16[16,12,16,128]{3,2,1,0:T(8,128)(2,1)}), bf16[16,12,16,128]{3,2,1,0:T(8,128)(2,1)S(1)}, u32[]{:S(2)}, u32[]{:S(2)}) async-start(bf16[16,12,16,128]{3,2,1,0:T(8,128)(2,1)} %combine.2), calls=%async_computation | async-start | bytes 1572864 | tf_op jit(solution)/shard_map/all_to_all | solution.py:331
  26.4 0.1 collective-permute-start.3
  26.5 1.7 %collective-permute-done.3 = bf16[3,1,256,256]{3,2,1,0:T(8,128)(2,1)S(1)} collective-permute-done((bf16[3,1,256,256]{3,2,1,0:T(8,128)(2,1)S(1)}, bf16[3,1,256,256]{3,2,1,0:T(8,128)(2,1)S(1)}, u32[]{:S(2)}, u32[]{:S(2)}) %collective-permute-start.3) | collective-permute-done | bytes 393248 | tf_op jit(solution)/shard_map/ppermute | solution.py:32
  28.2 0.0 copy-done
  28.2 0.0 copy-done.1
  28.2 12.2 %conditional.3 = (bf16[12,256,128]{2,1,0:T(8,128)(2,1)S(1)}, bf16[12,256,128]{2,1,0:T(8,128)(2,1)}) conditional(s32[]{:T(128)} %bitcast, () %tuple.23, (s32[1]{0:T(128)}, s32[4]{0:T(128)S(1)}, s32[4,8]{1,0:T(4,128)S(1)}, bf16[3,8,256,256]{3,2,1,0:T(8,128)(2,1)}, bf16[4,8,256,256]{3,2,1,0:T(8,128)(2,1)}, /*index=5*/bf16[4,8,256,256]{3,2,1,0:T(8,128)(2,1)}, ...), branch_computations={%region_2.0_spmd, %region_3.0_spmd} | conditional | flops 3221225472 | bytes 15728696 | solution.py:319
  28.2 9.5 %second_kernel.1 = (bf16[12,256,128]{2,1,0:T(8,128)(2,1)S(1)}, bf16[12,256,128]{2,1,0:T(8,128)(2,1)}) custom-call(s32[1]{0:T(128)} %get-tuple-element.41.me_ref, s32[4]{0:T(128)S(1)} %get-tuple-element.42.shifts, s32[4,8]{1,0:T(4,128)S(1)} %get-tuple-element.43.active, bf16[3,8,256,256]{3,2,1,0:T(8,128)(2,1)} %get-tuple-element.44.psi, ...), custom_call_target="tpu_custom_call" | custom-call | flops 3221225472 | bytes 12582912 | tf_op jit(solution)/shard_map/cond/branch_1_fun/second_kernel/pallas_call | solution.py:177
  37.8 0.2 collective-permute-start.1
  38.0 2.5 %collective-permute-done.1 = bf16[12,256,128]{2,1,0:T(8,128)(2,1)} collective-permute-done((bf16[12,256,128]{2,1,0:T(8,128)(2,1)}, bf16[12,256,128]{2,1,0:T(8,128)(2,1)}, u32[]{:S(2)}, u32[]{:S(2)}) %collective-permute-start.1) | collective-permute-done | bytes 786464 | tf_op jit(solution)/shard_map/cond/branch_1_fun/ppermute | solution.py:32
  40.5 6.0 %all-to-all-done.refs_2_.refs_0_ = bf16[16,12,16,128]{3,2,1,0:T(8,128)(2,1)S(1)} async-done(((bf16[16,12,16,128]{3,2,1,0:T(8,128)(2,1)}), bf16[16,12,16,128]{3,2,1,0:T(8,128)(2,1)S(1)}, u32[]{:S(2)}, u32[]{:S(2)}) %all-to-all-start) | async-done | bytes 786464 | tf_op jit(solution)/shard_map/all_to_all | solution.py:331
  46.5 1.4 %combine.3 = bf16[16,12,16,128]{3,2,1,0:T(8,128)(2,1)S(1)} custom-call(bf16[12,256,128]{2,1,0:T(8,128)(2,1)S(1)} %get-tuple-element.57.refs_0_, bf16[12,256,128]{2,1,0:T(8,128)(2,1)} %get-tuple-element.58.refs_1_, bf16[16,12,16,128]{3,2,1,0:T(8,128)(2,1)S(1)} %all-to-all-done.refs_2_.refs_0_), custom_call_target="tpu_custom_call" | custom-call | tf_op jit(solution)/shard_map/combine/pallas_call | solution.py:226
  47.9 25.0 %all_to_all.10.refs_1_ = bf16[16,12,16,128]{3,2,1,0:T(8,128)(2,1)S(1)} all-to-all(bf16[16,12,16,128]{3,2,1,0:T(8,128)(2,1)S(1)} %combine.3), channel_id=1, replica_groups=mesh['op'=2,'sec'=16] {'sec'}, dimensions={0} | all-to-all | bytes 1572864 | tf_op jit(solution)/shard_map/all_to_all | solution.py:334
  72.9 4.2 %arrange.1 = bf16[3,2048,128]{2,1,0:T(8,128)(2,1)} custom-call(bf16[16,12,16,128]{3,2,1,0:T(8,128)(2,1)S(1)} %all-to-all-done.refs_2_.refs_0_, bf16[16,12,16,128]{3,2,1,0:T(8,128)(2,1)S(1)} %all_to_all.10.refs_1_), custom_call_target="tpu_custom_call" | custom-call | tf_op jit(solution)/shard_map/arrange/pallas_call | solution.py:269
Async XLA Ops:
  1.0 17.2 %collective-permute-start.2 = (bf16[3,1,256,256]{3,2,1,0:T(8,128)(2,1)S(1)}, bf16[3,1,256,256]{3,2,1,0:T(8,128)(2,1)S(1)}, u32[]{:S(2)}, u32[]{:S(2)}) collective-permute-start(bf16[3,1,256,256]{3,2,1,0:T(8,128)(2,1)S(1)} %constant_dynamic-slice_fusion), channel_id=1, source_target_pairs={{0,1},{1,2},{2,3},{3,4},{4,5},{5,6},{6,7},{7,8},{8,9},{9,10},{10,1... | collective-permute-start | bytes 1179656 | tf_op jit(solution)/shard_map/ppermute | solution.py:28
  15.5 2.7 %collective-permute-start = (bf16[12,256,128]{2,1,0:T(8,128)(2,1)}, bf16[12,256,128]{2,1,0:T(8,128)(2,1)}, u32[]{:S(2)}, u32[]{:S(2)}) collective-permute-start(bf16[12,256,128]{2,1,0:T(8,128)(2,1)} %get-tuple-element.40), channel_id=1, source_target_pairs={{0,16},{16,0},{1,17},{17,1},{2,18},{18,2},{3,19},{19,3},{4,20},{20... | collective-permute-start | bytes 2359304 | tf_op jit(solution)/shard_map/cond/branch_1_fun/ppermute | solution.py:32
  18.2 10.0 %copy-start = (s32[4,8]{1,0:T(4,128)S(1)}, s32[4,8]{1,0:T(4,128)}, u32[]{:S(2)}) copy-start(s32[4,8]{1,0:T(4,128)} %param.13) | copy-start | bytes 388
  18.2 10.0 %copy-start.1 = (s32[4]{0:T(128)S(1)}, s32[4]{0:T(128)}, u32[]{:S(2)}) copy-start(s32[4]{0:T(128)} %param.12) | copy-start | bytes 52
  20.5 25.9 %all-to-all-start = ((bf16[16,12,16,128]{3,2,1,0:T(8,128)(2,1)}), bf16[16,12,16,128]{3,2,1,0:T(8,128)(2,1)S(1)}, u32[]{:S(2)}, u32[]{:S(2)}) async-start(bf16[16,12,16,128]{3,2,1,0:T(8,128)(2,1)} %combine.2), calls=%async_computation | async-start | bytes 1572864 | tf_op jit(solution)/shard_map/all_to_all | solution.py:331
  26.4 1.8 %collective-permute-start.3 = (bf16[3,1,256,256]{3,2,1,0:T(8,128)(2,1)S(1)}, bf16[3,1,256,256]{3,2,1,0:T(8,128)(2,1)S(1)}, u32[]{:S(2)}, u32[]{:S(2)}) collective-permute-start(bf16[3,1,256,256]{3,2,1,0:T(8,128)(2,1)S(1)} %collective-permute-done.2.refs_2_), channel_id=1, source_target_pairs={{0,16},{16,0},{1,17},{17,1},{2,18},{18,2},{3,19},{19,3},{4,20},{20... | collective-permute-start | bytes 1179656 | tf_op jit(solution)/shard_map/ppermute | solution.py:32
  37.8 2.7 %collective-permute-start.1 = (bf16[12,256,128]{2,1,0:T(8,128)(2,1)}, bf16[12,256,128]{2,1,0:T(8,128)(2,1)}, u32[]{:S(2)}, u32[]{:S(2)}) collective-permute-start(bf16[12,256,128]{2,1,0:T(8,128)(2,1)} %get-tuple-element.50), channel_id=1, source_target_pairs={{0,16},{16,0},{1,17},{17,1},{2,18},{18,2},{3,19},{19,3},{4,20},{20... | collective-permute-start | bytes 2359304 | tf_op jit(solution)/shard_map/cond/branch_1_fun/ppermute | solution.py:32

commit v3 on v2

--- a/solution.py
+++ b/solution.py
@@ -24,8 +24,9 @@
     size, sectors = lax.axis_size("sec"), psi.shape[1]
     ahead = [(i, i + 1) for i in range(size - 1)]
     back = [(size + j, size + i) for i, j in ahead]
+    turns = [(size - 1, 2 * size - 1), (size, 0)]
     part = lax.dynamic_slice_in_dim(psi, (1 - me) * (sectors - QMAX), QMAX, axis=1)
-    return lax.ppermute(part, ("op", "sec"), ahead + back)
+    return lax.ppermute(part, ("op", "sec"), ahead + turns + back)
 
 
 def swap(value):
@@ -33,20 +34,17 @@
 
 
 def plan(nvec, sectors, early):
-    inner = range(QMAX, sectors - QMAX)
+    inner = [*range(QMAX, sectors - QMAX)]
     edge = [*range(QMAX), *range(sectors - QMAX, sectors)]
-    first = [(v, t) for t in inner for v in range(early)]
-    inside = [(v, t) for t in inner for v in range(early, nvec)]
-    border = [(v, t) for t in edge for v in range(nvec)]
-    return first, inside, border
+    first, rest = inner[:early], inner[early:] + edge
+    return [[(v, t) for t in ts for v in range(nvec)] for ts in (first, rest)]
 
 
 class Work:
-    def __init__(self, refs, psi, left, right, shifts, active, me, vectors):
+    def __init__(self, refs, psi, left, right, shifts, active, me):
         self.ext, self.lbuf, self.rbuf, self.obuf, self.sem_p, self.sem_l, self.sem_r, self.sem_o = refs
         self.psi, self.left, self.right, self.shifts, self.active, self.me = psi, left, right, shifts, active, me
-        self.vectors = pl.ds(vectors[0], len(vectors)) if vectors else None
-        self.sectors = left.shape[1]
+        self.nvec = psi.shape[0]
 
     def operators(self, t):
         one = pl.ds(t, 1)
@@ -56,11 +54,7 @@
         ]
 
     def source(self, s):
-        return [
-            pltpu.make_async_copy(
-                self.psi.at[self.vectors, pl.ds(s, 1)], self.ext.at[self.vectors, pl.ds(s + QMAX, 1)], self.sem_p.at[s]
-            )
-        ]
+        return pltpu.make_async_copy(self.psi.at[:, pl.ds(s, 1)], self.ext.at[:, pl.ds(s + QMAX, 1)], self.sem_p.at[s])
 
     def stores(self, job, mine, theirs):
         return [
@@ -83,35 +77,33 @@
         for h in range(2):
             self.obuf[h, job] = total[:, h * half : (h + 1) * half].astype(B16)
 
-    def start_inner(self):
-        for s in range(2 * QMAX):
-            for copy in self.source(s):
+    def start(self, first, count):
+        for s in range(first - QMAX, first + QMAX):
+            self.source(s).start()
+        for t in range(first, first + count):
+            self.source(t + QMAX).start()
+            for copy in self.operators(t):
                 copy.start()
-        for t in range(QMAX, self.sectors - QMAX):
-            for copy in self.source(t + QMAX) + self.operators(t):
+
+    def sector(self, t, base, mine, theirs):
+        for copy in self.operators(t):
+            copy.wait()
+        for v in range(self.nvec):
+            self.product(v, t, base + v)
+        for v in range(self.nvec):
+            for copy in self.stores(base + v, mine, theirs):
                 copy.start()
 
-    def inner(self, vectors, group, mine, theirs):
-        for s in range(2 * QMAX):
-            for copy in self.source(s):
-                copy.wait()
+    def inner(self, first, count, mine, theirs):
+        for s in range(first - QMAX, first + QMAX):
+            self.source(s).wait()
 
         def body(index, carry):
-            at = [QMAX + index * group + place for place in range(group)]
-            for t in at:
-                for copy in self.source(t + QMAX) + self.operators(t):
-                    copy.wait()
-            self.several([(v, t) for t in at for v in vectors], index * group * len(vectors), mine, theirs)
+            self.source(first + index + QMAX).wait()
+            self.sector(first + index, index * self.nvec, mine, theirs)
             return carry
 
-        lax.fori_loop(0, (self.sectors - 2 * QMAX) // group, body, 0)
-
-    def several(self, jobs, base, mine, theirs):
-        for place, (v, t) in enumerate(jobs):
-            self.product(v, t, base + place)
-        for place in range(len(jobs)):
-            for copy in self.stores(base + place, mine, theirs):
-                copy.start()
+        lax.fori_loop(0, count, body, 0)
 
     def finish(self, jobs, mine, theirs):
         def body(job, carry):
@@ -123,52 +115,45 @@
 
 
 def first_kernel(early, me_ref, shifts, active, psi, left, right, mine, theirs, *refs):
-    work = Work(refs, psi, left, right, shifts, active, me_ref[0], range(early))
-    work.start_inner()
-    work.inner(range(early), 2, mine, theirs)
+    work = Work(refs, psi, left, right, shifts, active, me_ref[0])
+    work.start(QMAX, early)
+    work.inner(QMAX, early, mine, theirs)
     work.finish(mine.shape[0], mine, theirs)
 
 
 def second_kernel(early, me_ref, shifts, active, psi, left, right, halo, other, mine, theirs, *refs):
     nvec, sectors = psi.shape[:2]
     me = me_ref[0]
-    late = range(early, nvec)
     *refs, sem_h = refs
-    work = Work(refs, psi, left, right, shifts, active, me, late)
+    work = Work(refs, psi, left, right, shifts, active, me)
     sides = []
-    for index, at in enumerate((0, sectors - 2 * QMAX)):
-        sides.append(
-            pltpu.make_async_copy(
-                psi.at[pl.ds(0, early), pl.ds(at, 2 * QMAX)],
-                work.ext.at[pl.ds(0, early), pl.ds(at + QMAX, 2 * QMAX)],
-                sem_h.at[index],
-            )
-        )
     for index, (source, core) in enumerate(((halo, me), (other, 1 - me))):
         at = core * (sectors + QMAX)
-        sides.append(pltpu.make_async_copy(source, work.ext.at[:, pl.ds(at, QMAX)], sem_h.at[2 + index]))
+        sides.append(pltpu.make_async_copy(source, work.ext.at[:, pl.ds(at, QMAX)], sem_h.at[index]))
+    first, count = QMAX + early, sectors - 2 * QMAX - early
+    sides += [work.source(s) for s in range(min(2 * QMAX, first - QMAX))]
+    work.start(first, count)
     edge = [*range(QMAX), *range(sectors - QMAX, sectors)]
-    if late:
-        work.start_inner()
     for copy in sides:
         copy.start()
     for t in edge:
         for copy in work.operators(t):
             copy.start()
-    if late:
-        work.inner(late, 3, mine, theirs)
+    work.inner(first, count, mine, theirs)
     for copy in sides:
         copy.wait()
-    base = len(late) * (sectors - 2 * QMAX)
-    for t in edge:
-        for copy in work.operators(t):
-            copy.wait()
-        work.several([(v, t) for v in range(nvec)], base, mine, theirs)
-        base += nvec
+    for side, at in enumerate((0, sectors + QMAX)):
+
+        @pl.when(me_ref[1 + side] == 1)
+        def _(at=at):
+            work.ext[:, at : at + QMAX] = jnp.zeros((nvec, QMAX) + psi.shape[2:], psi.dtype)
+
+    for place, t in enumerate(edge):
+        work.sector(t, (count + place) * nvec, mine, theirs)
     work.finish(mine.shape[0], mine, theirs)
 
 
-def products(kernel, early, jobs, vectors, me, shifts, active, psi, left, right, *more):
+def products(kernel, early, jobs, me, shifts, active, psi, left, right, *more):
     count, sectors, blk, _ = left.shape
     half = blk // 2
     smem = pl.BlockSpec(memory_space=pltpu.SMEM)
@@ -180,7 +165,7 @@
         in_specs=[smem] * 3 + [hbm] * 3 + [hbm] * len(more),
         out_specs=(hbm, hbm),
         scratch_shapes=[
-            pltpu.VMEM((vectors, sectors + 2 * QMAX, blk, blk), B16),
+            pltpu.VMEM((psi.shape[0], sectors + 2 * QMAX, blk, blk), B16),
             pltpu.VMEM((count, sectors, blk, blk), B16),
             pltpu.VMEM((count, sectors, blk, blk), B16),
             pltpu.VMEM((2, jobs, blk, half), B16),
@@ -189,7 +174,7 @@
             pltpu.SemaphoreType.DMA((sectors,)),
             pltpu.SemaphoreType.DMA((2, jobs)),
         ]
-        + ([pltpu.SemaphoreType.DMA((4,))] if more else []),
+        + ([pltpu.SemaphoreType.DMA((2,))] if more else []),
         compiler_params=pltpu.CompilerParams(vmem_limit_bytes=60 * 2**20),
         cost_estimate=pl.CostEstimate(flops=2 * jobs * 2 * count * blk**3, bytes_accessed=12 * 2**20, transcendentals=0),
         name=kernel.__name__,
@@ -198,16 +183,11 @@
 
 def combine_kernel(parts, behind, *refs):
     pairs, refs = refs[: 2 * parts], refs[2 * parts + behind :]
-    owned, bufs, (obuf, sem) = refs[0], refs[1:-2], refs[-2:]
+    owned, (obuf, sem) = refs[0], refs[-2:]
     size, _, share, half = obuf.shape
-    loads = [pltpu.make_async_copy(ref, buf, sem.at[index]) for index, (ref, buf) in enumerate(zip(pairs, bufs))]
-    for copy in loads:
-        copy.start()
     base = 0
     for part in range(parts):
-        loads[2 * part].wait()
-        loads[2 * part + 1].wait()
-        abuf, bbuf = bufs[2 * part], bufs[2 * part + 1]
+        abuf, bbuf = pairs[2 * part], pairs[2 * part + 1]
         for job in range(abuf.shape[0]):
             total = (abuf[job].astype(F32) + bbuf[job].astype(F32)).astype(B16)
             obuf[:, base + job] = total.reshape(size, share, half)
@@ -226,10 +206,9 @@
     return pl.pallas_call(
         functools.partial(combine_kernel, len(pairs), len(behind)),
         out_shape=jax.ShapeDtypeStruct(block, B16),
-        in_specs=[hbm] * (len(refs) + len(behind)),
+        in_specs=[pl.BlockSpec(memory_space=pltpu.VMEM)] * len(refs) + [hbm] * len(behind),
         out_specs=hbm,
-        scratch_shapes=[pltpu.VMEM(ref.shape, B16) for ref in refs]
-        + [pltpu.VMEM(block, B16), pltpu.SemaphoreType.DMA((len(refs),))],
+        scratch_shapes=[pltpu.VMEM(block, B16), pltpu.SemaphoreType.DMA((1,))],
         compiler_params=pltpu.CompilerParams(vmem_limit_bytes=16 * 2**20),
         cost_estimate=pl.CostEstimate(flops=0, bytes_accessed=0, transcendentals=0),
         name="combine",
@@ -309,28 +288,29 @@
     if lax.axis_size("op") != 2 or sectors <= 2 * QMAX or blk % (16 * size):
         return general(psi, left_ops, right_ops, shifts, active)
     me = lax.axis_index("op")
-    state = (me.reshape(1), shifts, active, psi, left_ops, right_ops)
-    early = 2
-    first, inside, border = plan(nvec, sectors, early)
-    rest = inside + border
+    sec = lax.axis_index("sec")
+    place = jnp.stack([me, (sec == 0).astype(jnp.int32), (sec == size - 1).astype(jnp.int32)])
+    state = (place, shifts, active, psi, left_ops, right_ops)
+    early = 4
+    first, rest = plan(nvec, sectors, early)
 
     def fence(make, jobs, *operands):
         zeros = lambda *_: (jnp.zeros((len(jobs), blk, half), B16),) * 2
-        return lax.cond(shifts[0] <= QMAX, make, zeros, *operands)
+        return lax.cond(sec < size, make, zeros, *operands)
 
     def begin(*state):
-        mine, theirs = products(first_kernel, early, len(first), early, *state)
+        mine, theirs = products(first_kernel, early, len(first), *state)
         return mine, swap(theirs)
 
     def go_on(*state):
-        mine, theirs = products(second_kernel, early, len(rest), nvec, *state)
+        mine, theirs = products(second_kernel, early, len(rest), *state)
         return mine, swap(theirs)
 
     halo = fetch(psi, me)
     owned = combine([fence(begin, first, *state)], size, halo)
     views = [lax.all_to_all(owned, "sec", split_axis=0, concat_axis=0, tiled=True)]
     pair = fence(go_on, rest, *state, halo, swap(halo))
-    owned = combine([pair], size, views[0])
+    owned = combine([pair], size)
     views.append(lax.all_to_all(owned, "sec", split_axis=0, concat_axis=0, tiled=True))
     return arrange([first, rest], views, nvec, sectors)
 

time: 77.5 us -> 73.8 us (0.952)
  starting transfers between devices: 11.1 us -> 9.29 us
  waiting for transfers between devices: 12.8 us -> 12 us
    ppermute x1, starting transfers between devices: 4.87 us -> 2.99 us  [fetch(): return lax.ppermute(part, ('op', 'sec'), ahead + turns + back)]
    all_to_all x1, waiting for transfers between devices: 5.98 us -> 5.19 us  [per_device(): lax.all_to_all(owned, 'sec', split_axis=0, concat_axis=0, tiled=True)]
  transfers between devices with their start and end apart: 5 -> 5, of which waited for: 4 -> 4; matrix products, arithmetic and copies ran while one was open for 0% -> 0% of each run, Pallas kernels for 24% -> 26%
where the time goes in v3:
time: 73.8 us; the launch traced here: 73.4 us
  Pallas kernels  26 us (35%)
  blocking collectives  25 us (34%)
  waiting for transfers between devices  12 us (16%)
  starting transfers between devices  9.29 us (13%)
  local copies, waits for them, and re-layouts  1.03 us (1%)
    all_to_all x1, blocking collectives, per_device(): lax.all_to_all(owned, 'sec', split_axis=0, concat_axis=0, tiled=True)  25 us
    pallas_call x2, Pallas kernels, products(): pl.pallas_call(functools.partial(kernel, early), out_shape=(out, out), in...  18 us
    ppermute x3, waiting for transfers between devices, swap(): return lax.ppermute(value, 'op', [(0, 1), (1, 0)])  6.81 us
    all_to_all x1, starting transfers between devices, per_device(): lax.all_to_all(owned, 'sec', split_axis=0, concat_axis=0, tiled=True)  5.95 us
    all_to_all x1, waiting for transfers between devices, per_device(): lax.all_to_all(owned, 'sec', split_axis=0, concat_axis=0, tiled=True)  5.19 us
    pallas_call x1, Pallas kernels, arrange(): pl.pallas_call(functools.partial(arrange_kernel, plans, sectors), out_sha...  4.42 us
    pallas_call x2, Pallas kernels, combine(): pl.pallas_call(functools.partial(combine_kernel, len(pairs), len(behind))...  3.6 us
    ppermute x1, starting transfers between devices, fetch(): return lax.ppermute(part, ('op', 'sec'), ahead + turns + back)  2.99 us
  transfers between devices with their start and end apart: 5, of which 4 were waited for; matrix products, arithmetic and copies ran while one was open for 0% of the time, Pallas kernels for 26%

profile of v3, /device:TPU:0, one launch (start us, length us, event | category | flops | bytes accessed | tf_op | source)
XLA Modules:
  0.0 73.4 jit_solution(6815406155916880342)
XLA Ops:
  0.0 1.0 %constant_dynamic-slice_fusion = bf16[3,1,256,256]{3,2,1,0:T(8,128)(2,1)S(1)} fusion(bf16[3,8,256,256]{3,2,1,0:T(8,128)(2,1)} %param.9, s32[]{:T(128)S(6)} %select_n.3), kind=kLoop, calls=%fused_computation.1 | loop fusion | bytes 786436 | tf_op jit(solution)/shard_map/dynamic_slice | solution.py:28
  1.0 3.0 %collective-permute-start.2 = (bf16[3,1,256,256]{3,2,1,0:T(8,128)(2,1)S(1)}, bf16[3,1,256,256]{3,2,1,0:T(8,128)(2,1)S(1)}, u32[]{:S(2)}, u32[]{:S(2)}) collective-permute-start(bf16[3,1,256,256]{3,2,1,0:T(8,128)(2,1)S(1)} %constant_dynamic-slice_fusion), channel_id=1, source_target_pairs={{0,1},{1,2},{2,3},{3,4},{4,5},{5,6},{6,7},{7,8},{8,9},{9,10},{10,1... | collective-permute-start | bytes 1179656 | tf_op jit(solution)/shard_map/ppermute | solution.py:29
  4.0 0.1 pad_add_fusion
  4.1 11.7 %conditional.2 = (bf16[12,256,128]{2,1,0:T(8,128)(2,1)S(1)}, bf16[12,256,128]{2,1,0:T(8,128)(2,1)}) conditional(s32[]{:T(128)} %convert_element_type.2, () %tuple.21, (s32[3]{0:T(128)S(1)}, s32[4]{0:T(128)}, s32[4,8]{1,0:T(4,128)}, bf16[3,8,256,256]{3,2,1,0:T(8,128)(2,1)}, bf16[4,8,256,256]{3,2,1,0:T(8,128)(2,1)}, ...), branch_computations={%region_0.0_spmd, %region_1.0_spmd} | conditional | flops 3221225472 | bytes 15728696 | solution.py:299
  4.1 9.0 %first_kernel.1 = (bf16[12,256,128]{2,1,0:T(8,128)(2,1)S(1)}, bf16[12,256,128]{2,1,0:T(8,128)(2,1)}) custom-call(s32[3]{0:T(128)S(1)} %get-tuple-element.33.me_ref, s32[4]{0:T(128)} %get-tuple-element.34.shifts, s32[4,8]{1,0:T(4,128)} %get-tuple-element.35.active, bf16[3,8,256,256]{3,2,1,0:T(8,128)(2,1)} %get-tuple-element.36.psi, ...), custom_call_target="tpu_custom_call" | custom-call | flops 3221225472 | bytes 12582912 | tf_op jit(solution)/shard_map/cond/branch_1_fun/first_kernel/pallas_call | solution.py:162
  13.1 0.1 collective-permute-start
  13.2 2.6 %collective-permute-done = bf16[12,256,128]{2,1,0:T(8,128)(2,1)} collective-permute-done((bf16[12,256,128]{2,1,0:T(8,128)(2,1)}, bf16[12,256,128]{2,1,0:T(8,128)(2,1)}, u32[]{:S(2)}, u32[]{:S(2)}) %collective-permute-start) | collective-permute-done | bytes 786464 | tf_op jit(solution)/shard_map/cond/branch_1_fun/ppermute | solution.py:33
  15.8 0.0 copy-start
  15.8 0.0 copy-start.1
  15.8 0.0 collective-permute-done.2.refs_2_
  15.8 2.2 %combine.2 = bf16[16,12,16,128]{3,2,1,0:T(8,128)(2,1)} custom-call(bf16[12,256,128]{2,1,0:T(8,128)(2,1)S(1)} %get-tuple-element.55.refs_0_, bf16[12,256,128]{2,1,0:T(8,128)(2,1)} %get-tuple-element.56.refs_1_, bf16[3,1,256,256]{3,2,1,0:T(8,128)(2,1)S(1)} %collective-permute-done.2.refs_2_), custom_call_target="tpu_custom_call" | custom-call | tf_op jit(solution)/shard_map/combine/pallas_call | solution.py:206
  18.1 5.9 %all-to-all-start = ((bf16[16,12,16,128]{3,2,1,0:T(8,128)(2,1)}), bf16[16,12,16,128]{3,2,1,0:T(8,128)(2,1)S(1)}, u32[]{:S(2)}, u32[]{:S(2)}) async-start(bf16[16,12,16,128]{3,2,1,0:T(8,128)(2,1)} %combine.2), calls=%async_computation | async-start | bytes 1572864 | tf_op jit(solution)/shard_map/all_to_all | solution.py:311
  24.0 0.1 collective-permute-start.3
  24.1 1.7 %collective-permute-done.3 = bf16[3,1,256,256]{3,2,1,0:T(8,128)(2,1)S(1)} collective-permute-done((bf16[3,1,256,256]{3,2,1,0:T(8,128)(2,1)S(1)}, bf16[3,1,256,256]{3,2,1,0:T(8,128)(2,1)S(1)}, u32[]{:S(2)}, u32[]{:S(2)}) %collective-permute-start.3) | collective-permute-done | bytes 393248 | tf_op jit(solution)/shard_map/ppermute | solution.py:33
  25.8 0.0 copy-done
  25.8 0.0 copy-done.1
  25.8 11.6 %conditional.3 = (bf16[12,256,128]{2,1,0:T(8,128)(2,1)S(1)}, bf16[12,256,128]{2,1,0:T(8,128)(2,1)}) conditional(s32[]{:T(128)} %convert_element_type.2, () %tuple.23, (s32[3]{0:T(128)S(1)}, s32[4]{0:T(128)S(1)}, s32[4,8]{1,0:T(4,128)S(1)}, bf16[3,8,256,256]{3,2,1,0:T(8,128)(2,1)}, bf16[4,8,256,256]{3,2,1,0:T(8,128)(2,1)}, ...), branch_computations={%region_2.0_spmd, %region_3.0_spmd} | conditional | flops 3221225472 | bytes 15728696 | solution.py:299
  25.8 8.9 %second_kernel.1 = (bf16[12,256,128]{2,1,0:T(8,128)(2,1)S(1)}, bf16[12,256,128]{2,1,0:T(8,128)(2,1)}) custom-call(s32[3]{0:T(128)S(1)} %get-tuple-element.41.me_ref, s32[4]{0:T(128)S(1)} %get-tuple-element.42.shifts, s32[4,8]{1,0:T(4,128)S(1)} %get-tuple-element.43.active, bf16[3,8,256,256]{3,2,1,0:T(8,128)(2,1)} %get-tuple-element.44.psi, ...), custom_call_target="tpu_custom_call" | custom-call | flops 3221225472 | bytes 12582912 | tf_op jit(solution)/shard_map/cond/branch_1_fun/second_kernel/pallas_call | solution.py:162
  34.7 0.2 collective-permute-start.1
  35.0 2.5 %collective-permute-done.1 = bf16[12,256,128]{2,1,0:T(8,128)(2,1)} collective-permute-done((bf16[12,256,128]{2,1,0:T(8,128)(2,1)}, bf16[12,256,128]{2,1,0:T(8,128)(2,1)}, u32[]{:S(2)}, u32[]{:S(2)}) %collective-permute-start.1) | collective-permute-done | bytes 786464 | tf_op jit(solution)/shard_map/cond/branch_1_fun/ppermute | solution.py:33
  37.4 1.4 %combine.3 = bf16[16,12,16,128]{3,2,1,0:T(8,128)(2,1)S(1)} custom-call(bf16[12,256,128]{2,1,0:T(8,128)(2,1)S(1)} %get-tuple-element.57.refs_0_, bf16[12,256,128]{2,1,0:T(8,128)(2,1)} %get-tuple-element.58.refs_1_), custom_call_target="tpu_custom_call" | custom-call | tf_op jit(solution)/shard_map/combine/pallas_call | solution.py:206
  38.8 5.2 %all-to-all-done.refs_0_ = bf16[16,12,16,128]{3,2,1,0:T(8,128)(2,1)S(1)} async-done(((bf16[16,12,16,128]{3,2,1,0:T(8,128)(2,1)}), bf16[16,12,16,128]{3,2,1,0:T(8,128)(2,1)S(1)}, u32[]{:S(2)}, u32[]{:S(2)}) %all-to-all-start) | async-done | bytes 786464 | tf_op jit(solution)/shard_map/all_to_all | solution.py:311
  44.0 25.0 %all_to_all.10.refs_1_ = bf16[16,12,16,128]{3,2,1,0:T(8,128)(2,1)S(1)} all-to-all(bf16[16,12,16,128]{3,2,1,0:T(8,128)(2,1)S(1)} %combine.3), channel_id=1, replica_groups=mesh['op'=2,'sec'=16] {'sec'}, dimensions={0} | all-to-all | bytes 1572864 | tf_op jit(solution)/shard_map/all_to_all | solution.py:314
  69.0 4.4 %arrange.1 = bf16[3,2048,128]{2,1,0:T(8,128)(2,1)} custom-call(bf16[16,12,16,128]{3,2,1,0:T(8,128)(2,1)S(1)} %all-to-all-done.refs_0_, bf16[16,12,16,128]{3,2,1,0:T(8,128)(2,1)S(1)} %all_to_all.10.refs_1_), custom_call_target="tpu_custom_call" | custom-call | tf_op jit(solution)/shard_map/arrange/pallas_call | solution.py:248
Async XLA Ops:
  1.0 14.8 %collective-permute-start.2 = (bf16[3,1,256,256]{3,2,1,0:T(8,128)(2,1)S(1)}, bf16[3,1,256,256]{3,2,1,0:T(8,128)(2,1)S(1)}, u32[]{:S(2)}, u32[]{:S(2)}) collective-permute-start(bf16[3,1,256,256]{3,2,1,0:T(8,128)(2,1)S(1)} %constant_dynamic-slice_fusion), channel_id=1, source_target_pairs={{0,1},{1,2},{2,3},{3,4},{4,5},{5,6},{6,7},{7,8},{8,9},{9,10},{10,1... | collective-permute-start | bytes 1179656 | tf_op jit(solution)/shard_map/ppermute | solution.py:29
  13.1 2.7 %collective-permute-start = (bf16[12,256,128]{2,1,0:T(8,128)(2,1)}, bf16[12,256,128]{2,1,0:T(8,128)(2,1)}, u32[]{:S(2)}, u32[]{:S(2)}) collective-permute-start(bf16[12,256,128]{2,1,0:T(8,128)(2,1)} %get-tuple-element.40), channel_id=1, source_target_pairs={{0,16},{16,0},{1,17},{17,1},{2,18},{18,2},{3,19},{19,3},{4,20},{20... | collective-permute-start | bytes 2359304 | tf_op jit(solution)/shard_map/cond/branch_1_fun/ppermute | solution.py:33
  15.8 10.0 %copy-start = (s32[4,8]{1,0:T(4,128)S(1)}, s32[4,8]{1,0:T(4,128)}, u32[]{:S(2)}) copy-start(s32[4,8]{1,0:T(4,128)} %param.13) | copy-start | bytes 388
  15.8 10.0 %copy-start.1 = (s32[4]{0:T(128)S(1)}, s32[4]{0:T(128)}, u32[]{:S(2)}) copy-start(s32[4]{0:T(128)} %param.12) | copy-start | bytes 52
  18.1 26.0 %all-to-all-start = ((bf16[16,12,16,128]{3,2,1,0:T(8,128)(2,1)}), bf16[16,12,16,128]{3,2,1,0:T(8,128)(2,1)S(1)}, u32[]{:S(2)}, u32[]{:S(2)}) async-start(bf16[16,12,16,128]{3,2,1,0:T(8,128)(2,1)} %combine.2), calls=%async_computation | async-start | bytes 1572864 | tf_op jit(solution)/shard_map/all_to_all | solution.py:311
  24.0 1.8 %collective-permute-start.3 = (bf16[3,1,256,256]{3,2,1,0:T(8,128)(2,1)S(1)}, bf16[3,1,256,256]{3,2,1,0:T(8,128)(2,1)S(1)}, u32[]{:S(2)}, u32[]{:S(2)}) collective-permute-start(bf16[3,1,256,256]{3,2,1,0:T(8,128)(2,1)S(1)} %collective-permute-done.2.refs_2_), channel_id=1, source_target_pairs={{0,16},{16,0},{1,17},{17,1},{2,18},{18,2},{3,19},{19,3},{4,20},{20... | collective-permute-start | bytes 1179656 | tf_op jit(solution)/shard_map/ppermute | solution.py:33
  34.7 2.7 %collective-permute-start.1 = (bf16[12,256,128]{2,1,0:T(8,128)(2,1)}, bf16[12,256,128]{2,1,0:T(8,128)(2,1)}, u32[]{:S(2)}, u32[]{:S(2)}) collective-permute-start(bf16[12,256,128]{2,1,0:T(8,128)(2,1)} %get-tuple-element.50), channel_id=1, source_target_pairs={{0,16},{16,0},{1,17},{17,1},{2,18},{18,2},{3,19},{19,3},{4,20},{20... | collective-permute-start | bytes 2359304 | tf_op jit(solution)/shard_map/cond/branch_1_fun/ppermute | solution.py:33

commit v4 on v3

--- a/solution.py
+++ b/solution.py
@@ -42,7 +42,7 @@
 
 class Work:
     def __init__(self, refs, psi, left, right, shifts, active, me):
-        self.ext, self.lbuf, self.rbuf, self.obuf, self.sem_p, self.sem_l, self.sem_r, self.sem_o = refs
+        self.ext, self.lbuf, self.rbuf, self.sem_p, self.sem_l, self.sem_r = refs
         self.psi, self.left, self.right, self.shifts, self.active, self.me = psi, left, right, shifts, active, me
         self.nvec = psi.shape[0]
 
@@ -56,26 +56,21 @@
     def source(self, s):
         return pltpu.make_async_copy(self.psi.at[:, pl.ds(s, 1)], self.ext.at[:, pl.ds(s + QMAX, 1)], self.sem_p.at[s])
 
-    def stores(self, job, mine, theirs):
-        return [
-            pltpu.make_async_copy(self.obuf.at[self.me, job], mine.at[job], self.sem_o.at[0, job]),
-            pltpu.make_async_copy(self.obuf.at[1 - self.me, job], theirs.at[job], self.sem_o.at[1, job]),
-        ]
-
-    def product(self, v, t, job):
+    def products(self, t, base, mine, theirs):
         count, _, _, blk = self.left.shape
         half = blk // 2
         middles = []
         for k in range(count):
-            source = self.ext[v, t + QMAX - self.shifts[k]]
-            middle = jnp.dot(self.lbuf[k, t], source, preferred_element_type=F32)
+            sources = jnp.concatenate([self.ext[v, t + QMAX - self.shifts[k]] for v in range(self.nvec)], axis=1)
+            middle = jnp.dot(self.lbuf[k, t], sources, preferred_element_type=F32)
             middles.append((middle * self.active[k, t].astype(F32)).astype(B16))
         rights = jnp.concatenate([self.rbuf[k, t] for k in range(count)], axis=1)
-        total = lax.dot_general(
-            rights, jnp.concatenate(middles, axis=1), (((1,), (1,)), ((), ())), preferred_element_type=F32
-        )
-        for h in range(2):
-            self.obuf[h, job] = total[:, h * half : (h + 1) * half].astype(B16)
+        for v in range(self.nvec):
+            middle = jnp.concatenate([m[:, v * blk : (v + 1) * blk] for m in middles], axis=1)
+            total = lax.dot_general(rights, middle, (((1,), (1,)), ((), ())), preferred_element_type=F32)
+            low, high = total[:, :half], total[:, half:]
+            mine[base + v] = jnp.where(self.me == 0, low, high).astype(B16)
+            theirs[base + v] = jnp.where(self.me == 0, high, low).astype(B16)
 
     def start(self, first, count):
         for s in range(first - QMAX, first + QMAX):
@@ -88,11 +83,7 @@
     def sector(self, t, base, mine, theirs):
         for copy in self.operators(t):
             copy.wait()
-        for v in range(self.nvec):
-            self.product(v, t, base + v)
-        for v in range(self.nvec):
-            for copy in self.stores(base + v, mine, theirs):
-                copy.start()
+        self.products(t, base, mine, theirs)
 
     def inner(self, first, count, mine, theirs):
         for s in range(first - QMAX, first + QMAX):
@@ -105,20 +96,11 @@
 
         lax.fori_loop(0, count, body, 0)
 
-    def finish(self, jobs, mine, theirs):
-        def body(job, carry):
-            for copy in self.stores(job, mine, theirs):
-                copy.wait()
-            return carry
-
-        lax.fori_loop(0, jobs, body, 0)
-
 
 def first_kernel(early, me_ref, shifts, active, psi, left, right, mine, theirs, *refs):
     work = Work(refs, psi, left, right, shifts, active, me_ref[0])
     work.start(QMAX, early)
     work.inner(QMAX, early, mine, theirs)
-    work.finish(mine.shape[0], mine, theirs)
 
 
 def second_kernel(early, me_ref, shifts, active, psi, left, right, halo, other, mine, theirs, *refs):
@@ -150,7 +132,6 @@
 
     for place, t in enumerate(edge):
         work.sector(t, (count + place) * nvec, mine, theirs)
-    work.finish(mine.shape[0], mine, theirs)
 
 
 def products(kernel, early, jobs, me, shifts, active, psi, left, right, *more):
@@ -163,19 +144,17 @@
         functools.partial(kernel, early),
         out_shape=(out, out),
         in_specs=[smem] * 3 + [hbm] * 3 + [hbm] * len(more),
-        out_specs=(hbm, hbm),
+        out_specs=(pl.BlockSpec(memory_space=pltpu.VMEM),) * 2,
         scratch_shapes=[
             pltpu.VMEM((psi.shape[0], sectors + 2 * QMAX, blk, blk), B16),
             pltpu.VMEM((count, sectors, blk, blk), B16),
             pltpu.VMEM((count, sectors, blk, blk), B16),
-            pltpu.VMEM((2, jobs, blk, half), B16),
             pltpu.SemaphoreType.DMA((sectors,)),
             pltpu.SemaphoreType.DMA((sectors,)),
             pltpu.SemaphoreType.DMA((sectors,)),
-            pltpu.SemaphoreType.DMA((2, jobs)),
         ]
         + ([pltpu.SemaphoreType.DMA((2,))] if more else []),
-        compiler_params=pltpu.CompilerParams(vmem_limit_bytes=60 * 2**20),
+        compiler_params=pltpu.CompilerParams(vmem_limit_bytes=40 * 2**20),
         cost_estimate=pl.CostEstimate(flops=2 * jobs * 2 * count * blk**3, bytes_accessed=12 * 2**20, transcendentals=0),
         name=kernel.__name__,
     )(me, shifts, active, psi, left, right, *more)
@@ -195,6 +174,22 @@
     store = pltpu.make_async_copy(obuf, owned, sem.at[0])
     store.start()
     store.wait()
+
+
+def after_kernel(value, earlier, out):
+    pass
+
+
+def after(value, earlier):
+    hbm = pl.BlockSpec(memory_space=pl.ANY)
+    return pl.pallas_call(
+        after_kernel,
+        out_shape=jax.ShapeDtypeStruct(value.shape, value.dtype),
+        in_specs=[hbm, hbm],
+        out_specs=hbm,
+        input_output_aliases={0: 0},
+        name="after",
+    )(value, earlier)
 
 
 def combine(pairs, size, *behind):
@@ -217,25 +212,22 @@
 
 def arrange_kernel(plans, sectors, *refs):
     count = len(plans)
-    views, out, bufs, (acc, obuf, sem) = refs[:count], refs[count], refs[count + 1 : 2 * count + 1], refs[2 * count + 1 :]
-    size, _, share, _ = bufs[0].shape
-    loads = [pltpu.make_async_copy(view, buf, sem.at[index]) for index, (view, buf) in enumerate(zip(views, bufs))]
-    for copy in loads:
-        copy.start()
-    for copy in loads:
-        copy.wait()
-
-    def body(source, carry):
-        for buf, jobs in zip(bufs, plans):
-            for job, (v, t) in enumerate(jobs):
-                acc[v, pl.ds(source * sectors + t, share, stride=size * sectors), :] = buf[source, job].astype(F32)
-        return carry
-
-    lax.fori_loop(0, size, body, 0)
+    views, out, (acc, obuf, sem) = refs[:count], refs[count], refs[count + 1 :]
+    size, _, share, _ = views[0].shape
     stores = []
-    for v in range(obuf.shape[0]):
-        obuf[v] = acc[v].astype(B16)
-        stores.append(pltpu.make_async_copy(obuf.at[v], out.at[v], sem.at[count + v]))
+    for vector in range(obuf.shape[0]):
+
+        def body(source, carry, vector=vector):
+            for view, jobs in zip(views, plans):
+                for job, (v, t) in enumerate(jobs):
+                    if v == vector:
+                        rows = pl.ds(source * sectors + t, share, stride=size * sectors)
+                        acc[vector, rows, :] = view[source, job].astype(F32)
+            return carry
+
+        lax.fori_loop(0, size, body, 0, unroll=2)
+        obuf[vector] = acc[vector].astype(B16)
+        stores.append(pltpu.make_async_copy(obuf.at[vector], out.at[vector], sem.at[vector]))
         stores[-1].start()
     for copy in stores:
         copy.wait()
@@ -244,17 +236,15 @@
 def arrange(plans, views, nvec, sectors):
     size, _, share, half = views[0].shape
     rows = share * size * sectors
-    hbm = pl.BlockSpec(memory_space=pl.ANY)
     out = pl.pallas_call(
         functools.partial(arrange_kernel, plans, sectors),
         out_shape=jax.ShapeDtypeStruct((nvec, rows, half), B16),
-        in_specs=[hbm] * len(views),
-        out_specs=hbm,
-        scratch_shapes=[pltpu.VMEM(view.shape, B16) for view in views]
-        + [
+        in_specs=[pl.BlockSpec(memory_space=pltpu.VMEM)] * len(views),
+        out_specs=pl.BlockSpec(memory_space=pl.ANY),
+        scratch_shapes=[
             pltpu.VMEM((nvec, rows, half), F32),
             pltpu.VMEM((nvec, rows, half), B16),
-            pltpu.SemaphoreType.DMA((len(views) + nvec,)),
+            pltpu.SemaphoreType.DMA((nvec,)),
         ],
         compiler_params=pltpu.CompilerParams(vmem_limit_bytes=24 * 2**20),
         name="arrange",
@@ -291,26 +281,21 @@
     sec = lax.axis_index("sec")
     place = jnp.stack([me, (sec == 0).astype(jnp.int32), (sec == size - 1).astype(jnp.int32)])
     state = (place, shifts, active, psi, left_ops, right_ops)
-    early = 4
+    early = 3
     first, rest = plan(nvec, sectors, early)
 
-    def fence(make, jobs, *operands):
-        zeros = lambda *_: (jnp.zeros((len(jobs), blk, half), B16),) * 2
+    def fence(kernel, jobs, *operands):
+        def make(*operands):
+            mine, theirs = products(kernel, early, len(jobs), *operands)
+            return combine([(mine, swap(theirs))], size)
+
+        zeros = lambda *_: jnp.zeros((size, len(jobs), blk // size, half), B16)
         return lax.cond(sec < size, make, zeros, *operands)
 
-    def begin(*state):
-        mine, theirs = products(first_kernel, early, len(first), *state)
-        return mine, swap(theirs)
-
-    def go_on(*state):
-        mine, theirs = products(second_kernel, early, len(rest), *state)
-        return mine, swap(theirs)
-
     halo = fetch(psi, me)
-    owned = combine([fence(begin, first, *state)], size, halo)
+    owned = after(fence(first_kernel, first, *state), halo)
     views = [lax.all_to_all(owned, "sec", split_axis=0, concat_axis=0, tiled=True)]
-    pair = fence(go_on, rest, *state, halo, swap(halo))
-    owned = combine([pair], size)
+    owned = fence(second_kernel, rest, *state, halo, swap(halo))
     views.append(lax.all_to_all(owned, "sec", split_axis=0, concat_axis=0, tiled=True))
     return arrange([first, rest], views, nvec, sectors)
 

time: 73.8 us -> 69.3 us (0.939)
  Pallas kernels: 26 us -> 19 us
  blocking collectives: 25 us -> 29.5 us
  waiting for transfers between devices: 12 us -> 9.26 us
    all_to_all x1, blocking collectives: 25 us -> 29.5 us  [per_device(): lax.all_to_all(owned, 'sec', split_axis=0, concat_axis=0, tiled=True)]
    pallas_call x2, Pallas kernels: 18 us -> 13.9 us  [products(): pl.pallas_call(functools.partial(kernel, early), out_shape=(out, out), in...]
    all_to_all x1, waiting for transfers between devices: 5.19 us -> 2.56 us  [per_device(): lax.all_to_all(owned, 'sec', split_axis=0, concat_axis=0, tiled=True)]
    pallas_call x2, Pallas kernels: 3.6 us -> 1.5 us  [combine(): pl.pallas_call(functools.partial(combine_kernel, len(pairs), len(behind))...]
    pallas_call x1, Pallas kernels: 4.42 us -> 3.59 us  [arrange(): pl.pallas_call(functools.partial(arrange_kernel, plans, sectors), out_sha...]
  transfers between devices with their start and end apart: 5 -> 5, of which waited for: 4 -> 5; matrix products, arithmetic and copies ran while one was open for 0% -> 0% of each run, Pallas kernels for 26% -> 22%
where the time goes in v4:
time: 69.3 us; the launch traced here: 68.9 us
  blocking collectives  29.5 us (43%)
  Pallas kernels  19 us (27%)
  starting transfers between devices  10 us (14%)
  waiting for transfers between devices  9.26 us (13%)
  local copies, waits for them, and re-layouts  1.02 us (1%)
    all_to_all x1, blocking collectives, per_device(): lax.all_to_all(owned, 'sec', split_axis=0, concat_axis=0, tiled=True)  29.5 us
    pallas_call x2, Pallas kernels, products(): pl.pallas_call(functools.partial(kernel, early), out_shape=(out, out), in...  13.9 us
    all_to_all x1, starting transfers between devices, per_device(): lax.all_to_all(owned, 'sec', split_axis=0, concat_axis=0, tiled=True)  6.66 us
    ppermute x3, waiting for transfers between devices, swap(): return lax.ppermute(value, 'op', [(0, 1), (1, 0)])  6.13 us
    pallas_call x1, Pallas kernels, arrange(): pl.pallas_call(functools.partial(arrange_kernel, plans, sectors), out_sha...  3.59 us
    ppermute x1, starting transfers between devices, fetch(): return lax.ppermute(part, ('op', 'sec'), ahead + turns + back)  2.99 us
    all_to_all x1, waiting for transfers between devices, per_device(): lax.all_to_all(owned, 'sec', split_axis=0, concat_axis=0, tiled=True)  2.56 us
    pallas_call x2, Pallas kernels, combine(): pl.pallas_call(functools.partial(combine_kernel, len(pairs), len(behind))...  1.5 us
  transfers between devices with their start and end apart: 5, of which 5 were waited for; matrix products, arithmetic and copies ran while one was open for 0% of the time, Pallas kernels for 22%

profile of v4, /device:TPU:0, one launch (start us, length us, event | category | flops | bytes accessed | tf_op | source)
XLA Modules:
  0.0 68.9 jit_solution(2917592143277700751)
XLA Ops:
  0.0 1.0 %constant_dynamic-slice_fusion = bf16[3,1,256,256]{3,2,1,0:T(8,128)(2,1)S(1)} fusion(bf16[3,8,256,256]{3,2,1,0:T(8,128)(2,1)} %param.9, s32[]{:T(128)S(6)} %select_n.3), kind=kLoop, calls=%fused_computation.1 | loop fusion | bytes 786436 | tf_op jit(solution)/shard_map/dynamic_slice | solution.py:28
  1.0 3.0 %collective-permute-start.2 = (bf16[3,1,256,256]{3,2,1,0:T(8,128)(2,1)S(1)}, bf16[3,1,256,256]{3,2,1,0:T(8,128)(2,1)S(1)}, u32[]{:S(2)}, u32[]{:S(2)}) collective-permute-start(bf16[3,1,256,256]{3,2,1,0:T(8,128)(2,1)S(1)} %constant_dynamic-slice_fusion), channel_id=1, source_target_pairs={{0,1},{1,2},{2,3},{3,4},{4,5},{5,6},{6,7},{7,8},{8,9},{9,10},{10,1... | collective-permute-start | bytes 1179656 | tf_op jit(solution)/shard_map/ppermute | solution.py:29
  4.0 0.1 pad_add_fusion
  4.1 8.9 %conditional.2 = (bf16[16,9,16,128]{3,2,1,0:T(8,128)(2,1)}) conditional(s32[]{:T(128)} %convert_element_type.2, () %tuple.17, (s32[3]{0:T(128)S(1)}, s32[4]{0:T(128)}, s32[4,8]{1,0:T(4,128)}, bf16[3,8,256,256]{3,2,1,0:T(8,128)(2,1)}, bf16[4,8,256,256]{3,2,1,0:T(8,128)(2,1)}, /*index=5*/bf16[4,8,256,256]{3,2,1,0:T(8,128)(2,1)}) %tuple.18), branch_computations={%region_0.0_spmd, %region_1.0_spmd} | conditional | flops 2415919104 | bytes 14942256 | solution.py:293
  4.1 5.8 %first_kernel.1 = (bf16[9,256,128]{2,1,0:T(8,128)(2,1)S(1)}, bf16[9,256,128]{2,1,0:T(8,128)(2,1)S(1)}) custom-call(s32[3]{0:T(128)S(1)} %get-tuple-element.38.me_ref, s32[4]{0:T(128)} %get-tuple-element.40.shifts, s32[4,8]{1,0:T(4,128)} %get-tuple-element.41.active, bf16[3,8,256,256]{3,2,1,0:T(8,128)(2,1)} %get-tuple-element.42.psi, ...), custom_call_target="tpu_custom_call" | custom-call | flops 2415919104 | bytes 12582912 | tf_op jit(solution)/shard_map/cond/branch_1_fun/first_kernel/pallas_call | solution.py:143
  9.9 0.1 collective-permute-start
  10.0 2.0 %collective-permute-done.refs_1_ = bf16[9,256,128]{2,1,0:T(8,128)(2,1)S(1)} collective-permute-done((bf16[9,256,128]{2,1,0:T(8,128)(2,1)S(1)}, bf16[9,256,128]{2,1,0:T(8,128)(2,1)S(1)}, u32[]{:S(2)}, u32[]{:S(2)}) %collective-permute-start) | collective-permute-done | bytes 589856 | tf_op jit(solution)/shard_map/cond/branch_1_fun/ppermute | solution.py:33
  12.0 1.0 %combine.2 = bf16[16,9,16,128]{3,2,1,0:T(8,128)(2,1)} custom-call(bf16[9,256,128]{2,1,0:T(8,128)(2,1)S(1)} %get-tuple-element.45.refs_0_, bf16[9,256,128]{2,1,0:T(8,128)(2,1)S(1)} %collective-permute-done.refs_1_), custom_call_target="tpu_custom_call" | custom-call | tf_op jit(solution)/shard_map/cond/branch_1_fun/combine/pallas_call | solution.py:201
  13.0 0.6 collective-permute-done.2.earlier
  13.5 6.7 %all-to-all-start = ((bf16[16,9,16,128]{3,2,1,0:T(8,128)(2,1)}), bf16[16,9,16,128]{3,2,1,0:T(8,128)(2,1)S(1)}, u32[]{:S(2)}, u32[]{:S(2)}) async-start(bf16[16,9,16,128]{3,2,1,0:T(8,128)(2,1)} %after.1), calls=%async_computation | async-start | bytes 1179648 | tf_op jit(solution)/shard_map/all_to_all | solution.py:297
  20.2 0.1 collective-permute-start.3
  20.3 1.7 %collective-permute-done.3 = bf16[3,1,256,256]{3,2,1,0:T(8,128)(2,1)S(1)} collective-permute-done((bf16[3,1,256,256]{3,2,1,0:T(8,128)(2,1)S(1)}, bf16[3,1,256,256]{3,2,1,0:T(8,128)(2,1)S(1)}, u32[]{:S(2)}, u32[]{:S(2)}) %collective-permute-start.3) | collective-permute-done | bytes 393248 | tf_op jit(solution)/shard_map/ppermute | solution.py:33
  22.0 11.3 %conditional.3 = (bf16[16,15,16,128]{3,2,1,0:T(8,128)(2,1)S(1)}) conditional(s32[]{:T(128)} %convert_element_type.2, () %tuple.19, (s32[3]{0:T(128)S(1)}, s32[4]{0:T(128)}, s32[4,8]{1,0:T(4,128)}, bf16[3,8,256,256]{3,2,1,0:T(8,128)(2,1)}, bf16[4,8,256,256]{3,2,1,0:T(8,128)(2,1)}, /*index=5*/bf16[4,8,256,256]{3,2,1,0:T(8,128)(2,1)}, ...), branch_computations={%region_2.0_spmd, %region_3.0_spmd} | conditional | flops 4026531840 | bytes 16515120 | solution.py:293
  22.0 8.1 %second_kernel.1 = (bf16[15,256,128]{2,1,0:T(8,128)(2,1)S(1)}, bf16[15,256,128]{2,1,0:T(8,128)(2,1)S(1)}) custom-call(s32[3]{0:T(128)S(1)} %get-tuple-element.47.me_ref, s32[4]{0:T(128)} %get-tuple-element.48.shifts, s32[4,8]{1,0:T(4,128)} %get-tuple-element.49.active, bf16[3,8,256,256]{3,2,1,0:T(8,128)(2,1)} %get-tuple-element.50.psi, ...), custom_call_target="tpu_custom_call" | custom-call | flops 4026531840 | bytes 12582912 | tf_op jit(solution)/shard_map/cond/branch_1_fun/second_kernel/pallas_call | solution.py:143
  30.1 0.2 collective-permute-start.1
  30.3 2.4 %collective-permute-done.1.refs_1_ = bf16[15,256,128]{2,1,0:T(8,128)(2,1)S(1)} collective-permute-done((bf16[15,256,128]{2,1,0:T(8,128)(2,1)S(1)}, bf16[15,256,128]{2,1,0:T(8,128)(2,1)S(1)}, u32[]{:S(2)}, u32[]{:S(2)}) %collective-permute-start.1) | collective-permute-done | bytes 983072 | tf_op jit(solution)/shard_map/cond/branch_1_fun/ppermute | solution.py:33
  32.7 0.5 combine.3
  33.3 2.6 %all-to-all-done.refs_0_ = bf16[16,9,16,128]{3,2,1,0:T(8,128)(2,1)S(1)} async-done(((bf16[16,9,16,128]{3,2,1,0:T(8,128)(2,1)}), bf16[16,9,16,128]{3,2,1,0:T(8,128)(2,1)S(1)}, u32[]{:S(2)}, u32[]{:S(2)}) %all-to-all-start) | async-done | bytes 589856 | tf_op jit(solution)/shard_map/all_to_all | solution.py:297
  35.8 29.5 %all_to_all.10.refs_1_ = bf16[16,15,16,128]{3,2,1,0:T(8,128)(2,1)S(1)} all-to-all(bf16[16,15,16,128]{3,2,1,0:T(8,128)(2,1)S(1)} %get-tuple-element.58), channel_id=1, replica_groups=mesh['op'=2,'sec'=16] {'sec'}, dimensions={0} | all-to-all | bytes 1966080 | tf_op jit(solution)/shard_map/all_to_all | solution.py:299
  65.3 3.6 %arrange.1 = bf16[3,2048,128]{2,1,0:T(8,128)(2,1)} custom-call(bf16[16,9,16,128]{3,2,1,0:T(8,128)(2,1)S(1)} %all-to-all-done.refs_0_, bf16[16,15,16,128]{3,2,1,0:T(8,128)(2,1)S(1)} %all_to_all.10.refs_1_), custom_call_target="tpu_custom_call" | custom-call | tf_op jit(solution)/shard_map/arrange/pallas_call | solution.py:239
  (1 shorter events, 0.0 us)
Async XLA Ops:
  1.0 12.5 %collective-permute-start.2 = (bf16[3,1,256,256]{3,2,1,0:T(8,128)(2,1)S(1)}, bf16[3,1,256,256]{3,2,1,0:T(8,128)(2,1)S(1)}, u32[]{:S(2)}, u32[]{:S(2)}) collective-permute-start(bf16[3,1,256,256]{3,2,1,0:T(8,128)(2,1)S(1)} %constant_dynamic-slice_fusion), channel_id=1, source_target_pairs={{0,1},{1,2},{2,3},{3,4},{4,5},{5,6},{6,7},{7,8},{8,9},{9,10},{10,1... | collective-permute-start | bytes 1179656 | tf_op jit(solution)/shard_map/ppermute | solution.py:29
  9.9 2.1 %collective-permute-start = (bf16[9,256,128]{2,1,0:T(8,128)(2,1)S(1)}, bf16[9,256,128]{2,1,0:T(8,128)(2,1)S(1)}, u32[]{:S(2)}, u32[]{:S(2)}) collective-permute-start(bf16[9,256,128]{2,1,0:T(8,128)(2,1)S(1)} %get-tuple-element.46), channel_id=1, source_target_pairs={{0,16},{16,0},{1,17},{17,1},{2,18},{18,2},{3,19},{19,3},{4,20},{20... | collective-permute-start | bytes 1769480 | tf_op jit(solution)/shard_map/cond/branch_1_fun/ppermute | solution.py:33
  13.5 22.3 %all-to-all-start = ((bf16[16,9,16,128]{3,2,1,0:T(8,128)(2,1)}), bf16[16,9,16,128]{3,2,1,0:T(8,128)(2,1)S(1)}, u32[]{:S(2)}, u32[]{:S(2)}) async-start(bf16[16,9,16,128]{3,2,1,0:T(8,128)(2,1)} %after.1), calls=%async_computation | async-start | bytes 1179648 | tf_op jit(solution)/shard_map/all_to_all | solution.py:297
  20.2 1.8 %collective-permute-start.3 = (bf16[3,1,256,256]{3,2,1,0:T(8,128)(2,1)S(1)}, bf16[3,1,256,256]{3,2,1,0:T(8,128)(2,1)S(1)}, u32[]{:S(2)}, u32[]{:S(2)}) collective-permute-start(bf16[3,1,256,256]{3,2,1,0:T(8,128)(2,1)S(1)} %collective-permute-done.2.earlier), channel_id=1, source_target_pairs={{0,16},{16,0},{1,17},{17,1},{2,18},{18,2},{3,19},{19,3},{4,20},{20... | collective-permute-start | bytes 1179656 | tf_op jit(solution)/shard_map/ppermute | solution.py:33
  30.1 2.6 %collective-permute-start.1 = (bf16[15,256,128]{2,1,0:T(8,128)(2,1)S(1)}, bf16[15,256,128]{2,1,0:T(8,128)(2,1)S(1)}, u32[]{:S(2)}, u32[]{:S(2)}) collective-permute-start(bf16[15,256,128]{2,1,0:T(8,128)(2,1)S(1)} %get-tuple-element.56), channel_id=1, source_target_pairs={{0,16},{16,0},{1,17},{17,1},{2,18},{18,2},{3,19},{19,3},{4,20},{20... | collective-permute-start | bytes 2949128 | tf_op jit(solution)/shard_map/cond/branch_1_fun/ppermute | solution.py:33

commit v5 on v4

--- a/solution.py
+++ b/solution.py
@@ -218,15 +218,16 @@
     for vector in range(obuf.shape[0]):
 
         def body(source, carry, vector=vector):
+            base = source * share * sectors
             for view, jobs in zip(views, plans):
                 for job, (v, t) in enumerate(jobs):
                     if v == vector:
-                        rows = pl.ds(source * sectors + t, share, stride=size * sectors)
-                        acc[vector, rows, :] = view[source, job].astype(F32)
+                        acc[vector, pl.ds(base + t, share, stride=sectors), :] = view[source, job].astype(F32)
             return carry
 
         lax.fori_loop(0, size, body, 0, unroll=2)
-        obuf[vector] = acc[vector].astype(B16)
+        tiles = acc[vector].reshape(size, share, sectors, acc.shape[2])
+        obuf[vector] = jnp.swapaxes(tiles, 0, 1).reshape(obuf.shape[1:]).astype(B16)
         stores.append(pltpu.make_async_copy(obuf.at[vector], out.at[vector], sem.at[vector]))
         stores[-1].start()
     for copy in stores:
@@ -275,7 +276,7 @@
 def per_device(psi, left_ops, right_ops, shifts, active):
     nvec, sectors, blk, _ = psi.shape
     size, half = lax.axis_size("sec"), blk // 2
-    if lax.axis_size("op") != 2 or sectors <= 2 * QMAX or blk % (16 * size):
+    if lax.axis_size("op") != 2 or sectors != 8 or blk % (16 * size):
         return general(psi, left_ops, right_ops, shifts, active)
     me = lax.axis_index("op")
     sec = lax.axis_index("sec")

time: 69.3 us -> 67.2 us (0.970)
  Pallas kernels: 19 us -> 17 us
    pallas_call x1, Pallas kernels: 3.59 us -> 1.57 us  [arrange(): pl.pallas_call(functools.partial(arrange_kernel, plans, sectors), out_sha...]
  transfers between devices with their start and end apart: 5 -> 5, of which waited for: 5 -> 5; matrix products, arithmetic and copies ran while one was open for 0% -> 0% of each run, Pallas kernels for 22% -> 23%
where the time goes in v5:
time: 67.2 us; the launch traced here: 66.9 us
  blocking collectives  29.5 us (44%)
  Pallas kernels  17 us (25%)
  starting transfers between devices  10 us (15%)
  waiting for transfers between devices  9.26 us (14%)
  local copies, waits for them, and re-layouts  1.02 us (2%)
    all_to_all x1, blocking collectives, per_device(): lax.all_to_all(owned, 'sec', split_axis=0, concat_axis=0, tiled=True)  29.5 us
    pallas_call x2, Pallas kernels, products(): pl.pallas_call(functools.partial(kernel, early), out_shape=(out, out), in...  13.9 us
    all_to_all x1, starting transfers between devices, per_device(): lax.all_to_all(owned, 'sec', split_axis=0, concat_axis=0, tiled=True)  6.66 us
    ppermute x3, waiting for transfers between devices, swap(): return lax.ppermute(value, 'op', [(0, 1), (1, 0)])  6.13 us
    ppermute x1, starting transfers between devices, fetch(): return lax.ppermute(part, ('op', 'sec'), ahead + turns + back)  2.99 us
    all_to_all x1, waiting for transfers between devices, per_device(): lax.all_to_all(owned, 'sec', split_axis=0, concat_axis=0, tiled=True)  2.56 us
    pallas_call x1, Pallas kernels, arrange(): pl.pallas_call(functools.partial(arrange_kernel, plans, sectors), out_sha...  1.57 us
    pallas_call x2, Pallas kernels, combine(): pl.pallas_call(functools.partial(combine_kernel, len(pairs), len(behind))...  1.5 us
  transfers between devices with their start and end apart: 5, of which 5 were waited for; matrix products, arithmetic and copies ran while one was open for 0% of the time, Pallas kernels for 23%

profile of v5, /device:TPU:0, one launch (start us, length us, event | category | flops | bytes accessed | tf_op | source)
XLA Modules:
  0.0 66.9 jit_solution(6245990215976825798)
XLA Ops:
  0.0 1.0 %constant_dynamic-slice_fusion = bf16[3,1,256,256]{3,2,1,0:T(8,128)(2,1)S(1)} fusion(bf16[3,8,256,256]{3,2,1,0:T(8,128)(2,1)} %param.9, s32[]{:T(128)S(6)} %select_n.3), kind=kLoop, calls=%fused_computation.1 | loop fusion | bytes 786436 | tf_op jit(solution)/shard_map/dynamic_slice | solution.py:28
  1.0 3.0 %collective-permute-start.2 = (bf16[3,1,256,256]{3,2,1,0:T(8,128)(2,1)S(1)}, bf16[3,1,256,256]{3,2,1,0:T(8,128)(2,1)S(1)}, u32[]{:S(2)}, u32[]{:S(2)}) collective-permute-start(bf16[3,1,256,256]{3,2,1,0:T(8,128)(2,1)S(1)} %constant_dynamic-slice_fusion), channel_id=1, source_target_pairs={{0,1},{1,2},{2,3},{3,4},{4,5},{5,6},{6,7},{7,8},{8,9},{9,10},{10,1... | collective-permute-start | bytes 1179656 | tf_op jit(solution)/shard_map/ppermute | solution.py:29
  4.0 0.1 pad_add_fusion
  4.1 8.9 %conditional.2 = (bf16[16,9,16,128]{3,2,1,0:T(8,128)(2,1)}) conditional(s32[]{:T(128)} %convert_element_type.2, () %tuple.17, (s32[3]{0:T(128)S(1)}, s32[4]{0:T(128)}, s32[4,8]{1,0:T(4,128)}, bf16[3,8,256,256]{3,2,1,0:T(8,128)(2,1)}, bf16[4,8,256,256]{3,2,1,0:T(8,128)(2,1)}, /*index=5*/bf16[4,8,256,256]{3,2,1,0:T(8,128)(2,1)}) %tuple.18), branch_computations={%region_0.0_spmd, %region_1.0_spmd} | conditional | flops 2415919104 | bytes 14942256 | solution.py:294
  4.1 5.8 %first_kernel.1 = (bf16[9,256,128]{2,1,0:T(8,128)(2,1)S(1)}, bf16[9,256,128]{2,1,0:T(8,128)(2,1)S(1)}) custom-call(s32[3]{0:T(128)S(1)} %get-tuple-element.38.me_ref, s32[4]{0:T(128)} %get-tuple-element.40.shifts, s32[4,8]{1,0:T(4,128)} %get-tuple-element.41.active, bf16[3,8,256,256]{3,2,1,0:T(8,128)(2,1)} %get-tuple-element.42.psi, ...), custom_call_target="tpu_custom_call" | custom-call | flops 2415919104 | bytes 12582912 | tf_op jit(solution)/shard_map/cond/branch_1_fun/first_kernel/pallas_call | solution.py:143
  9.9 0.1 collective-permute-start
  10.0 2.0 %collective-permute-done.refs_1_ = bf16[9,256,128]{2,1,0:T(8,128)(2,1)S(1)} collective-permute-done((bf16[9,256,128]{2,1,0:T(8,128)(2,1)S(1)}, bf16[9,256,128]{2,1,0:T(8,128)(2,1)S(1)}, u32[]{:S(2)}, u32[]{:S(2)}) %collective-permute-start) | collective-permute-done | bytes 589856 | tf_op jit(solution)/shard_map/cond/branch_1_fun/ppermute | solution.py:33
  12.0 1.0 %combine.2 = bf16[16,9,16,128]{3,2,1,0:T(8,128)(2,1)} custom-call(bf16[9,256,128]{2,1,0:T(8,128)(2,1)S(1)} %get-tuple-element.45.refs_0_, bf16[9,256,128]{2,1,0:T(8,128)(2,1)S(1)} %collective-permute-done.refs_1_), custom_call_target="tpu_custom_call" | custom-call | tf_op jit(solution)/shard_map/cond/branch_1_fun/combine/pallas_call | solution.py:201
  13.0 0.6 collective-permute-done.2.earlier
  13.5 6.7 %all-to-all-start = ((bf16[16,9,16,128]{3,2,1,0:T(8,128)(2,1)}), bf16[16,9,16,128]{3,2,1,0:T(8,128)(2,1)S(1)}, u32[]{:S(2)}, u32[]{:S(2)}) async-start(bf16[16,9,16,128]{3,2,1,0:T(8,128)(2,1)} %after.1), calls=%async_computation | async-start | bytes 1179648 | tf_op jit(solution)/shard_map/all_to_all | solution.py:298
  20.2 0.1 collective-permute-start.3
  20.3 1.7 %collective-permute-done.3 = bf16[3,1,256,256]{3,2,1,0:T(8,128)(2,1)S(1)} collective-permute-done((bf16[3,1,256,256]{3,2,1,0:T(8,128)(2,1)S(1)}, bf16[3,1,256,256]{3,2,1,0:T(8,128)(2,1)S(1)}, u32[]{:S(2)}, u32[]{:S(2)}) %collective-permute-start.3) | collective-permute-done | bytes 393248 | tf_op jit(solution)/shard_map/ppermute | solution.py:33
  22.0 11.3 %conditional.3 = (bf16[16,15,16,128]{3,2,1,0:T(8,128)(2,1)S(1)}) conditional(s32[]{:T(128)} %convert_element_type.2, () %tuple.19, (s32[3]{0:T(128)S(1)}, s32[4]{0:T(128)}, s32[4,8]{1,0:T(4,128)}, bf16[3,8,256,256]{3,2,1,0:T(8,128)(2,1)}, bf16[4,8,256,256]{3,2,1,0:T(8,128)(2,1)}, /*index=5*/bf16[4,8,256,256]{3,2,1,0:T(8,128)(2,1)}, ...), branch_computations={%region_2.0_spmd, %region_3.0_spmd} | conditional | flops 4026531840 | bytes 16515120 | solution.py:294
  22.0 8.1 %second_kernel.1 = (bf16[15,256,128]{2,1,0:T(8,128)(2,1)S(1)}, bf16[15,256,128]{2,1,0:T(8,128)(2,1)S(1)}) custom-call(s32[3]{0:T(128)S(1)} %get-tuple-element.47.me_ref, s32[4]{0:T(128)} %get-tuple-element.48.shifts, s32[4,8]{1,0:T(4,128)} %get-tuple-element.49.active, bf16[3,8,256,256]{3,2,1,0:T(8,128)(2,1)} %get-tuple-element.50.psi, ...), custom_call_target="tpu_custom_call" | custom-call | flops 4026531840 | bytes 12582912 | tf_op jit(solution)/shard_map/cond/branch_1_fun/second_kernel/pallas_call | solution.py:143
  30.1 0.2 collective-permute-start.1
  30.3 2.4 %collective-permute-done.1.refs_1_ = bf16[15,256,128]{2,1,0:T(8,128)(2,1)S(1)} collective-permute-done((bf16[15,256,128]{2,1,0:T(8,128)(2,1)S(1)}, bf16[15,256,128]{2,1,0:T(8,128)(2,1)S(1)}, u32[]{:S(2)}, u32[]{:S(2)}) %collective-permute-start.1) | collective-permute-done | bytes 983072 | tf_op jit(solution)/shard_map/cond/branch_1_fun/ppermute | solution.py:33
  32.7 0.5 combine.3
  33.3 2.6 %all-to-all-done.refs_0_ = bf16[16,9,16,128]{3,2,1,0:T(8,128)(2,1)S(1)} async-done(((bf16[16,9,16,128]{3,2,1,0:T(8,128)(2,1)}), bf16[16,9,16,128]{3,2,1,0:T(8,128)(2,1)S(1)}, u32[]{:S(2)}, u32[]{:S(2)}) %all-to-all-start) | async-done | bytes 589856 | tf_op jit(solution)/shard_map/all_to_all | solution.py:298
  35.8 29.5 %all_to_all.10.refs_1_ = bf16[16,15,16,128]{3,2,1,0:T(8,128)(2,1)S(1)} all-to-all(bf16[16,15,16,128]{3,2,1,0:T(8,128)(2,1)S(1)} %get-tuple-element.58), channel_id=1, replica_groups=mesh['op'=2,'sec'=16] {'sec'}, dimensions={0} | all-to-all | bytes 1966080 | tf_op jit(solution)/shard_map/all_to_all | solution.py:300
  65.3 1.6 %arrange.1 = bf16[3,2048,128]{2,1,0:T(8,128)(2,1)} custom-call(bf16[16,9,16,128]{3,2,1,0:T(8,128)(2,1)S(1)} %all-to-all-done.refs_0_, bf16[16,15,16,128]{3,2,1,0:T(8,128)(2,1)S(1)} %all_to_all.10.refs_1_), custom_call_target="tpu_custom_call" | custom-call | tf_op jit(solution)/shard_map/arrange/pallas_call | solution.py:240
  (1 shorter events, 0.0 us)
Async XLA Ops:
  1.0 12.5 %collective-permute-start.2 = (bf16[3,1,256,256]{3,2,1,0:T(8,128)(2,1)S(1)}, bf16[3,1,256,256]{3,2,1,0:T(8,128)(2,1)S(1)}, u32[]{:S(2)}, u32[]{:S(2)}) collective-permute-start(bf16[3,1,256,256]{3,2,1,0:T(8,128)(2,1)S(1)} %constant_dynamic-slice_fusion), channel_id=1, source_target_pairs={{0,1},{1,2},{2,3},{3,4},{4,5},{5,6},{6,7},{7,8},{8,9},{9,10},{10,1... | collective-permute-start | bytes 1179656 | tf_op jit(solution)/shard_map/ppermute | solution.py:29
  9.9 2.1 %collective-permute-start = (bf16[9,256,128]{2,1,0:T(8,128)(2,1)S(1)}, bf16[9,256,128]{2,1,0:T(8,128)(2,1)S(1)}, u32[]{:S(2)}, u32[]{:S(2)}) collective-permute-start(bf16[9,256,128]{2,1,0:T(8,128)(2,1)S(1)} %get-tuple-element.46), channel_id=1, source_target_pairs={{0,16},{16,0},{1,17},{17,1},{2,18},{18,2},{3,19},{19,3},{4,20},{20... | collective-permute-start | bytes 1769480 | tf_op jit(solution)/shard_map/cond/branch_1_fun/ppermute | solution.py:33
  13.5 22.3 %all-to-all-start = ((bf16[16,9,16,128]{3,2,1,0:T(8,128)(2,1)}), bf16[16,9,16,128]{3,2,1,0:T(8,128)(2,1)S(1)}, u32[]{:S(2)}, u32[]{:S(2)}) async-start(bf16[16,9,16,128]{3,2,1,0:T(8,128)(2,1)} %after.1), calls=%async_computation | async-start | bytes 1179648 | tf_op jit(solution)/shard_map/all_to_all | solution.py:298
  20.2 1.8 %collective-permute-start.3 = (bf16[3,1,256,256]{3,2,1,0:T(8,128)(2,1)S(1)}, bf16[3,1,256,256]{3,2,1,0:T(8,128)(2,1)S(1)}, u32[]{:S(2)}, u32[]{:S(2)}) collective-permute-start(bf16[3,1,256,256]{3,2,1,0:T(8,128)(2,1)S(1)} %collective-permute-done.2.earlier), channel_id=1, source_target_pairs={{0,16},{16,0},{1,17},{17,1},{2,18},{18,2},{3,19},{19,3},{4,20},{20... | collective-permute-start | bytes 1179656 | tf_op jit(solution)/shard_map/ppermute | solution.py:33
  30.1 2.6 %collective-permute-start.1 = (bf16[15,256,128]{2,1,0:T(8,128)(2,1)S(1)}, bf16[15,256,128]{2,1,0:T(8,128)(2,1)S(1)}, u32[]{:S(2)}, u32[]{:S(2)}) collective-permute-start(bf16[15,256,128]{2,1,0:T(8,128)(2,1)S(1)} %get-tuple-element.56), channel_id=1, source_target_pairs={{0,16},{16,0},{1,17},{17,1},{2,18},{18,2},{3,19},{19,3},{4,20},{20... | collective-permute-start | bytes 2949128 | tf_op jit(solution)/shard_map/cond/branch_1_fun/ppermute | solution.py:33

commit v6 on v5

--- a/solution.py
+++ b/solution.py
@@ -8,6 +8,7 @@
 from jax.sharding import PartitionSpec as P
 
 QMAX = 1
+NEAR = 4
 F32, B16 = jnp.float32, jnp.bfloat16
 
 
@@ -103,7 +104,7 @@
     work.inner(QMAX, early, mine, theirs)
 
 
-def second_kernel(early, me_ref, shifts, active, psi, left, right, halo, other, mine, theirs, *refs):
+def second_kernel(early, me_ref, shifts, active, psi, left, right, halo, other, earlier, mine, theirs, *refs):
     nvec, sectors = psi.shape[:2]
     me = me_ref[0]
     *refs, sem_h = refs
@@ -176,20 +177,20 @@
     store.wait()
 
 
-def after_kernel(value, earlier, out):
+def after_kernel(value, *refs):
     pass
 
 
-def after(value, earlier):
+def after(value, *earlier):
     hbm = pl.BlockSpec(memory_space=pl.ANY)
     return pl.pallas_call(
         after_kernel,
         out_shape=jax.ShapeDtypeStruct(value.shape, value.dtype),
-        in_specs=[hbm, hbm],
+        in_specs=[hbm] * (1 + len(earlier)),
         out_specs=hbm,
         input_output_aliases={0: 0},
         name="after",
-    )(value, earlier)
+    )(value, *earlier)
 
 
 def combine(pairs, size, *behind):
@@ -210,22 +211,77 @@
     )(*refs, *behind)
 
 
-def arrange_kernel(plans, sectors, *refs):
-    count = len(plans)
-    views, out, (acc, obuf, sem) = refs[:count], refs[count], refs[count + 1 :]
-    size, _, share, _ = views[0].shape
+def blocks_kernel(place, mine, other, *outs):
+    rows_of, near = len(outs), outs[0].shape[0]
+    share = outs[0].shape[2]
+    z, q = place[3], place[4]
+    for a, out in enumerate(outs):
+        for b in range(near):
+            to = lax.rem(z + a, rows_of) * near + lax.rem(q + b, near)
+            rows = pl.ds(pl.multiple_of(to * share, share), share)
+            out[b] = (mine[:, rows, :].astype(F32) + other[:, rows, :].astype(F32)).astype(B16)
+
+
+def blocks(place, mine, other, far, near):
+    jobs, blk, half = mine.shape
+    vmem = pl.BlockSpec(memory_space=pltpu.VMEM)
+    block = jax.ShapeDtypeStruct((near, jobs, blk // (far * near), half), B16)
+    return pl.pallas_call(
+        blocks_kernel,
+        out_shape=(block,) * far,
+        in_specs=[pl.BlockSpec(memory_space=pltpu.SMEM), vmem, vmem],
+        out_specs=(vmem,) * far,
+        compiler_params=pltpu.CompilerParams(vmem_limit_bytes=16 * 2**20),
+        cost_estimate=pl.CostEstimate(flops=0, bytes_accessed=0, transcendentals=0),
+        name="blocks",
+    )(place, mine, other)
+
+
+def regroup_kernel(far, *refs):
+    for b, out in enumerate(refs[far:]):
+        for a in range(far):
+            out[a] = refs[a][b]
+
+
+def regroup(parts):
+    near, *block = parts[0].shape
+    vmem = pl.BlockSpec(memory_space=pltpu.VMEM)
+    out = jax.ShapeDtypeStruct((len(parts), *block), B16)
+    return pl.pallas_call(
+        functools.partial(regroup_kernel, len(parts)),
+        out_shape=(out,) * near,
+        in_specs=[vmem] * len(parts),
+        out_specs=(vmem,) * near,
+        compiler_params=pltpu.CompilerParams(vmem_limit_bytes=16 * 2**20),
+        cost_estimate=pl.CostEstimate(flops=16 * 10**9, bytes_accessed=0, transcendentals=0),
+        name="regroup",
+    )(*parts)
+
+
+def arrange_kernel(plans, sectors, place, *refs):
+    view, pieces, (out, acc, obuf, sem) = refs[0], refs[1:-4], refs[-4:]
+    stepped, direct = plans
+    size, _, share, _ = view.shape
     stores = []
     for vector in range(obuf.shape[0]):
 
-        def body(source, carry, vector=vector):
-            base = source * share * sectors
-            for view, jobs in zip(views, plans):
-                for job, (v, t) in enumerate(jobs):
-                    if v == vector:
-                        acc[vector, pl.ds(base + t, share, stride=sectors), :] = view[source, job].astype(F32)
+        def put(source, job, value, vector=vector):
+            v, t = job
+            if v == vector:
+                acc[vector, pl.ds(source * share * sectors + t, share, stride=sectors), :] = value().astype(F32)
+
+        def body(source, carry):
+            for index, job in enumerate(direct):
+                put(source, job, lambda: view[source, index])
             return carry
 
         lax.fori_loop(0, size, body, 0, unroll=2)
+        near, far = len(pieces), pieces[0].shape[0]
+        for b, piece in enumerate(pieces):
+            for a in range(far):
+                source = lax.rem(place[3] + far - a, far) * near + lax.rem(place[4] + near - b, near)
+                for index, job in enumerate(stepped):
+                    put(source, job, lambda: piece[a, index])
         tiles = acc[vector].reshape(size, share, sectors, acc.shape[2])
         obuf[vector] = jnp.swapaxes(tiles, 0, 1).reshape(obuf.shape[1:]).astype(B16)
         stores.append(pltpu.make_async_copy(obuf.at[vector], out.at[vector], sem.at[vector]))
@@ -234,13 +290,14 @@
         copy.wait()
 
 
-def arrange(plans, views, nvec, sectors):
-    size, _, share, half = views[0].shape
+def arrange(plans, sectors, nvec, place, view, pieces):
+    size, _, share, half = view.shape
     rows = share * size * sectors
     out = pl.pallas_call(
         functools.partial(arrange_kernel, plans, sectors),
         out_shape=jax.ShapeDtypeStruct((nvec, rows, half), B16),
-        in_specs=[pl.BlockSpec(memory_space=pltpu.VMEM)] * len(views),
+        in_specs=[pl.BlockSpec(memory_space=pltpu.SMEM)]
+        + [pl.BlockSpec(memory_space=pltpu.VMEM)] * (1 + len(pieces)),
         out_specs=pl.BlockSpec(memory_space=pl.ANY),
         scratch_shapes=[
             pltpu.VMEM((nvec, rows, half), F32),
@@ -249,7 +306,7 @@
         ],
         compiler_params=pltpu.CompilerParams(vmem_limit_bytes=24 * 2**20),
         name="arrange",
-    )(*views)
+    )(place, view, *pieces)
     return out.reshape(nvec, share, size * sectors, half)
 
 
@@ -276,29 +333,48 @@
 def per_device(psi, left_ops, right_ops, shifts, active):
     nvec, sectors, blk, _ = psi.shape
     size, half = lax.axis_size("sec"), blk // 2
-    if lax.axis_size("op") != 2 or sectors != 8 or blk % (16 * size):
+    if lax.axis_size("op") != 2 or sectors != 8 or blk % (16 * size) or size % NEAR:
         return general(psi, left_ops, right_ops, shifts, active)
     me = lax.axis_index("op")
     sec = lax.axis_index("sec")
-    place = jnp.stack([me, (sec == 0).astype(jnp.int32), (sec == size - 1).astype(jnp.int32)])
+    place = jnp.stack([me, (sec == 0).astype(jnp.int32), (sec == size - 1).astype(jnp.int32), sec // NEAR, sec % NEAR])
     state = (place, shifts, active, psi, left_ops, right_ops)
     early = 3
     first, rest = plan(nvec, sectors, early)
-
-    def fence(kernel, jobs, *operands):
-        def make(*operands):
-            mine, theirs = products(kernel, early, len(jobs), *operands)
-            return combine([(mine, swap(theirs))], size)
-
-        zeros = lambda *_: jnp.zeros((size, len(jobs), blk // size, half), B16)
+    share, far = blk // size, size // NEAR
+
+    def fence(make, shape, *operands):
+        zeros = lambda *_: jax.tree.map(lambda one: jnp.zeros(one.shape, one.dtype), shape)
         return lax.cond(sec < size, make, zeros, *operands)
 
+    def begin(*state):
+        mine, theirs = products(first_kernel, early, len(first), *state)
+        return blocks(place, mine, swap(theirs), far, NEAR)
+
+    def go_on(*operands):
+        *state, halo, earlier = operands
+        mine, theirs = products(second_kernel, early, len(rest), *state, halo, swap(halo), earlier)
+        return combine([(mine, swap(theirs))], size)
+
+    def near_steps(*parts):
+        pieces = [*regroup(parts)]
+        for b in range(1, NEAR):
+            steps = [(i, i - i % NEAR + (i + b) % NEAR) for i in range(size)]
+            pieces[b] = lax.ppermute(pieces[b], "sec", steps)
+        return tuple(pieces)
+
     halo = fetch(psi, me)
-    owned = after(fence(first_kernel, first, *state), halo)
-    views = [lax.all_to_all(owned, "sec", split_axis=0, concat_axis=0, tiled=True)]
-    owned = fence(second_kernel, rest, *state, halo, swap(halo))
-    views.append(lax.all_to_all(owned, "sec", split_axis=0, concat_axis=0, tiled=True))
-    return arrange([first, rest], views, nvec, sectors)
+    block = jax.ShapeDtypeStruct((NEAR, len(first), share, half), B16)
+    parts = [*fence(begin, (block,) * far, *state)]
+    for a in range(1, far):
+        steps = [(i, (i + a * NEAR) % size) for i in range(size)]
+        parts[a] = lax.ppermute(parts[a], "sec", steps)
+    block = jax.ShapeDtypeStruct((size, len(rest), share, half), B16)
+    owned = after(fence(go_on, block, *state, halo, parts[0]), *parts[1:])
+    view = lax.all_to_all(owned, "sec", split_axis=0, concat_axis=0, tiled=True)
+    block = jax.ShapeDtypeStruct((far, len(first), share, half), B16)
+    pieces = fence(near_steps, (block,) * NEAR, *parts)
+    return arrange([first, rest], sectors, nvec, place, view, pieces)
 
 
 def solution(mesh):

time: 67.2 us -> 62.3 us (0.927)
  blocking collectives: 29.5 us -> 0 us
  waiting for transfers between devices: 9.26 us -> 24.7 us
  starting transfers between devices: 10 us -> 17.5 us
  Pallas kernels: 17 us -> 18.6 us
    all_to_all x1 -> x0, blocking collectives: 29.5 us -> none  [per_device(): lax.all_to_all(owned, 'sec', split_axis=0, concat_axis=0, tiled=True)]
    ppermute x0 -> x6, waiting for transfers between devices: none -> 12.3 us  [the longest x3 12.3 us: near_steps(): pieces[b] = lax.ppermute(pieces[b], 'sec', steps)]
    ppermute x0 -> x6, starting transfers between devices: none -> 10.5 us  [the longest x3 5.6 us: per_device(): parts[a] = lax.ppermute(parts[a], 'sec', steps)]
    all_to_all x1, waiting for transfers between devices: 2.56 us -> 6.24 us  [per_device(): view = lax.all_to_all(owned, 'sec', split_axis=0, concat_axis=0, tiled=True)]
    all_to_all x1, starting transfers between devices: 6.66 us -> 3.78 us  [per_device(): view = lax.all_to_all(owned, 'sec', split_axis=0, concat_axis=0, tiled=True)]
    pallas_call x1, Pallas kernels: 1.57 us -> 2.77 us  [arrange(): pl.pallas_call(functools.partial(arrange_kernel, plans, sectors), out_sha...]
    pallas_call x0 -> x2, Pallas kernels: none -> 0.75 us  [the longest x1 0.71 us: blocks(): pl.pallas_call(blocks_kernel, out_shape=(block,) * far, in_specs=[pl.Bloc...]
    pallas_call x2 -> x1, Pallas kernels: 1.5 us -> 1.18 us  [combine(): pl.pallas_call(functools.partial(combine_kernel, len(pairs), len(behind))...]
  transfers between devices with their start and end apart: 5 -> 11, of which waited for: 5 -> 6; matrix products, arithmetic and copies ran while one was open for 0% -> 0% of each run, Pallas kernels for 23% -> 26%
where the time goes in v6:
time: 62.3 us; the launch traced here: 62 us
  waiting for transfers between devices  24.7 us (40%)
  Pallas kernels  18.6 us (30%)
  starting transfers between devices  17.5 us (28%)
  local copies, waits for them, and re-layouts  1.11 us (2%)
    pallas_call x2, Pallas kernels, products(): pl.pallas_call(functools.partial(kernel, early), out_shape=(out, out), in...  13.9 us
    ppermute x3, waiting for transfers between devices, near_steps(): pieces[b] = lax.ppermute(pieces[b], 'sec', steps)  12.3 us
    all_to_all x1, waiting for transfers between devices, per_device(): view = lax.all_to_all(owned, 'sec', split_axis=0, concat_axis=0, tiled=True)  6.24 us
    ppermute x3, waiting for transfers between devices, swap(): return lax.ppermute(value, 'op', [(0, 1), (1, 0)])  6.14 us
    ppermute x3, starting transfers between devices, per_device(): parts[a] = lax.ppermute(parts[a], 'sec', steps)  5.6 us
    ppermute x3, starting transfers between devices, near_steps(): pieces[b] = lax.ppermute(pieces[b], 'sec', steps)  4.89 us
    all_to_all x1, starting transfers between devices, per_device(): view = lax.all_to_all(owned, 'sec', split_axis=0, concat_axis=0, tiled=True)  3.78 us
    ppermute x1, starting transfers between devices, fetch(): return lax.ppermute(part, ('op', 'sec'), ahead + turns + back)  2.99 us
  transfers between devices with their start and end apart: 11, of which 6 were waited for; matrix products, arithmetic and copies ran while one was open for 0% of the time, Pallas kernels for 26%

profile of v6, /device:TPU:0, one launch (start us, length us, event | category | flops | bytes accessed | tf_op | source)
XLA Modules:
  0.0 62.0 jit_solution(7563472956905876229)
XLA Ops:
  0.0 1.0 %constant_dynamic-slice_fusion = bf16[3,1,256,256]{3,2,1,0:T(8,128)(2,1)S(1)} fusion(bf16[3,8,256,256]{3,2,1,0:T(8,128)(2,1)} %param.11, s32[]{:T(128)S(6)} %select_n.16), kind=kLoop, calls=%fused_computation | loop fusion | bytes 786436 | tf_op jit(solution)/shard_map/dynamic_slice | solution.py:29
  1.0 3.0 %collective-permute-start.6 = (bf16[3,1,256,256]{3,2,1,0:T(8,128)(2,1)S(1)}, bf16[3,1,256,256]{3,2,1,0:T(8,128)(2,1)S(1)}, u32[]{:S(2)}, u32[]{:S(2)}) collective-permute-start(bf16[3,1,256,256]{3,2,1,0:T(8,128)(2,1)S(1)} %constant_dynamic-slice_fusion), channel_id=1, source_target_pairs={{0,1},{1,2},{2,3},{3,4},{4,5},{5,6},{6,7},{7,8},{8,9},{9,10},{10,1... | collective-permute-start | bytes 1179656 | tf_op jit(solution)/shard_map/ppermute | solution.py:30
  4.0 0.1 stack.31.place
  4.1 8.6 %conditional.3 = ((bf16[4,9,16,128]{3,2,1,0:T(8,128)(2,1)S(1)}, bf16[4,9,16,128]{3,2,1,0:T(8,128)(2,1)S(1)}, bf16[4,9,16,128]{3,2,1,0:T(8,128)(2,1)S(1)}, bf16[4,9,16,128]{3,2,1,0:T(8,128)(2,1)S(1)})) conditional(s32[]{:T(128)} %convert_element_type.2, () %tuple.27, (s32[5]{0:T(128)S(1)}, s32[4]{0:T(128)}, s32[4,8]{1,0:T(4,128)}, ...), branch_computations={%region_0.1_spmd, %region_1.2_spmd} | conditional | flops 2415919104 | bytes 14942256 | solution.py:348
  4.1 5.8 %first_kernel.1 = (bf16[9,256,128]{2,1,0:T(8,128)(2,1)S(1)}, bf16[9,256,128]{2,1,0:T(8,128)(2,1)S(1)}) custom-call(s32[5]{0:T(128)S(1)} %get-tuple-element.44.me_ref.place, s32[4]{0:T(128)} %get-tuple-element.45.shifts, s32[4,8]{1,0:T(4,128)} %get-tuple-element.46.active, bf16[3,8,256,256]{3,2,1,0:T(8,128)(2,1)} %get-tuple-element.47.psi, ...), custom_call_target="tpu_custom_call" | custom-call | flops 2415919104 | bytes 12582912 | tf_op jit(solution)/shard_map/cond/branch_1_fun/first_kernel/pallas_call | solution.py:144
  9.9 0.1 collective-permute-start
  10.0 2.0 %collective-permute-done.other = bf16[9,256,128]{2,1,0:T(8,128)(2,1)S(1)} collective-permute-done((bf16[9,256,128]{2,1,0:T(8,128)(2,1)S(1)}, bf16[9,256,128]{2,1,0:T(8,128)(2,1)S(1)}, u32[]{:S(2)}, u32[]{:S(2)}) %collective-permute-start) | collective-permute-done | bytes 589856 | tf_op jit(solution)/shard_map/cond/branch_1_fun/ppermute | solution.py:34
  12.0 0.7 %blocks.1 = (bf16[4,9,16,128]{3,2,1,0:T(8,128)(2,1)S(1)}, bf16[4,9,16,128]{3,2,1,0:T(8,128)(2,1)S(1)}, bf16[4,9,16,128]{3,2,1,0:T(8,128)(2,1)S(1)}, bf16[4,9,16,128]{3,2,1,0:T(8,128)(2,1)S(1)}) custom-call(s32[5]{0:T(128)S(1)} %get-tuple-element.44.me_ref.place, bf16[9,256,128]{2,1,0:T(8,128)(2,1)S(1)} %get-tuple-element.50.mine, ...), custom_call_target="tpu_custom_call" | custom-call | tf_op jit(solution)/shard_map/cond/branch_1_fun/blocks/pallas_call | solution.py:229
  12.7 1.7 %collective-permute-start.7 = (bf16[4,9,16,128]{3,2,1,0:T(8,128)(2,1)S(1)}, bf16[4,9,16,128]{3,2,1,0:T(8,128)(2,1)S(1)}, u32[]{:S(2)}, u32[]{:S(2)}) collective-permute-start(bf16[4,9,16,128]{3,2,1,0:T(8,128)(2,1)S(1)} %get-tuple-element.79), channel_id=1, source_target_pairs={{0,4},{1,5},{2,6},{3,7},{4,8},{5,9},{6,10},{7,11},{8,12},{9,13},{1... | collective-permute-start | bytes 442376 | tf_op jit(solution)/shard_map/ppermute | solution.py:371
  14.4 2.6 %collective-permute-start.8 = (bf16[4,9,16,128]{3,2,1,0:T(8,128)(2,1)S(1)}, bf16[4,9,16,128]{3,2,1,0:T(8,128)(2,1)S(1)}, u32[]{:S(2)}, u32[]{:S(2)}) collective-permute-start(bf16[4,9,16,128]{3,2,1,0:T(8,128)(2,1)S(1)} %get-tuple-element.80), channel_id=1, source_target_pairs={{0,8},{1,9},{2,10},{3,11},{4,12},{5,13},{6,14},{7,15},{8,0},{9,1},... | collective-permute-start | bytes 442376 | tf_op jit(solution)/shard_map/ppermute | solution.py:371
  17.0 1.4 %collective-permute-start.9 = (bf16[4,9,16,128]{3,2,1,0:T(8,128)(2,1)S(1)}, bf16[4,9,16,128]{3,2,1,0:T(8,128)(2,1)S(1)}, u32[]{:S(2)}, u32[]{:S(2)}) collective-permute-start(bf16[4,9,16,128]{3,2,1,0:T(8,128)(2,1)S(1)} %get-tuple-element.81), channel_id=1, source_target_pairs={{0,12},{1,13},{2,14},{3,15},{4,0},{5,1},{6,2},{7,3},{8,4},{9,5},{1... | collective-permute-start | bytes 442376 | tf_op jit(solution)/shard_map/ppermute | solution.py:371
  18.3 0.0 collective-permute-done.6
  18.3 13.6 %conditional.4 = (bf16[16,15,16,128]{3,2,1,0:T(8,128)(2,1)}) conditional(s32[]{:T(128)} %convert_element_type.2, () %tuple.26, (bf16[3,1,256,256]{3,2,1,0:T(8,128)(2,1)S(1)}, s32[5]{0:T(128)S(1)}, s32[4]{0:T(128)}, s32[4,8]{1,0:T(4,128)}, bf16[3,8,256,256]{3,2,1,0:T(8,128)(2,1)}, /*index=5*/bf16[4,8,256,256]{3,2,1,0:T(8,128)(2,1)}, ...), branch_computations={%region_2.3_spmd, %region_3.4_spmd} | conditional | flops 4026531840 | bytes 18088024 | solution.py:348
  18.3 0.0 collective-permute-start.1
  18.3 1.7 %collective-permute-done.1.other = bf16[3,1,256,256]{3,2,1,0:T(8,128)(2,1)S(1)} collective-permute-done((bf16[3,1,256,256]{3,2,1,0:T(8,128)(2,1)S(1)}, bf16[3,1,256,256]{3,2,1,0:T(8,128)(2,1)S(1)}, u32[]{:S(2)}, u32[]{:S(2)}) %collective-permute-start.1) | collective-permute-done | bytes 393248 | tf_op jit(solution)/shard_map/cond/branch_1_fun/ppermute | solution.py:34
  20.0 8.1 %second_kernel.1 = (bf16[15,256,128]{2,1,0:T(8,128)(2,1)S(1)}, bf16[15,256,128]{2,1,0:T(8,128)(2,1)S(1)}) custom-call(s32[5]{0:T(128)S(1)} %get-tuple-element.52.me_ref, s32[4]{0:T(128)} %get-tuple-element.53.shifts, s32[4,8]{1,0:T(4,128)} %get-tuple-element.54.active, bf16[3,8,256,256]{3,2,1,0:T(8,128)(2,1)} %get-tuple-element.55.psi, ...), custom_call_target="tpu_custom_call" | custom-call | flops 4026531840 | bytes 12582912 | tf_op jit(solution)/shard_map/cond/branch_1_fun/second_kernel/pallas_call | solution.py:144
  28.1 0.2 collective-permute-start.2
  28.4 2.4 %collective-permute-done.2.refs_1_ = bf16[15,256,128]{2,1,0:T(8,128)(2,1)S(1)} collective-permute-done((bf16[15,256,128]{2,1,0:T(8,128)(2,1)S(1)}, bf16[15,256,128]{2,1,0:T(8,128)(2,1)S(1)}, u32[]{:S(2)}, u32[]{:S(2)}) %collective-permute-start.2) | collective-permute-done | bytes 983072 | tf_op jit(solution)/shard_map/cond/branch_1_fun/ppermute | solution.py:34
  30.8 1.2 %combine.1 = bf16[16,15,16,128]{3,2,1,0:T(8,128)(2,1)} custom-call(bf16[15,256,128]{2,1,0:T(8,128)(2,1)S(1)} %get-tuple-element.60.refs_0_, bf16[15,256,128]{2,1,0:T(8,128)(2,1)S(1)} %collective-permute-done.2.refs_1_), custom_call_target="tpu_custom_call" | custom-call | tf_op jit(solution)/shard_map/cond/branch_1_fun/combine/pallas_call | solution.py:202
  32.0 0.0 collective-permute-done.7.refs_0_
  32.0 0.0 collective-permute-done.8.refs_1_
  32.0 0.0 collective-permute-done.9.refs_2_
  32.0 3.8 %all-to-all-start = ((bf16[16,15,16,128]{3,2,1,0:T(8,128)(2,1)}), bf16[16,15,16,128]{3,2,1,0:T(8,128)(2,1)S(1)}, u32[]{:S(2)}, u32[]{:S(2)}) async-start(bf16[16,15,16,128]{3,2,1,0:T(8,128)(2,1)} %after.1), calls=%async_computation | async-start | bytes 1966080 | tf_op jit(solution)/shard_map/all_to_all | solution.py:374
  35.8 17.2 %conditional.5 = (bf16[4,9,16,128]{3,2,1,0:T(8,128)(2,1)S(1)}, bf16[4,9,16,128]{3,2,1,0:T(8,128)(2,1)}, bf16[4,9,16,128]{3,2,1,0:T(8,128)(2,1)}, bf16[4,9,16,128]{3,2,1,0:T(8,128)(2,1)}) conditional(s32[]{:T(128)} %convert_element_type.2, () %tuple.30, (bf16[4,9,16,128]{3,2,1,0:T(8,128)(2,1)S(1)}, bf16[4,9,16,128]{3,2,1,0:T(8,128)(2,1)S(1)}, ...), branch_computations={%region_4.5_spmd, %region_5.6_spmd} | conditional | flops 16000000000 | bytes 1769624 | solution.py:348
  35.9 2.0 %collective-permute-start.3 = (bf16[4,9,16,128]{3,2,1,0:T(8,128)(2,1)S(1)}, bf16[4,9,16,128]{3,2,1,0:T(8,128)(2,1)}, u32[]{:S(2)}, u32[]{:S(2)}) collective-permute-start(bf16[4,9,16,128]{3,2,1,0:T(8,128)(2,1)S(1)} %get-tuple-element.67), channel_id=1, source_target_pairs={{0,1},{1,2},{2,3},{3,0},{4,5},{5,6},{6,7},{7,4},{8,9},{9,10},{10,1... | collective-permute-start | bytes 442376 | tf_op jit(solution)/shard_map/cond/branch_1_fun/ppermute | solution.py:363
  37.8 1.5 %collective-permute-start.4 = (bf16[4,9,16,128]{3,2,1,0:T(8,128)(2,1)S(1)}, bf16[4,9,16,128]{3,2,1,0:T(8,128)(2,1)}, u32[]{:S(2)}, u32[]{:S(2)}) collective-permute-start(bf16[4,9,16,128]{3,2,1,0:T(8,128)(2,1)S(1)} %get-tuple-element.68), channel_id=1, source_target_pairs={{0,2},{1,3},{2,0},{3,1},{4,6},{5,7},{6,4},{7,5},{8,10},{9,11},{10,... | collective-permute-start | bytes 442376 | tf_op jit(solution)/shard_map/cond/branch_1_fun/ppermute | solution.py:363
  39.3 1.5 %collective-permute-start.5 = (bf16[4,9,16,128]{3,2,1,0:T(8,128)(2,1)S(1)}, bf16[4,9,16,128]{3,2,1,0:T(8,128)(2,1)}, u32[]{:S(2)}, u32[]{:S(2)}) collective-permute-start(bf16[4,9,16,128]{3,2,1,0:T(8,128)(2,1)S(1)} %get-tuple-element.69), channel_id=1, source_target_pairs={{0,3},{1,0},{2,1},{3,2},{4,7},{5,4},{6,5},{7,6},{8,11},{9,8},{10,9... | collective-permute-start | bytes 442376 | tf_op jit(solution)/shard_map/cond/branch_1_fun/ppermute | solution.py:363
  40.7 11.2 %collective-permute-done.3 = bf16[4,9,16,128]{3,2,1,0:T(8,128)(2,1)} collective-permute-done((bf16[4,9,16,128]{3,2,1,0:T(8,128)(2,1)S(1)}, bf16[4,9,16,128]{3,2,1,0:T(8,128)(2,1)}, u32[]{:S(2)}, u32[]{:S(2)}) %collective-permute-start.3) | collective-permute-done | bytes 147488 | tf_op jit(solution)/shard_map/cond/branch_1_fun/ppermute | solution.py:363
  52.0 1.0 %collective-permute-done.4 = bf16[4,9,16,128]{3,2,1,0:T(8,128)(2,1)} collective-permute-done((bf16[4,9,16,128]{3,2,1,0:T(8,128)(2,1)S(1)}, bf16[4,9,16,128]{3,2,1,0:T(8,128)(2,1)}, u32[]{:S(2)}, u32[]{:S(2)}) %collective-permute-start.4) | collective-permute-done | bytes 147488 | tf_op jit(solution)/shard_map/cond/branch_1_fun/ppermute | solution.py:363
  53.0 0.0 collective-permute-done.5
  53.0 6.2 %all-to-all-done.refs_0_ = bf16[16,15,16,128]{3,2,1,0:T(8,128)(2,1)S(1)} async-done(((bf16[16,15,16,128]{3,2,1,0:T(8,128)(2,1)}), bf16[16,15,16,128]{3,2,1,0:T(8,128)(2,1)S(1)}, u32[]{:S(2)}, u32[]{:S(2)}) %all-to-all-start) | async-done | bytes 983072 | tf_op jit(solution)/shard_map/all_to_all | solution.py:374
  59.3 2.8 %arrange.1 = bf16[3,2048,128]{2,1,0:T(8,128)(2,1)} custom-call(s32[5]{0:T(128)S(1)} %stack.31.place, bf16[16,15,16,128]{3,2,1,0:T(8,128)(2,1)S(1)} %all-to-all-done.refs_0_, bf16[4,9,16,128]{3,2,1,0:T(8,128)(2,1)S(1)} %get-tuple-element.82.refs_1_, bf16[4,9,16,128]{3,2,1,0:T(8,128)(2,1)} %get-tuple-element.83.refs_2_, ...), custom_call_target="tpu_custom_call" | custom-call | tf_op jit(solution)/shard_map/arrange/pallas_call | solution.py:296
  (2 shorter events, 0.0 us)
Async XLA Ops:
  1.0 17.3 %collective-permute-start.6 = (bf16[3,1,256,256]{3,2,1,0:T(8,128)(2,1)S(1)}, bf16[3,1,256,256]{3,2,1,0:T(8,128)(2,1)S(1)}, u32[]{:S(2)}, u32[]{:S(2)}) collective-permute-start(bf16[3,1,256,256]{3,2,1,0:T(8,128)(2,1)S(1)} %constant_dynamic-slice_fusion), channel_id=1, source_target_pairs={{0,1},{1,2},{2,3},{3,4},{4,5},{5,6},{6,7},{7,8},{8,9},{9,10},{10,1... | collective-permute-start | bytes 1179656 | tf_op jit(solution)/shard_map/ppermute | solution.py:30
  9.9 2.1 %collective-permute-start = (bf16[9,256,128]{2,1,0:T(8,128)(2,1)S(1)}, bf16[9,256,128]{2,1,0:T(8,128)(2,1)S(1)}, u32[]{:S(2)}, u32[]{:S(2)}) collective-permute-start(bf16[9,256,128]{2,1,0:T(8,128)(2,1)S(1)} %get-tuple-element.51), channel_id=1, source_target_pairs={{0,16},{16,0},{1,17},{17,1},{2,18},{18,2},{3,19},{19,3},{4,20},{20... | collective-permute-start | bytes 1769480 | tf_op jit(solution)/shard_map/cond/branch_1_fun/ppermute | solution.py:34
  12.7 19.3 %collective-permute-start.7 = (bf16[4,9,16,128]{3,2,1,0:T(8,128)(2,1)S(1)}, bf16[4,9,16,128]{3,2,1,0:T(8,128)(2,1)S(1)}, u32[]{:S(2)}, u32[]{:S(2)}) collective-permute-start(bf16[4,9,16,128]{3,2,1,0:T(8,128)(2,1)S(1)} %get-tuple-element.79), channel_id=1, source_target_pairs={{0,4},{1,5},{2,6},{3,7},{4,8},{5,9},{6,10},{7,11},{8,12},{9,13},{1... | collective-permute-start | bytes 442376 | tf_op jit(solution)/shard_map/ppermute | solution.py:371
  14.4 17.6 %collective-permute-start.8 = (bf16[4,9,16,128]{3,2,1,0:T(8,128)(2,1)S(1)}, bf16[4,9,16,128]{3,2,1,0:T(8,128)(2,1)S(1)}, u32[]{:S(2)}, u32[]{:S(2)}) collective-permute-start(bf16[4,9,16,128]{3,2,1,0:T(8,128)(2,1)S(1)} %get-tuple-element.80), channel_id=1, source_target_pairs={{0,8},{1,9},{2,10},{3,11},{4,12},{5,13},{6,14},{7,15},{8,0},{9,1},... | collective-permute-start | bytes 442376 | tf_op jit(solution)/shard_map/ppermute | solution.py:371
  17.0 15.0 %collective-permute-start.9 = (bf16[4,9,16,128]{3,2,1,0:T(8,128)(2,1)S(1)}, bf16[4,9,16,128]{3,2,1,0:T(8,128)(2,1)S(1)}, u32[]{:S(2)}, u32[]{:S(2)}) collective-permute-start(bf16[4,9,16,128]{3,2,1,0:T(8,128)(2,1)S(1)} %get-tuple-element.81), channel_id=1, source_target_pairs={{0,12},{1,13},{2,14},{3,15},{4,0},{5,1},{6,2},{7,3},{8,4},{9,5},{1... | collective-permute-start | bytes 442376 | tf_op jit(solution)/shard_map/ppermute | solution.py:371
  18.3 1.7 %collective-permute-start.1 = (bf16[3,1,256,256]{3,2,1,0:T(8,128)(2,1)S(1)}, bf16[3,1,256,256]{3,2,1,0:T(8,128)(2,1)S(1)}, u32[]{:S(2)}, u32[]{:S(2)}) collective-permute-start(bf16[3,1,256,256]{3,2,1,0:T(8,128)(2,1)S(1)} %get-tuple-element.58.halo), channel_id=1, source_target_pairs={{0,16},{16,0},{1,17},{17,1},{2,18},{18,2},{3,19},{19,3},{4,20},{20... | collective-permute-start | bytes 1179656 | tf_op jit(solution)/shard_map/cond/branch_1_fun/ppermute | solution.py:34
  28.1 2.6 %collective-permute-start.2 = (bf16[15,256,128]{2,1,0:T(8,128)(2,1)S(1)}, bf16[15,256,128]{2,1,0:T(8,128)(2,1)S(1)}, u32[]{:S(2)}, u32[]{:S(2)}) collective-permute-start(bf16[15,256,128]{2,1,0:T(8,128)(2,1)S(1)} %get-tuple-element.61), channel_id=1, source_target_pairs={{0,16},{16,0},{1,17},{17,1},{2,18},{18,2},{3,19},{19,3},{4,20},{20... | collective-permute-start | bytes 2949128 | tf_op jit(solution)/shard_map/cond/branch_1_fun/ppermute | solution.py:34
  32.0 27.3 %all-to-all-start = ((bf16[16,15,16,128]{3,2,1,0:T(8,128)(2,1)}), bf16[16,15,16,128]{3,2,1,0:T(8,128)(2,1)S(1)}, u32[]{:S(2)}, u32[]{:S(2)}) async-start(bf16[16,15,16,128]{3,2,1,0:T(8,128)(2,1)} %after.1), calls=%async_computation | async-start | bytes 1966080 | tf_op jit(solution)/shard_map/all_to_all | solution.py:374
  35.9 16.1 %collective-permute-start.3 = (bf16[4,9,16,128]{3,2,1,0:T(8,128)(2,1)S(1)}, bf16[4,9,16,128]{3,2,1,0:T(8,128)(2,1)}, u32[]{:S(2)}, u32[]{:S(2)}) collective-permute-start(bf16[4,9,16,128]{3,2,1,0:T(8,128)(2,1)S(1)} %get-tuple-element.67), channel_id=1, source_target_pairs={{0,1},{1,2},{2,3},{3,0},{4,5},{5,6},{6,7},{7,4},{8,9},{9,10},{10,1... | collective-permute-start | bytes 442376 | tf_op jit(solution)/shard_map/cond/branch_1_fun/ppermute | solution.py:363
  37.8 15.2 %collective-permute-start.4 = (bf16[4,9,16,128]{3,2,1,0:T(8,128)(2,1)S(1)}, bf16[4,9,16,128]{3,2,1,0:T(8,128)(2,1)}, u32[]{:S(2)}, u32[]{:S(2)}) collective-permute-start(bf16[4,9,16,128]{3,2,1,0:T(8,128)(2,1)S(1)} %get-tuple-element.68), channel_id=1, source_target_pairs={{0,2},{1,3},{2,0},{3,1},{4,6},{5,7},{6,4},{7,5},{8,10},{9,11},{10,... | collective-permute-start | bytes 442376 | tf_op jit(solution)/shard_map/cond/branch_1_fun/ppermute | solution.py:363
  39.3 13.7 %collective-permute-start.5 = (bf16[4,9,16,128]{3,2,1,0:T(8,128)(2,1)S(1)}, bf16[4,9,16,128]{3,2,1,0:T(8,128)(2,1)}, u32[]{:S(2)}, u32[]{:S(2)}) collective-permute-start(bf16[4,9,16,128]{3,2,1,0:T(8,128)(2,1)S(1)} %get-tuple-element.69), channel_id=1, source_target_pairs={{0,3},{1,0},{2,1},{3,2},{4,7},{5,4},{6,5},{7,6},{8,11},{9,8},{10,9... | collective-permute-start | bytes 442376 | tf_op jit(solution)/shard_map/cond/branch_1_fun/ppermute | solution.py:363

commit v7 on v6

--- a/solution.py
+++ b/solution.py
@@ -66,12 +66,18 @@
             middle = jnp.dot(self.lbuf[k, t], sources, preferred_element_type=F32)
             middles.append((middle * self.active[k, t].astype(F32)).astype(B16))
         rights = jnp.concatenate([self.rbuf[k, t] for k in range(count)], axis=1)
+        stacked = jnp.concatenate(
+            [
+                jnp.concatenate([m[:, v * blk : (v + 1) * blk] for m in middles], axis=1)
+                for v in range(self.nvec)
+            ],
+            axis=0,
+        )
+        total = lax.dot_general(stacked, rights, (((1,), (1,)), ((), ())), preferred_element_type=F32).astype(B16)
         for v in range(self.nvec):
-            middle = jnp.concatenate([m[:, v * blk : (v + 1) * blk] for m in middles], axis=1)
-            total = lax.dot_general(rights, middle, (((1,), (1,)), ((), ())), preferred_element_type=F32)
-            low, high = total[:, :half], total[:, half:]
-            mine[base + v] = jnp.where(self.me == 0, low, high).astype(B16)
-            theirs[base + v] = jnp.where(self.me == 0, high, low).astype(B16)
+            low, high = (total[v * blk + h * half : v * blk + (h + 1) * half] for h in range(2))
+            mine[base + v] = jnp.where(self.me == 0, low, high).T
+            theirs[base + v] = jnp.where(self.me == 0, high, low).T
 
     def start(self, first, count):
         for s in range(first - QMAX, first + QMAX):
@@ -122,17 +128,31 @@
     for t in edge:
         for copy in work.operators(t):
             copy.start()
-    work.inner(first, count, mine, theirs)
-    for copy in sides:
-        copy.wait()
-    for side, at in enumerate((0, sectors + QMAX)):
-
-        @pl.when(me_ref[1 + side] == 1)
-        def _(at=at):
-            work.ext[:, at : at + QMAX] = jnp.zeros((nvec, QMAX) + psi.shape[2:], psi.dtype)
-
-    for place, t in enumerate(edge):
-        work.sector(t, (count + place) * nvec, mine, theirs)
+    for s in range(first - QMAX, first + QMAX):
+        work.source(s).wait()
+
+    def body(index, carry):
+        inner = index < count
+
+        @pl.when(inner)
+        def _():
+            work.source(first + index + QMAX).wait()
+
+        @pl.when(index == count)
+        def _():
+            for copy in sides:
+                copy.wait()
+            for side, at in enumerate((0, sectors + QMAX)):
+
+                @pl.when(me_ref[1 + side] == 1)
+                def _(at=at):
+                    work.ext[:, at : at + QMAX] = jnp.zeros((nvec, QMAX) + psi.shape[2:], psi.dtype)
+
+        t = jnp.where(inner, first + index, (index - count) * (sectors - QMAX))
+        work.sector(t, index * nvec, mine, theirs)
+        return carry
+
+    lax.fori_loop(0, count + 2 * QMAX, body, 0)
 
 
 def products(kernel, early, jobs, me, shifts, active, psi, left, right, *more):
@@ -168,9 +188,13 @@
     base = 0
     for part in range(parts):
         abuf, bbuf = pairs[2 * part], pairs[2 * part + 1]
-        for job in range(abuf.shape[0]):
+
+        def body(job, carry, base=base):
             total = (abuf[job].astype(F32) + bbuf[job].astype(F32)).astype(B16)
             obuf[:, base + job] = total.reshape(size, share, half)
+            return carry
+
+        lax.fori_loop(0, abuf.shape[0], body, 0)
         base += abuf.shape[0]
     store = pltpu.make_async_copy(obuf, owned, sem.at[0])
     store.start()
@@ -216,10 +240,14 @@
     share = outs[0].shape[2]
     z, q = place[3], place[4]
     for a, out in enumerate(outs):
-        for b in range(near):
+
+        def body(b, carry, a=a, out=out):
             to = lax.rem(z + a, rows_of) * near + lax.rem(q + b, near)
             rows = pl.ds(pl.multiple_of(to * share, share), share)
             out[b] = (mine[:, rows, :].astype(F32) + other[:, rows, :].astype(F32)).astype(B16)
+            return carry
+
+        lax.fori_loop(0, near, body, 0)
 
 
 def blocks(place, mine, other, far, near):
@@ -258,46 +286,68 @@
     )(*parts)
 
 
-def arrange_kernel(plans, sectors, place, *refs):
-    view, pieces, (out, acc, obuf, sem) = refs[0], refs[1:-4], refs[-4:]
-    stepped, direct = plans
-    size, _, share, _ = view.shape
+def settle_kernel(jobs, sectors, place, *refs):
+    pieces, (out, acc) = refs[:-2], refs[-2:]
+    near, (far, _, share, half) = len(pieces), pieces[0].shape
+    for a in range(far):
+        for b in range(near):
+            source = lax.rem(place[3] + far - a, far) * near + lax.rem(place[4] + near - b, near)
+            for index, (v, t) in enumerate(jobs):
+                rows = pl.ds(source * share * sectors + t, share, stride=sectors)
+                acc[v, rows, :] = pieces[b][a, index].astype(F32)
+    for v in range(out.shape[0]):
+        tiles = acc[v].reshape(far * near, share, sectors, half)
+        out[v] = jnp.swapaxes(tiles, 0, 1).reshape(out.shape[1:]).astype(B16)
+
+
+def settle(jobs, sectors, nvec, place, pieces):
+    far, _, share, half = pieces[0].shape
+    vmem = pl.BlockSpec(memory_space=pltpu.VMEM)
+    return pl.pallas_call(
+        functools.partial(settle_kernel, jobs, sectors),
+        out_shape=jax.ShapeDtypeStruct((nvec, far * len(pieces) * share * sectors, half), B16),
+        in_specs=[pl.BlockSpec(memory_space=pltpu.SMEM)] + [vmem] * len(pieces),
+        out_specs=vmem,
+        scratch_shapes=[pltpu.VMEM((nvec, far * len(pieces) * share * sectors, half), F32)],
+        compiler_params=pltpu.CompilerParams(vmem_limit_bytes=24 * 2**20),
+        cost_estimate=pl.CostEstimate(flops=10**9, bytes_accessed=0, transcendentals=0),
+        name="settle",
+    )(place, *pieces)
+
+
+def arrange_kernel(jobs, sectors, view, settled, out, acc, obuf, sem):
+    size, _, share, half = view.shape
+    here = sorted({t for _, t in jobs})
     stores = []
     for vector in range(obuf.shape[0]):
 
-        def put(source, job, value, vector=vector):
-            v, t = job
-            if v == vector:
-                acc[vector, pl.ds(source * share * sectors + t, share, stride=sectors), :] = value().astype(F32)
-
-        def body(source, carry):
-            for index, job in enumerate(direct):
-                put(source, job, lambda: view[source, index])
+        def body(source, carry, vector=vector):
+            for index, (v, t) in enumerate(jobs):
+                if v == vector:
+                    rows = pl.ds(source * share * sectors + t, share, stride=sectors)
+                    acc[vector, rows, :] = view[source, index].astype(F32)
             return carry
 
         lax.fori_loop(0, size, body, 0, unroll=2)
-        near, far = len(pieces), pieces[0].shape[0]
-        for b, piece in enumerate(pieces):
-            for a in range(far):
-                source = lax.rem(place[3] + far - a, far) * near + lax.rem(place[4] + near - b, near)
-                for index, job in enumerate(stepped):
-                    put(source, job, lambda: piece[a, index])
-        tiles = acc[vector].reshape(size, share, sectors, acc.shape[2])
-        obuf[vector] = jnp.swapaxes(tiles, 0, 1).reshape(obuf.shape[1:]).astype(B16)
+        tiles = jnp.swapaxes(acc[vector].reshape(size, share, sectors, half), 0, 1)
+        before = settled[vector].astype(F32).reshape(tiles.shape)
+        row = lax.broadcasted_iota(jnp.int32, tiles.shape, 2)
+        direct = functools.reduce(jnp.logical_or, [row == t for t in here])
+        obuf[vector] = jnp.where(direct, tiles, before).reshape(obuf.shape[1:]).astype(B16)
         stores.append(pltpu.make_async_copy(obuf.at[vector], out.at[vector], sem.at[vector]))
         stores[-1].start()
     for copy in stores:
         copy.wait()
 
 
-def arrange(plans, sectors, nvec, place, view, pieces):
+def arrange(jobs, sectors, view, settled):
     size, _, share, half = view.shape
-    rows = share * size * sectors
+    nvec, rows, _ = settled.shape
+    vmem = pl.BlockSpec(memory_space=pltpu.VMEM)
     out = pl.pallas_call(
-        functools.partial(arrange_kernel, plans, sectors),
+        functools.partial(arrange_kernel, jobs, sectors),
         out_shape=jax.ShapeDtypeStruct((nvec, rows, half), B16),
-        in_specs=[pl.BlockSpec(memory_space=pltpu.SMEM)]
-        + [pl.BlockSpec(memory_space=pltpu.VMEM)] * (1 + len(pieces)),
+        in_specs=[vmem, vmem],
         out_specs=pl.BlockSpec(memory_space=pl.ANY),
         scratch_shapes=[
             pltpu.VMEM((nvec, rows, half), F32),
@@ -306,7 +356,7 @@
         ],
         compiler_params=pltpu.CompilerParams(vmem_limit_bytes=24 * 2**20),
         name="arrange",
-    )(place, view, *pieces)
+    )(view, settled)
     return out.reshape(nvec, share, size * sectors, half)
 
 
@@ -352,8 +402,7 @@
         return blocks(place, mine, swap(theirs), far, NEAR)
 
     def go_on(*operands):
-        *state, halo, earlier = operands
-        mine, theirs = products(second_kernel, early, len(rest), *state, halo, swap(halo), earlier)
+        mine, theirs = products(second_kernel, early, len(rest), *operands)
         return combine([(mine, swap(theirs))], size)
 
     def near_steps(*parts):
@@ -366,15 +415,17 @@
     halo = fetch(psi, me)
     block = jax.ShapeDtypeStruct((NEAR, len(first), share, half), B16)
     parts = [*fence(begin, (block,) * far, *state)]
+    own = parts[0]
     for a in range(1, far):
         steps = [(i, (i + a * NEAR) % size) for i in range(size)]
         parts[a] = lax.ppermute(parts[a], "sec", steps)
     block = jax.ShapeDtypeStruct((size, len(rest), share, half), B16)
-    owned = after(fence(go_on, block, *state, halo, parts[0]), *parts[1:])
+    halo = after(halo, own)
+    owned = after(fence(go_on, block, *state, halo, swap(halo), own), *parts[1:])
     view = lax.all_to_all(owned, "sec", split_axis=0, concat_axis=0, tiled=True)
     block = jax.ShapeDtypeStruct((far, len(first), share, half), B16)
     pieces = fence(near_steps, (block,) * NEAR, *parts)
-    return arrange([first, rest], sectors, nvec, place, view, pieces)
+    return arrange(rest, sectors, view, settle(first, sectors, nvec, place, pieces))
 
 
 def solution(mesh):

time: 62.3 us -> 60.9 us (0.978)
  waiting for transfers between devices: 24.7 us -> 21.9 us
  starting transfers between devices: 17.5 us -> 18.7 us
    ppermute x3, waiting for transfers between devices: 6.14 us -> 4.55 us  [swap(): return lax.ppermute(value, 'op', [(0, 1), (1, 0)])]
    all_to_all x1, starting transfers between devices: 3.78 us -> 5.2 us  [per_device(): view = lax.all_to_all(owned, 'sec', split_axis=0, concat_axis=0, tiled=True)]
    all_to_all x1, waiting for transfers between devices: 6.24 us -> 4.83 us  [per_device(): view = lax.all_to_all(owned, 'sec', split_axis=0, concat_axis=0, tiled=True)]
    ppermute x1, waiting for transfers between devices: 0.01 us -> 0.79 us  [fetch(): return lax.ppermute(part, ('op', 'sec'), ahead + turns + back)]
    pallas_call x1 -> x2, Pallas kernels: 2.77 us -> 3.01 us  [the longest x1 1.52 us: settle(): pl.pallas_call(functools.partial(settle_kernel, jobs, sectors), out_shape...]
  transfers between devices with their start and end apart: 11 -> 11, of which waited for: 6 -> 6; matrix products, arithmetic and copies ran while one was open for 0% -> 0% of each run, Pallas kernels for 26% -> 28%
where the time goes in v7:
time: 60.9 us; the launch traced here: 60.6 us
  waiting for transfers between devices  21.9 us (36%)
  starting transfers between devices  18.7 us (31%)
  Pallas kernels  18.7 us (31%)
  local copies, waits for them, and re-layouts  1.11 us (2%)
    pallas_call x2, Pallas kernels, products(): pl.pallas_call(functools.partial(kernel, early), out_shape=(out, out), in...  13.6 us
    ppermute x3, waiting for transfers between devices, near_steps(): pieces[b] = lax.ppermute(pieces[b], 'sec', steps)  11.8 us
    ppermute x3, starting transfers between devices, per_device(): parts[a] = lax.ppermute(parts[a], 'sec', steps)  5.51 us
    all_to_all x1, starting transfers between devices, per_device(): view = lax.all_to_all(owned, 'sec', split_axis=0, concat_axis=0, tiled=True)  5.2 us
    ppermute x3, starting transfers between devices, near_steps(): pieces[b] = lax.ppermute(pieces[b], 'sec', steps)  4.89 us
    all_to_all x1, waiting for transfers between devices, per_device(): view = lax.all_to_all(owned, 'sec', split_axis=0, concat_axis=0, tiled=True)  4.83 us
    ppermute x3, waiting for transfers between devices, swap(): return lax.ppermute(value, 'op', [(0, 1), (1, 0)])  4.55 us
    ppermute x1, starting transfers between devices, fetch(): return lax.ppermute(part, ('op', 'sec'), ahead + turns + back)  2.99 us
  transfers between devices with their start and end apart: 11, of which 6 were waited for; matrix products, arithmetic and copies ran while one was open for 0% of the time, Pallas kernels for 28%

profile of v7, /device:TPU:0, one launch (start us, length us, event | category | flops | bytes accessed | tf_op | source)
XLA Modules:
  0.0 60.6 jit_solution(8529452339055823896)
XLA Ops:
  0.0 1.0 %constant_dynamic-slice_fusion = bf16[3,1,256,256]{3,2,1,0:T(8,128)(2,1)S(1)} fusion(bf16[3,8,256,256]{3,2,1,0:T(8,128)(2,1)} %param.11, s32[]{:T(128)S(6)} %select_n.16), kind=kLoop, calls=%fused_computation | loop fusion | bytes 786436 | tf_op jit(solution)/shard_map/dynamic_slice | solution.py:29
  1.0 3.0 %collective-permute-start.5 = (bf16[3,1,256,256]{3,2,1,0:T(8,128)(2,1)S(1)}, bf16[3,1,256,256]{3,2,1,0:T(8,128)(2,1)S(1)}, u32[]{:S(2)}, u32[]{:S(2)}) collective-permute-start(bf16[3,1,256,256]{3,2,1,0:T(8,128)(2,1)S(1)} %constant_dynamic-slice_fusion), channel_id=1, source_target_pairs={{0,1},{1,2},{2,3},{3,4},{4,5},{5,6},{6,7},{7,8},{8,9},{9,10},{10,1... | collective-permute-start | bytes 1179656 | tf_op jit(solution)/shard_map/ppermute | solution.py:30
  4.0 0.1 stack.31.place
  4.1 8.6 %conditional.3 = ((bf16[4,9,16,128]{3,2,1,0:T(8,128)(2,1)S(1)}, bf16[4,9,16,128]{3,2,1,0:T(8,128)(2,1)S(1)}, bf16[4,9,16,128]{3,2,1,0:T(8,128)(2,1)S(1)}, bf16[4,9,16,128]{3,2,1,0:T(8,128)(2,1)S(1)})) conditional(s32[]{:T(128)} %convert_element_type.2, () %tuple.27, (s32[5]{0:T(128)S(1)}, s32[4]{0:T(128)}, s32[4,8]{1,0:T(4,128)}, ...), branch_computations={%region_0.1_spmd, %region_1.2_spmd} | conditional | flops 2415919104 | bytes 14942256 | solution.py:398
  4.1 5.7 %first_kernel.1 = (bf16[9,256,128]{2,1,0:T(8,128)(2,1)S(1)}, bf16[9,256,128]{2,1,0:T(8,128)(2,1)S(1)}) custom-call(s32[5]{0:T(128)S(1)} %get-tuple-element.46.me_ref.place, s32[4]{0:T(128)} %get-tuple-element.47.shifts, s32[4,8]{1,0:T(4,128)} %get-tuple-element.48.active, bf16[3,8,256,256]{3,2,1,0:T(8,128)(2,1)} %get-tuple-element.49.psi, ...), custom_call_target="tpu_custom_call" | custom-call | flops 2415919104 | bytes 12582912 | tf_op jit(solution)/shard_map/cond/branch_1_fun/first_kernel/pallas_call | solution.py:164
  9.8 0.1 collective-permute-start
  9.9 2.0 %collective-permute-done.other = bf16[9,256,128]{2,1,0:T(8,128)(2,1)S(1)} collective-permute-done((bf16[9,256,128]{2,1,0:T(8,128)(2,1)S(1)}, bf16[9,256,128]{2,1,0:T(8,128)(2,1)S(1)}, u32[]{:S(2)}, u32[]{:S(2)}) %collective-permute-start) | collective-permute-done | bytes 589856 | tf_op jit(solution)/shard_map/cond/branch_1_fun/ppermute | solution.py:34
  11.9 0.9 %blocks.1 = (bf16[4,9,16,128]{3,2,1,0:T(8,128)(2,1)S(1)}, bf16[4,9,16,128]{3,2,1,0:T(8,128)(2,1)S(1)}, bf16[4,9,16,128]{3,2,1,0:T(8,128)(2,1)S(1)}, bf16[4,9,16,128]{3,2,1,0:T(8,128)(2,1)S(1)}) custom-call(s32[5]{0:T(128)S(1)} %get-tuple-element.46.me_ref.place, bf16[9,256,128]{2,1,0:T(8,128)(2,1)S(1)} %get-tuple-element.52.mine, ...), custom_call_target="tpu_custom_call" | custom-call | tf_op jit(solution)/shard_map/cond/branch_1_fun/blocks/pallas_call | solution.py:257
  12.7 0.8 %collective-permute-done.5.value = bf16[3,1,256,256]{3,2,1,0:T(8,128)(2,1)S(1)} collective-permute-done((bf16[3,1,256,256]{3,2,1,0:T(8,128)(2,1)S(1)}, bf16[3,1,256,256]{3,2,1,0:T(8,128)(2,1)S(1)}, u32[]{:S(2)}, u32[]{:S(2)}) %collective-permute-start.5) | collective-permute-done | bytes 393248 | tf_op jit(solution)/shard_map/ppermute | solution.py:30
  13.5 0.0 collective-permute-start.6
  13.5 1.6 %collective-permute-start.7 = (bf16[4,9,16,128]{3,2,1,0:T(8,128)(2,1)S(1)}, bf16[4,9,16,128]{3,2,1,0:T(8,128)(2,1)S(1)}, u32[]{:S(2)}, u32[]{:S(2)}) collective-permute-start(bf16[4,9,16,128]{3,2,1,0:T(8,128)(2,1)S(1)} %get-tuple-element.82), channel_id=1, source_target_pairs={{0,4},{1,5},{2,6},{3,7},{4,8},{5,9},{6,10},{7,11},{8,12},{9,13},{1... | collective-permute-start | bytes 442376 | tf_op jit(solution)/shard_map/ppermute | solution.py:421
  15.1 2.3 %collective-permute-start.8 = (bf16[4,9,16,128]{3,2,1,0:T(8,128)(2,1)S(1)}, bf16[4,9,16,128]{3,2,1,0:T(8,128)(2,1)S(1)}, u32[]{:S(2)}, u32[]{:S(2)}) collective-permute-start(bf16[4,9,16,128]{3,2,1,0:T(8,128)(2,1)S(1)} %get-tuple-element.83), channel_id=1, source_target_pairs={{0,8},{1,9},{2,10},{3,11},{4,12},{5,13},{6,14},{7,15},{8,0},{9,1},... | collective-permute-start | bytes 442376 | tf_op jit(solution)/shard_map/ppermute | solution.py:421
  17.4 1.7 %collective-permute-start.9 = (bf16[4,9,16,128]{3,2,1,0:T(8,128)(2,1)S(1)}, bf16[4,9,16,128]{3,2,1,0:T(8,128)(2,1)S(1)}, u32[]{:S(2)}, u32[]{:S(2)}) collective-permute-start(bf16[4,9,16,128]{3,2,1,0:T(8,128)(2,1)S(1)} %get-tuple-element.84), channel_id=1, source_target_pairs={{0,12},{1,13},{2,14},{3,15},{4,0},{5,1},{6,2},{7,3},{8,4},{9,5},{1... | collective-permute-start | bytes 442376 | tf_op jit(solution)/shard_map/ppermute | solution.py:421
  19.0 0.0 collective-permute-done.6
  19.1 11.8 %conditional.4 = (bf16[16,15,16,128]{3,2,1,0:T(8,128)(2,1)}) conditional(s32[]{:T(128)} %convert_element_type.2, () %tuple.26, (s32[5]{0:T(128)S(1)}, s32[4]{0:T(128)}, s32[4,8]{1,0:T(4,128)}, bf16[3,8,256,256]{3,2,1,0:T(8,128)(2,1)}, bf16[4,8,256,256]{3,2,1,0:T(8,128)(2,1)}, /*index=5*/bf16[4,8,256,256]{3,2,1,0:T(8,128)(2,1)}, ...), branch_computations={%region_2.3_spmd, %region_3.4_spmd} | conditional | flops 4026531840 | bytes 16515120 | solution.py:398
  19.1 7.9 %second_kernel.1 = (bf16[15,256,128]{2,1,0:T(8,128)(2,1)S(1)}, bf16[15,256,128]{2,1,0:T(8,128)(2,1)S(1)}) custom-call(s32[5]{0:T(128)S(1)} %get-tuple-element.54.me_ref, s32[4]{0:T(128)} %get-tuple-element.55.shifts, s32[4,8]{1,0:T(4,128)} %get-tuple-element.56.active, bf16[3,8,256,256]{3,2,1,0:T(8,128)(2,1)} %get-tuple-element.57.psi, ...), custom_call_target="tpu_custom_call" | custom-call | flops 4026531840 | bytes 12582912 | tf_op jit(solution)/shard_map/cond/branch_1_fun/second_kernel/pallas_call | solution.py:164
  26.9 0.1 collective-permute-start.1
  27.0 2.6 %collective-permute-done.1.refs_1_ = bf16[15,256,128]{2,1,0:T(8,128)(2,1)S(1)} collective-permute-done((bf16[15,256,128]{2,1,0:T(8,128)(2,1)S(1)}, bf16[15,256,128]{2,1,0:T(8,128)(2,1)S(1)}, u32[]{:S(2)}, u32[]{:S(2)}) %collective-permute-start.1) | collective-permute-done | bytes 983072 | tf_op jit(solution)/shard_map/cond/branch_1_fun/ppermute | solution.py:34
  29.6 1.2 %combine.1 = bf16[16,15,16,128]{3,2,1,0:T(8,128)(2,1)} custom-call(bf16[15,256,128]{2,1,0:T(8,128)(2,1)S(1)} %get-tuple-element.63.refs_0_, bf16[15,256,128]{2,1,0:T(8,128)(2,1)S(1)} %collective-permute-done.1.refs_1_), custom_call_target="tpu_custom_call" | custom-call | tf_op jit(solution)/shard_map/cond/branch_1_fun/combine/pallas_call | solution.py:226
  30.8 0.0 collective-permute-done.7.refs_0_
  30.8 0.0 collective-permute-done.8.refs_1_
  30.9 5.2 %all-to-all-start = ((bf16[16,15,16,128]{3,2,1,0:T(8,128)(2,1)}), bf16[16,15,16,128]{3,2,1,0:T(8,128)(2,1)S(1)}, u32[]{:S(2)}, u32[]{:S(2)}) async-start(bf16[16,15,16,128]{3,2,1,0:T(8,128)(2,1)} %after.3), calls=%async_computation | async-start | bytes 1966080 | tf_op jit(solution)/shard_map/all_to_all | solution.py:425
  36.1 16.7 %conditional.5 = (bf16[4,9,16,128]{3,2,1,0:T(8,128)(2,1)S(1)}, bf16[4,9,16,128]{3,2,1,0:T(8,128)(2,1)}, bf16[4,9,16,128]{3,2,1,0:T(8,128)(2,1)}, bf16[4,9,16,128]{3,2,1,0:T(8,128)(2,1)}) conditional(s32[]{:T(128)} %convert_element_type.2, () %tuple.30, (bf16[4,9,16,128]{3,2,1,0:T(8,128)(2,1)S(1)}, bf16[4,9,16,128]{3,2,1,0:T(8,128)(2,1)S(1)}, ...), branch_computations={%region_4.5_spmd, %region_5.6_spmd} | conditional | flops 16000000000 | bytes 1769624 | solution.py:398
  36.1 2.0 %collective-permute-start.2 = (bf16[4,9,16,128]{3,2,1,0:T(8,128)(2,1)S(1)}, bf16[4,9,16,128]{3,2,1,0:T(8,128)(2,1)}, u32[]{:S(2)}, u32[]{:S(2)}) collective-permute-start(bf16[4,9,16,128]{3,2,1,0:T(8,128)(2,1)S(1)} %get-tuple-element.70), channel_id=1, source_target_pairs={{0,1},{1,2},{2,3},{3,0},{4,5},{5,6},{6,7},{7,4},{8,9},{9,10},{10,1... | collective-permute-start | bytes 442376 | tf_op jit(solution)/shard_map/cond/branch_1_fun/ppermute | solution.py:412
  38.1 1.5 %collective-permute-start.3 = (bf16[4,9,16,128]{3,2,1,0:T(8,128)(2,1)S(1)}, bf16[4,9,16,128]{3,2,1,0:T(8,128)(2,1)}, u32[]{:S(2)}, u32[]{:S(2)}) collective-permute-start(bf16[4,9,16,128]{3,2,1,0:T(8,128)(2,1)S(1)} %get-tuple-element.71), channel_id=1, source_target_pairs={{0,2},{1,3},{2,0},{3,1},{4,6},{5,7},{6,4},{7,5},{8,10},{9,11},{10,... | collective-permute-start | bytes 442376 | tf_op jit(solution)/shard_map/cond/branch_1_fun/ppermute | solution.py:412
  39.6 1.5 %collective-permute-start.4 = (bf16[4,9,16,128]{3,2,1,0:T(8,128)(2,1)S(1)}, bf16[4,9,16,128]{3,2,1,0:T(8,128)(2,1)}, u32[]{:S(2)}, u32[]{:S(2)}) collective-permute-start(bf16[4,9,16,128]{3,2,1,0:T(8,128)(2,1)S(1)} %get-tuple-element.72), channel_id=1, source_target_pairs={{0,3},{1,0},{2,1},{3,2},{4,7},{5,4},{6,5},{7,6},{8,11},{9,8},{10,9... | collective-permute-start | bytes 442376 | tf_op jit(solution)/shard_map/cond/branch_1_fun/ppermute | solution.py:412
  41.0 11.4 %collective-permute-done.2 = bf16[4,9,16,128]{3,2,1,0:T(8,128)(2,1)} collective-permute-done((bf16[4,9,16,128]{3,2,1,0:T(8,128)(2,1)S(1)}, bf16[4,9,16,128]{3,2,1,0:T(8,128)(2,1)}, u32[]{:S(2)}, u32[]{:S(2)}) %collective-permute-start.2) | collective-permute-done | bytes 147488 | tf_op jit(solution)/shard_map/cond/branch_1_fun/ppermute | solution.py:412
  52.4 0.4 collective-permute-done.3
  52.8 0.0 collective-permute-done.4
  52.8 1.5 %settle.1.settled = bf16[3,2048,128]{2,1,0:T(8,128)(2,1)S(1)} custom-call(s32[5]{0:T(128)S(1)} %stack.31.place, bf16[4,9,16,128]{3,2,1,0:T(8,128)(2,1)S(1)} %get-tuple-element.85.refs_0_, bf16[4,9,16,128]{3,2,1,0:T(8,128)(2,1)} %get-tuple-element.86.refs_1_, bf16[4,9,16,128]{3,2,1,0:T(8,128)(2,1)} %get-tuple-element.87.refs_2_, ...), custom_call_target="tpu_custom_call" | custom-call | flops 1000000000 | tf_op jit(solution)/shard_map/settle/pallas_call | solution.py:306
  54.3 4.8 %all-to-all-done.view = bf16[16,15,16,128]{3,2,1,0:T(8,128)(2,1)S(1)} async-done(((bf16[16,15,16,128]{3,2,1,0:T(8,128)(2,1)}), bf16[16,15,16,128]{3,2,1,0:T(8,128)(2,1)S(1)}, u32[]{:S(2)}, u32[]{:S(2)}) %all-to-all-start) | async-done | bytes 983072 | tf_op jit(solution)/shard_map/all_to_all | solution.py:425
  59.1 1.5 %arrange.1 = bf16[3,2048,128]{2,1,0:T(8,128)(2,1)} custom-call(bf16[16,15,16,128]{3,2,1,0:T(8,128)(2,1)S(1)} %all-to-all-done.view, bf16[3,2048,128]{2,1,0:T(8,128)(2,1)S(1)} %settle.1.settled), custom_call_target="tpu_custom_call" | custom-call | tf_op jit(solution)/shard_map/arrange/pallas_call | solution.py:347
  (4 shorter events, 0.0 us)
Async XLA Ops:
  1.0 12.5 %collective-permute-start.5 = (bf16[3,1,256,256]{3,2,1,0:T(8,128)(2,1)S(1)}, bf16[3,1,256,256]{3,2,1,0:T(8,128)(2,1)S(1)}, u32[]{:S(2)}, u32[]{:S(2)}) collective-permute-start(bf16[3,1,256,256]{3,2,1,0:T(8,128)(2,1)S(1)} %constant_dynamic-slice_fusion), channel_id=1, source_target_pairs={{0,1},{1,2},{2,3},{3,4},{4,5},{5,6},{6,7},{7,8},{8,9},{9,10},{10,1... | collective-permute-start | bytes 1179656 | tf_op jit(solution)/shard_map/ppermute | solution.py:30
  9.8 2.1 %collective-permute-start = (bf16[9,256,128]{2,1,0:T(8,128)(2,1)S(1)}, bf16[9,256,128]{2,1,0:T(8,128)(2,1)S(1)}, u32[]{:S(2)}, u32[]{:S(2)}) collective-permute-start(bf16[9,256,128]{2,1,0:T(8,128)(2,1)S(1)} %get-tuple-element.53), channel_id=1, source_target_pairs={{0,16},{16,0},{1,17},{17,1},{2,18},{18,2},{3,19},{19,3},{4,20},{20... | collective-permute-start | bytes 1769480 | tf_op jit(solution)/shard_map/cond/branch_1_fun/ppermute | solution.py:34
  13.5 5.5 %collective-permute-start.6 = (bf16[3,1,256,256]{3,2,1,0:T(8,128)(2,1)S(1)}, bf16[3,1,256,256]{3,2,1,0:T(8,128)(2,1)S(1)}, u32[]{:S(2)}, u32[]{:S(2)}) collective-permute-start(bf16[3,1,256,256]{3,2,1,0:T(8,128)(2,1)S(1)} %after.2), channel_id=1, source_target_pairs={{0,16},{16,0},{1,17},{17,1},{2,18},{18,2},{3,19},{19,3},{4,20},{20... | collective-permute-start | bytes 1179656 | tf_op jit(solution)/shard_map/ppermute | solution.py:34
  13.5 17.3 %collective-permute-start.7 = (bf16[4,9,16,128]{3,2,1,0:T(8,128)(2,1)S(1)}, bf16[4,9,16,128]{3,2,1,0:T(8,128)(2,1)S(1)}, u32[]{:S(2)}, u32[]{:S(2)}) collective-permute-start(bf16[4,9,16,128]{3,2,1,0:T(8,128)(2,1)S(1)} %get-tuple-element.82), channel_id=1, source_target_pairs={{0,4},{1,5},{2,6},{3,7},{4,8},{5,9},{6,10},{7,11},{8,12},{9,13},{1... | collective-permute-start | bytes 442376 | tf_op jit(solution)/shard_map/ppermute | solution.py:421
  15.1 15.7 %collective-permute-start.8 = (bf16[4,9,16,128]{3,2,1,0:T(8,128)(2,1)S(1)}, bf16[4,9,16,128]{3,2,1,0:T(8,128)(2,1)S(1)}, u32[]{:S(2)}, u32[]{:S(2)}) collective-permute-start(bf16[4,9,16,128]{3,2,1,0:T(8,128)(2,1)S(1)} %get-tuple-element.83), channel_id=1, source_target_pairs={{0,8},{1,9},{2,10},{3,11},{4,12},{5,13},{6,14},{7,15},{8,0},{9,1},... | collective-permute-start | bytes 442376 | tf_op jit(solution)/shard_map/ppermute | solution.py:421
  17.4 13.5 %collective-permute-start.9 = (bf16[4,9,16,128]{3,2,1,0:T(8,128)(2,1)S(1)}, bf16[4,9,16,128]{3,2,1,0:T(8,128)(2,1)S(1)}, u32[]{:S(2)}, u32[]{:S(2)}) collective-permute-start(bf16[4,9,16,128]{3,2,1,0:T(8,128)(2,1)S(1)} %get-tuple-element.84), channel_id=1, source_target_pairs={{0,12},{1,13},{2,14},{3,15},{4,0},{5,1},{6,2},{7,3},{8,4},{9,5},{1... | collective-permute-start | bytes 442376 | tf_op jit(solution)/shard_map/ppermute | solution.py:421
  26.9 2.6 %collective-permute-start.1 = (bf16[15,256,128]{2,1,0:T(8,128)(2,1)S(1)}, bf16[15,256,128]{2,1,0:T(8,128)(2,1)S(1)}, u32[]{:S(2)}, u32[]{:S(2)}) collective-permute-start(bf16[15,256,128]{2,1,0:T(8,128)(2,1)S(1)} %get-tuple-element.64), channel_id=1, source_target_pairs={{0,16},{16,0},{1,17},{17,1},{2,18},{18,2},{3,19},{19,3},{4,20},{20... | collective-permute-start | bytes 2949128 | tf_op jit(solution)/shard_map/cond/branch_1_fun/ppermute | solution.py:34
  30.9 28.3 %all-to-all-start = ((bf16[16,15,16,128]{3,2,1,0:T(8,128)(2,1)}), bf16[16,15,16,128]{3,2,1,0:T(8,128)(2,1)S(1)}, u32[]{:S(2)}, u32[]{:S(2)}) async-start(bf16[16,15,16,128]{3,2,1,0:T(8,128)(2,1)} %after.3), calls=%async_computation | async-start | bytes 1966080 | tf_op jit(solution)/shard_map/all_to_all | solution.py:425
  36.1 16.3 %collective-permute-start.2 = (bf16[4,9,16,128]{3,2,1,0:T(8,128)(2,1)S(1)}, bf16[4,9,16,128]{3,2,1,0:T(8,128)(2,1)}, u32[]{:S(2)}, u32[]{:S(2)}) collective-permute-start(bf16[4,9,16,128]{3,2,1,0:T(8,128)(2,1)S(1)} %get-tuple-element.70), channel_id=1, source_target_pairs={{0,1},{1,2},{2,3},{3,0},{4,5},{5,6},{6,7},{7,4},{8,9},{9,10},{10,1... | collective-permute-start | bytes 442376 | tf_op jit(solution)/shard_map/cond/branch_1_fun/ppermute | solution.py:412
  38.1 14.7 %collective-permute-start.3 = (bf16[4,9,16,128]{3,2,1,0:T(8,128)(2,1)S(1)}, bf16[4,9,16,128]{3,2,1,0:T(8,128)(2,1)}, u32[]{:S(2)}, u32[]{:S(2)}) collective-permute-start(bf16[4,9,16,128]{3,2,1,0:T(8,128)(2,1)S(1)} %get-tuple-element.71), channel_id=1, source_target_pairs={{0,2},{1,3},{2,0},{3,1},{4,6},{5,7},{6,4},{7,5},{8,10},{9,11},{10,... | collective-permute-start | bytes 442376 | tf_op jit(solution)/shard_map/cond/branch_1_fun/ppermute | solution.py:412
  39.6 13.2 %collective-permute-start.4 = (bf16[4,9,16,128]{3,2,1,0:T(8,128)(2,1)S(1)}, bf16[4,9,16,128]{3,2,1,0:T(8,128)(2,1)}, u32[]{:S(2)}, u32[]{:S(2)}) collective-permute-start(bf16[4,9,16,128]{3,2,1,0:T(8,128)(2,1)S(1)} %get-tuple-element.72), channel_id=1, source_target_pairs={{0,3},{1,0},{2,1},{3,2},{4,7},{5,4},{6,5},{7,6},{8,11},{9,8},{10,9... | collective-permute-start | bytes 442376 | tf_op jit(solution)/shard_map/cond/branch_1_fun/ppermute | solution.py:412

commit v8 on v7

--- a/solution.py
+++ b/solution.py
@@ -296,7 +296,7 @@
                 rows = pl.ds(source * share * sectors + t, share, stride=sectors)
                 acc[v, rows, :] = pieces[b][a, index].astype(F32)
     for v in range(out.shape[0]):
-        tiles = acc[v].reshape(far * near, share, sectors, half)
+        tiles = acc[v, : out.shape[1]].reshape(far * near, share, sectors, half)
         out[v] = jnp.swapaxes(tiles, 0, 1).reshape(out.shape[1:]).astype(B16)
 
 
@@ -308,7 +308,7 @@
         out_shape=jax.ShapeDtypeStruct((nvec, far * len(pieces) * share * sectors, half), B16),
         in_specs=[pl.BlockSpec(memory_space=pltpu.SMEM)] + [vmem] * len(pieces),
         out_specs=vmem,
-        scratch_shapes=[pltpu.VMEM((nvec, far * len(pieces) * share * sectors, half), F32)],
+        scratch_shapes=[pltpu.VMEM((nvec, (far * len(pieces) * share + 1) * sectors, half), F32)],
         compiler_params=pltpu.CompilerParams(vmem_limit_bytes=24 * 2**20),
         cost_estimate=pl.CostEstimate(flops=10**9, bytes_accessed=0, transcendentals=0),
         name="settle",
@@ -329,7 +329,7 @@
             return carry
 
         lax.fori_loop(0, size, body, 0, unroll=2)
-        tiles = jnp.swapaxes(acc[vector].reshape(size, share, sectors, half), 0, 1)
+        tiles = jnp.swapaxes(acc[vector, : out.shape[1]].reshape(size, share, sectors, half), 0, 1)
         before = settled[vector].astype(F32).reshape(tiles.shape)
         row = lax.broadcasted_iota(jnp.int32, tiles.shape, 2)
         direct = functools.reduce(jnp.logical_or, [row == t for t in here])
@@ -350,7 +350,7 @@
         in_specs=[vmem, vmem],
         out_specs=pl.BlockSpec(memory_space=pl.ANY),
         scratch_shapes=[
-            pltpu.VMEM((nvec, rows, half), F32),
+            pltpu.VMEM((nvec, rows + sectors, half), F32),
             pltpu.VMEM((nvec, rows, half), B16),
             pltpu.SemaphoreType.DMA((nvec,)),
         ],

time: 60.9 us -> 60.9 us (level)
  no operation moved by 1% of the time
where the time goes in v8:
time: 60.9 us; the launch traced here: 60.6 us
  waiting for transfers between devices  21.9 us (36%)
  starting transfers between devices  18.7 us (31%)
  Pallas kernels  18.7 us (31%)
  local copies, waits for them, and re-layouts  1.11 us (2%)
    pallas_call x2, Pallas kernels, products(): pl.pallas_call(functools.partial(kernel, early), out_shape=(out, out), in...  13.6 us
    ppermute x3, waiting for transfers between devices, near_steps(): pieces[b] = lax.ppermute(pieces[b], 'sec', steps)  11.8 us
    ppermute x3, starting transfers between devices, per_device(): parts[a] = lax.ppermute(parts[a], 'sec', steps)  5.51 us
    all_to_all x1, starting transfers between devices, per_device(): view = lax.all_to_all(owned, 'sec', split_axis=0, concat_axis=0, tiled=True)  5.2 us
    ppermute x3, starting transfers between devices, near_steps(): pieces[b] = lax.ppermute(pieces[b], 'sec', steps)  4.89 us
    all_to_all x1, waiting for transfers between devices, per_device(): view = lax.all_to_all(owned, 'sec', split_axis=0, concat_axis=0, tiled=True)  4.83 us
    ppermute x3, waiting for transfers between devices, swap(): return lax.ppermute(value, 'op', [(0, 1), (1, 0)])  4.55 us
    ppermute x1, starting transfers between devices, fetch(): return lax.ppermute(part, ('op', 'sec'), ahead + turns + back)  2.99 us
  transfers between devices with their start and end apart: 11, of which 6 were waited for; matrix products, arithmetic and copies ran while one was open for 0% of the time, Pallas kernels for 28%

profile of v8, /device:TPU:0, one launch (start us, length us, event | category | flops | bytes accessed | tf_op | source)
XLA Modules:
  0.0 60.6 jit_solution(2865726837763880417)
XLA Ops:
  0.0 1.0 %constant_dynamic-slice_fusion = bf16[3,1,256,256]{3,2,1,0:T(8,128)(2,1)S(1)} fusion(bf16[3,8,256,256]{3,2,1,0:T(8,128)(2,1)} %param.11, s32[]{:T(128)S(6)} %select_n.16), kind=kLoop, calls=%fused_computation | loop fusion | bytes 786436 | tf_op jit(solution)/shard_map/dynamic_slice | solution.py:29
  1.0 3.0 %collective-permute-start.5 = (bf16[3,1,256,256]{3,2,1,0:T(8,128)(2,1)S(1)}, bf16[3,1,256,256]{3,2,1,0:T(8,128)(2,1)S(1)}, u32[]{:S(2)}, u32[]{:S(2)}) collective-permute-start(bf16[3,1,256,256]{3,2,1,0:T(8,128)(2,1)S(1)} %constant_dynamic-slice_fusion), channel_id=1, source_target_pairs={{0,1},{1,2},{2,3},{3,4},{4,5},{5,6},{6,7},{7,8},{8,9},{9,10},{10,1... | collective-permute-start | bytes 1179656 | tf_op jit(solution)/shard_map/ppermute | solution.py:30
  4.0 0.1 stack.31.place
  4.1 8.6 %conditional.3 = ((bf16[4,9,16,128]{3,2,1,0:T(8,128)(2,1)S(1)}, bf16[4,9,16,128]{3,2,1,0:T(8,128)(2,1)S(1)}, bf16[4,9,16,128]{3,2,1,0:T(8,128)(2,1)S(1)}, bf16[4,9,16,128]{3,2,1,0:T(8,128)(2,1)S(1)})) conditional(s32[]{:T(128)} %convert_element_type.2, () %tuple.27, (s32[5]{0:T(128)S(1)}, s32[4]{0:T(128)}, s32[4,8]{1,0:T(4,128)}, ...), branch_computations={%region_0.1_spmd, %region_1.2_spmd} | conditional | flops 2415919104 | bytes 14942256 | solution.py:398
  4.1 5.7 %first_kernel.1 = (bf16[9,256,128]{2,1,0:T(8,128)(2,1)S(1)}, bf16[9,256,128]{2,1,0:T(8,128)(2,1)S(1)}) custom-call(s32[5]{0:T(128)S(1)} %get-tuple-element.46.me_ref.place, s32[4]{0:T(128)} %get-tuple-element.47.shifts, s32[4,8]{1,0:T(4,128)} %get-tuple-element.48.active, bf16[3,8,256,256]{3,2,1,0:T(8,128)(2,1)} %get-tuple-element.49.psi, ...), custom_call_target="tpu_custom_call" | custom-call | flops 2415919104 | bytes 12582912 | tf_op jit(solution)/shard_map/cond/branch_1_fun/first_kernel/pallas_call | solution.py:164
  9.8 0.1 collective-permute-start
  9.9 2.0 %collective-permute-done.other = bf16[9,256,128]{2,1,0:T(8,128)(2,1)S(1)} collective-permute-done((bf16[9,256,128]{2,1,0:T(8,128)(2,1)S(1)}, bf16[9,256,128]{2,1,0:T(8,128)(2,1)S(1)}, u32[]{:S(2)}, u32[]{:S(2)}) %collective-permute-start) | collective-permute-done | bytes 589856 | tf_op jit(solution)/shard_map/cond/branch_1_fun/ppermute | solution.py:34
  11.9 0.9 %blocks.1 = (bf16[4,9,16,128]{3,2,1,0:T(8,128)(2,1)S(1)}, bf16[4,9,16,128]{3,2,1,0:T(8,128)(2,1)S(1)}, bf16[4,9,16,128]{3,2,1,0:T(8,128)(2,1)S(1)}, bf16[4,9,16,128]{3,2,1,0:T(8,128)(2,1)S(1)}) custom-call(s32[5]{0:T(128)S(1)} %get-tuple-element.46.me_ref.place, bf16[9,256,128]{2,1,0:T(8,128)(2,1)S(1)} %get-tuple-element.52.mine, ...), custom_call_target="tpu_custom_call" | custom-call | tf_op jit(solution)/shard_map/cond/branch_1_fun/blocks/pallas_call | solution.py:257
  12.7 0.8 %collective-permute-done.5.value = bf16[3,1,256,256]{3,2,1,0:T(8,128)(2,1)S(1)} collective-permute-done((bf16[3,1,256,256]{3,2,1,0:T(8,128)(2,1)S(1)}, bf16[3,1,256,256]{3,2,1,0:T(8,128)(2,1)S(1)}, u32[]{:S(2)}, u32[]{:S(2)}) %collective-permute-start.5) | collective-permute-done | bytes 393248 | tf_op jit(solution)/shard_map/ppermute | solution.py:30
  13.5 0.0 collective-permute-start.6
  13.5 1.6 %collective-permute-start.7 = (bf16[4,9,16,128]{3,2,1,0:T(8,128)(2,1)S(1)}, bf16[4,9,16,128]{3,2,1,0:T(8,128)(2,1)S(1)}, u32[]{:S(2)}, u32[]{:S(2)}) collective-permute-start(bf16[4,9,16,128]{3,2,1,0:T(8,128)(2,1)S(1)} %get-tuple-element.82), channel_id=1, source_target_pairs={{0,4},{1,5},{2,6},{3,7},{4,8},{5,9},{6,10},{7,11},{8,12},{9,13},{1... | collective-permute-start | bytes 442376 | tf_op jit(solution)/shard_map/ppermute | solution.py:421
  15.1 2.3 %collective-permute-start.8 = (bf16[4,9,16,128]{3,2,1,0:T(8,128)(2,1)S(1)}, bf16[4,9,16,128]{3,2,1,0:T(8,128)(2,1)S(1)}, u32[]{:S(2)}, u32[]{:S(2)}) collective-permute-start(bf16[4,9,16,128]{3,2,1,0:T(8,128)(2,1)S(1)} %get-tuple-element.83), channel_id=1, source_target_pairs={{0,8},{1,9},{2,10},{3,11},{4,12},{5,13},{6,14},{7,15},{8,0},{9,1},... | collective-permute-start | bytes 442376 | tf_op jit(solution)/shard_map/ppermute | solution.py:421
  17.4 1.7 %collective-permute-start.9 = (bf16[4,9,16,128]{3,2,1,0:T(8,128)(2,1)S(1)}, bf16[4,9,16,128]{3,2,1,0:T(8,128)(2,1)S(1)}, u32[]{:S(2)}, u32[]{:S(2)}) collective-permute-start(bf16[4,9,16,128]{3,2,1,0:T(8,128)(2,1)S(1)} %get-tuple-element.84), channel_id=1, source_target_pairs={{0,12},{1,13},{2,14},{3,15},{4,0},{5,1},{6,2},{7,3},{8,4},{9,5},{1... | collective-permute-start | bytes 442376 | tf_op jit(solution)/shard_map/ppermute | solution.py:421
  19.0 0.0 collective-permute-done.6
  19.1 11.8 %conditional.4 = (bf16[16,15,16,128]{3,2,1,0:T(8,128)(2,1)}) conditional(s32[]{:T(128)} %convert_element_type.2, () %tuple.26, (s32[5]{0:T(128)S(1)}, s32[4]{0:T(128)}, s32[4,8]{1,0:T(4,128)}, bf16[3,8,256,256]{3,2,1,0:T(8,128)(2,1)}, bf16[4,8,256,256]{3,2,1,0:T(8,128)(2,1)}, /*index=5*/bf16[4,8,256,256]{3,2,1,0:T(8,128)(2,1)}, ...), branch_computations={%region_2.3_spmd, %region_3.4_spmd} | conditional | flops 4026531840 | bytes 16515120 | solution.py:398
  19.1 7.9 %second_kernel.1 = (bf16[15,256,128]{2,1,0:T(8,128)(2,1)S(1)}, bf16[15,256,128]{2,1,0:T(8,128)(2,1)S(1)}) custom-call(s32[5]{0:T(128)S(1)} %get-tuple-element.54.me_ref, s32[4]{0:T(128)} %get-tuple-element.55.shifts, s32[4,8]{1,0:T(4,128)} %get-tuple-element.56.active, bf16[3,8,256,256]{3,2,1,0:T(8,128)(2,1)} %get-tuple-element.57.psi, ...), custom_call_target="tpu_custom_call" | custom-call | flops 4026531840 | bytes 12582912 | tf_op jit(solution)/shard_map/cond/branch_1_fun/second_kernel/pallas_call | solution.py:164
  26.9 0.1 collective-permute-start.1
  27.0 2.6 %collective-permute-done.1.refs_1_ = bf16[15,256,128]{2,1,0:T(8,128)(2,1)S(1)} collective-permute-done((bf16[15,256,128]{2,1,0:T(8,128)(2,1)S(1)}, bf16[15,256,128]{2,1,0:T(8,128)(2,1)S(1)}, u32[]{:S(2)}, u32[]{:S(2)}) %collective-permute-start.1) | collective-permute-done | bytes 983072 | tf_op jit(solution)/shard_map/cond/branch_1_fun/ppermute | solution.py:34
  29.6 1.2 %combine.1 = bf16[16,15,16,128]{3,2,1,0:T(8,128)(2,1)} custom-call(bf16[15,256,128]{2,1,0:T(8,128)(2,1)S(1)} %get-tuple-element.63.refs_0_, bf16[15,256,128]{2,1,0:T(8,128)(2,1)S(1)} %collective-permute-done.1.refs_1_), custom_call_target="tpu_custom_call" | custom-call | tf_op jit(solution)/shard_map/cond/branch_1_fun/combine/pallas_call | solution.py:226
  30.8 0.0 collective-permute-done.7.refs_0_
  30.8 0.0 collective-permute-done.8.refs_1_
  30.9 5.2 %all-to-all-start = ((bf16[16,15,16,128]{3,2,1,0:T(8,128)(2,1)}), bf16[16,15,16,128]{3,2,1,0:T(8,128)(2,1)S(1)}, u32[]{:S(2)}, u32[]{:S(2)}) async-start(bf16[16,15,16,128]{3,2,1,0:T(8,128)(2,1)} %after.3), calls=%async_computation | async-start | bytes 1966080 | tf_op jit(solution)/shard_map/all_to_all | solution.py:425
  36.1 16.7 %conditional.5 = (bf16[4,9,16,128]{3,2,1,0:T(8,128)(2,1)S(1)}, bf16[4,9,16,128]{3,2,1,0:T(8,128)(2,1)}, bf16[4,9,16,128]{3,2,1,0:T(8,128)(2,1)}, bf16[4,9,16,128]{3,2,1,0:T(8,128)(2,1)}) conditional(s32[]{:T(128)} %convert_element_type.2, () %tuple.30, (bf16[4,9,16,128]{3,2,1,0:T(8,128)(2,1)S(1)}, bf16[4,9,16,128]{3,2,1,0:T(8,128)(2,1)S(1)}, ...), branch_computations={%region_4.5_spmd, %region_5.6_spmd} | conditional | flops 16000000000 | bytes 1769624 | solution.py:398
  36.1 2.0 %collective-permute-start.2 = (bf16[4,9,16,128]{3,2,1,0:T(8,128)(2,1)S(1)}, bf16[4,9,16,128]{3,2,1,0:T(8,128)(2,1)}, u32[]{:S(2)}, u32[]{:S(2)}) collective-permute-start(bf16[4,9,16,128]{3,2,1,0:T(8,128)(2,1)S(1)} %get-tuple-element.70), channel_id=1, source_target_pairs={{0,1},{1,2},{2,3},{3,0},{4,5},{5,6},{6,7},{7,4},{8,9},{9,10},{10,1... | collective-permute-start | bytes 442376 | tf_op jit(solution)/shard_map/cond/branch_1_fun/ppermute | solution.py:412
  38.1 1.5 %collective-permute-start.3 = (bf16[4,9,16,128]{3,2,1,0:T(8,128)(2,1)S(1)}, bf16[4,9,16,128]{3,2,1,0:T(8,128)(2,1)}, u32[]{:S(2)}, u32[]{:S(2)}) collective-permute-start(bf16[4,9,16,128]{3,2,1,0:T(8,128)(2,1)S(1)} %get-tuple-element.71), channel_id=1, source_target_pairs={{0,2},{1,3},{2,0},{3,1},{4,6},{5,7},{6,4},{7,5},{8,10},{9,11},{10,... | collective-permute-start | bytes 442376 | tf_op jit(solution)/shard_map/cond/branch_1_fun/ppermute | solution.py:412
  39.6 1.5 %collective-permute-start.4 = (bf16[4,9,16,128]{3,2,1,0:T(8,128)(2,1)S(1)}, bf16[4,9,16,128]{3,2,1,0:T(8,128)(2,1)}, u32[]{:S(2)}, u32[]{:S(2)}) collective-permute-start(bf16[4,9,16,128]{3,2,1,0:T(8,128)(2,1)S(1)} %get-tuple-element.72), channel_id=1, source_target_pairs={{0,3},{1,0},{2,1},{3,2},{4,7},{5,4},{6,5},{7,6},{8,11},{9,8},{10,9... | collective-permute-start | bytes 442376 | tf_op jit(solution)/shard_map/cond/branch_1_fun/ppermute | solution.py:412
  41.0 11.4 %collective-permute-done.2 = bf16[4,9,16,128]{3,2,1,0:T(8,128)(2,1)} collective-permute-done((bf16[4,9,16,128]{3,2,1,0:T(8,128)(2,1)S(1)}, bf16[4,9,16,128]{3,2,1,0:T(8,128)(2,1)}, u32[]{:S(2)}, u32[]{:S(2)}) %collective-permute-start.2) | collective-permute-done | bytes 147488 | tf_op jit(solution)/shard_map/cond/branch_1_fun/ppermute | solution.py:412
  52.4 0.4 collective-permute-done.3
  52.8 0.0 collective-permute-done.4
  52.8 1.5 %settle.1.settled = bf16[3,2048,128]{2,1,0:T(8,128)(2,1)S(1)} custom-call(s32[5]{0:T(128)S(1)} %stack.31.place, bf16[4,9,16,128]{3,2,1,0:T(8,128)(2,1)S(1)} %get-tuple-element.85.refs_0_, bf16[4,9,16,128]{3,2,1,0:T(8,128)(2,1)} %get-tuple-element.86.refs_1_, bf16[4,9,16,128]{3,2,1,0:T(8,128)(2,1)} %get-tuple-element.87.refs_2_, ...), custom_call_target="tpu_custom_call" | custom-call | flops 1000000000 | tf_op jit(solution)/shard_map/settle/pallas_call | solution.py:306
  54.3 4.8 %all-to-all-done.view = bf16[16,15,16,128]{3,2,1,0:T(8,128)(2,1)S(1)} async-done(((bf16[16,15,16,128]{3,2,1,0:T(8,128)(2,1)}), bf16[16,15,16,128]{3,2,1,0:T(8,128)(2,1)S(1)}, u32[]{:S(2)}, u32[]{:S(2)}) %all-to-all-start) | async-done | bytes 983072 | tf_op jit(solution)/shard_map/all_to_all | solution.py:425
  59.1 1.5 %arrange.1 = bf16[3,2048,128]{2,1,0:T(8,128)(2,1)} custom-call(bf16[16,15,16,128]{3,2,1,0:T(8,128)(2,1)S(1)} %all-to-all-done.view, bf16[3,2048,128]{2,1,0:T(8,128)(2,1)S(1)} %settle.1.settled), custom_call_target="tpu_custom_call" | custom-call | tf_op jit(solution)/shard_map/arrange/pallas_call | solution.py:347
  (4 shorter events, 0.0 us)
Async XLA Ops:
  1.0 12.5 %collective-permute-start.5 = (bf16[3,1,256,256]{3,2,1,0:T(8,128)(2,1)S(1)}, bf16[3,1,256,256]{3,2,1,0:T(8,128)(2,1)S(1)}, u32[]{:S(2)}, u32[]{:S(2)}) collective-permute-start(bf16[3,1,256,256]{3,2,1,0:T(8,128)(2,1)S(1)} %constant_dynamic-slice_fusion), channel_id=1, source_target_pairs={{0,1},{1,2},{2,3},{3,4},{4,5},{5,6},{6,7},{7,8},{8,9},{9,10},{10,1... | collective-permute-start | bytes 1179656 | tf_op jit(solution)/shard_map/ppermute | solution.py:30
  9.8 2.1 %collective-permute-start = (bf16[9,256,128]{2,1,0:T(8,128)(2,1)S(1)}, bf16[9,256,128]{2,1,0:T(8,128)(2,1)S(1)}, u32[]{:S(2)}, u32[]{:S(2)}) collective-permute-start(bf16[9,256,128]{2,1,0:T(8,128)(2,1)S(1)} %get-tuple-element.53), channel_id=1, source_target_pairs={{0,16},{16,0},{1,17},{17,1},{2,18},{18,2},{3,19},{19,3},{4,20},{20... | collective-permute-start | bytes 1769480 | tf_op jit(solution)/shard_map/cond/branch_1_fun/ppermute | solution.py:34
  13.5 5.5 %collective-permute-start.6 = (bf16[3,1,256,256]{3,2,1,0:T(8,128)(2,1)S(1)}, bf16[3,1,256,256]{3,2,1,0:T(8,128)(2,1)S(1)}, u32[]{:S(2)}, u32[]{:S(2)}) collective-permute-start(bf16[3,1,256,256]{3,2,1,0:T(8,128)(2,1)S(1)} %after.2), channel_id=1, source_target_pairs={{0,16},{16,0},{1,17},{17,1},{2,18},{18,2},{3,19},{19,3},{4,20},{20... | collective-permute-start | bytes 1179656 | tf_op jit(solution)/shard_map/ppermute | solution.py:34
  13.5 17.3 %collective-permute-start.7 = (bf16[4,9,16,128]{3,2,1,0:T(8,128)(2,1)S(1)}, bf16[4,9,16,128]{3,2,1,0:T(8,128)(2,1)S(1)}, u32[]{:S(2)}, u32[]{:S(2)}) collective-permute-start(bf16[4,9,16,128]{3,2,1,0:T(8,128)(2,1)S(1)} %get-tuple-element.82), channel_id=1, source_target_pairs={{0,4},{1,5},{2,6},{3,7},{4,8},{5,9},{6,10},{7,11},{8,12},{9,13},{1... | collective-permute-start | bytes 442376 | tf_op jit(solution)/shard_map/ppermute | solution.py:421
  15.1 15.7 %collective-permute-start.8 = (bf16[4,9,16,128]{3,2,1,0:T(8,128)(2,1)S(1)}, bf16[4,9,16,128]{3,2,1,0:T(8,128)(2,1)S(1)}, u32[]{:S(2)}, u32[]{:S(2)}) collective-permute-start(bf16[4,9,16,128]{3,2,1,0:T(8,128)(2,1)S(1)} %get-tuple-element.83), channel_id=1, source_target_pairs={{0,8},{1,9},{2,10},{3,11},{4,12},{5,13},{6,14},{7,15},{8,0},{9,1},... | collective-permute-start | bytes 442376 | tf_op jit(solution)/shard_map/ppermute | solution.py:421
  17.4 13.5 %collective-permute-start.9 = (bf16[4,9,16,128]{3,2,1,0:T(8,128)(2,1)S(1)}, bf16[4,9,16,128]{3,2,1,0:T(8,128)(2,1)S(1)}, u32[]{:S(2)}, u32[]{:S(2)}) collective-permute-start(bf16[4,9,16,128]{3,2,1,0:T(8,128)(2,1)S(1)} %get-tuple-element.84), channel_id=1, source_target_pairs={{0,12},{1,13},{2,14},{3,15},{4,0},{5,1},{6,2},{7,3},{8,4},{9,5},{1... | collective-permute-start | bytes 442376 | tf_op jit(solution)/shard_map/ppermute | solution.py:421
  26.9 2.6 %collective-permute-start.1 = (bf16[15,256,128]{2,1,0:T(8,128)(2,1)S(1)}, bf16[15,256,128]{2,1,0:T(8,128)(2,1)S(1)}, u32[]{:S(2)}, u32[]{:S(2)}) collective-permute-start(bf16[15,256,128]{2,1,0:T(8,128)(2,1)S(1)} %get-tuple-element.64), channel_id=1, source_target_pairs={{0,16},{16,0},{1,17},{17,1},{2,18},{18,2},{3,19},{19,3},{4,20},{20... | collective-permute-start | bytes 2949128 | tf_op jit(solution)/shard_map/cond/branch_1_fun/ppermute | solution.py:34
  30.9 28.3 %all-to-all-start = ((bf16[16,15,16,128]{3,2,1,0:T(8,128)(2,1)}), bf16[16,15,16,128]{3,2,1,0:T(8,128)(2,1)S(1)}, u32[]{:S(2)}, u32[]{:S(2)}) async-start(bf16[16,15,16,128]{3,2,1,0:T(8,128)(2,1)} %after.3), calls=%async_computation | async-start | bytes 1966080 | tf_op jit(solution)/shard_map/all_to_all | solution.py:425
  36.1 16.3 %collective-permute-start.2 = (bf16[4,9,16,128]{3,2,1,0:T(8,128)(2,1)S(1)}, bf16[4,9,16,128]{3,2,1,0:T(8,128)(2,1)}, u32[]{:S(2)}, u32[]{:S(2)}) collective-permute-start(bf16[4,9,16,128]{3,2,1,0:T(8,128)(2,1)S(1)} %get-tuple-element.70), channel_id=1, source_target_pairs={{0,1},{1,2},{2,3},{3,0},{4,5},{5,6},{6,7},{7,4},{8,9},{9,10},{10,1... | collective-permute-start | bytes 442376 | tf_op jit(solution)/shard_map/cond/branch_1_fun/ppermute | solution.py:412
  38.1 14.7 %collective-permute-start.3 = (bf16[4,9,16,128]{3,2,1,0:T(8,128)(2,1)S(1)}, bf16[4,9,16,128]{3,2,1,0:T(8,128)(2,1)}, u32[]{:S(2)}, u32[]{:S(2)}) collective-permute-start(bf16[4,9,16,128]{3,2,1,0:T(8,128)(2,1)S(1)} %get-tuple-element.71), channel_id=1, source_target_pairs={{0,2},{1,3},{2,0},{3,1},{4,6},{5,7},{6,4},{7,5},{8,10},{9,11},{10,... | collective-permute-start | bytes 442376 | tf_op jit(solution)/shard_map/cond/branch_1_fun/ppermute | solution.py:412
  39.6 13.2 %collective-permute-start.4 = (bf16[4,9,16,128]{3,2,1,0:T(8,128)(2,1)S(1)}, bf16[4,9,16,128]{3,2,1,0:T(8,128)(2,1)}, u32[]{:S(2)}, u32[]{:S(2)}) collective-permute-start(bf16[4,9,16,128]{3,2,1,0:T(8,128)(2,1)S(1)} %get-tuple-element.72), channel_id=1, source_target_pairs={{0,3},{1,0},{2,1},{3,2},{4,7},{5,4},{6,5},{7,6},{8,11},{9,8},{10,9... | collective-permute-start | bytes 442376 | tf_op jit(solution)/shard_map/cond/branch_1_fun/ppermute | solution.py:412

commit v9 on v8

--- a/solution.py
+++ b/solution.py
@@ -8,6 +8,7 @@
 from jax.sharding import PartitionSpec as P
 
 QMAX = 1
+SHARE = 1
 NEAR = 4
 F32, B16 = jnp.float32, jnp.bfloat16
 
@@ -37,8 +38,10 @@
 def plan(nvec, sectors, early):
     inner = [*range(QMAX, sectors - QMAX)]
     edge = [*range(QMAX), *range(sectors - QMAX, sectors)]
-    first, rest = inner[:early], inner[early:] + edge
-    return [[(v, t) for t in ts for v in range(nvec)] for ts in (first, rest)]
+    shared, *later = inner[early:] + edge
+    first = [(v, t) for t in inner[:early] for v in range(nvec)] + [(v, shared) for v in range(SHARE)]
+    rest = [(v, shared) for v in range(SHARE, nvec)] + [(v, t) for t in later for v in range(nvec)]
+    return first, rest
 
 
 class Work:
@@ -57,24 +60,24 @@
     def source(self, s):
         return pltpu.make_async_copy(self.psi.at[:, pl.ds(s, 1)], self.ext.at[:, pl.ds(s + QMAX, 1)], self.sem_p.at[s])
 
-    def products(self, t, base, mine, theirs):
+    def products(self, t, base, mine, theirs, vectors):
         count, _, _, blk = self.left.shape
         half = blk // 2
         middles = []
         for k in range(count):
-            sources = jnp.concatenate([self.ext[v, t + QMAX - self.shifts[k]] for v in range(self.nvec)], axis=1)
+            sources = jnp.concatenate([self.ext[v, t + QMAX - self.shifts[k]] for v in vectors], axis=1)
             middle = jnp.dot(self.lbuf[k, t], sources, preferred_element_type=F32)
             middles.append((middle * self.active[k, t].astype(F32)).astype(B16))
         rights = jnp.concatenate([self.rbuf[k, t] for k in range(count)], axis=1)
         stacked = jnp.concatenate(
             [
                 jnp.concatenate([m[:, v * blk : (v + 1) * blk] for m in middles], axis=1)
-                for v in range(self.nvec)
+                for v in range(len(vectors))
             ],
             axis=0,
         )
         total = lax.dot_general(stacked, rights, (((1,), (1,)), ((), ())), preferred_element_type=F32).astype(B16)
-        for v in range(self.nvec):
+        for v in range(len(vectors)):
             low, high = (total[v * blk + h * half : v * blk + (h + 1) * half] for h in range(2))
             mine[base + v] = jnp.where(self.me == 0, low, high).T
             theirs[base + v] = jnp.where(self.me == 0, high, low).T
@@ -87,10 +90,10 @@
             for copy in self.operators(t):
                 copy.start()
 
-    def sector(self, t, base, mine, theirs):
+    def sector(self, t, base, mine, theirs, vectors):
         for copy in self.operators(t):
             copy.wait()
-        self.products(t, base, mine, theirs)
+        self.products(t, base, mine, theirs, vectors)
 
     def inner(self, first, count, mine, theirs):
         for s in range(first - QMAX, first + QMAX):
@@ -98,7 +101,7 @@
 
         def body(index, carry):
             self.source(first + index + QMAX).wait()
-            self.sector(first + index, index * self.nvec, mine, theirs)
+            self.sector(first + index, index * self.nvec, mine, theirs, range(self.nvec))
             return carry
 
         lax.fori_loop(0, count, body, 0)
@@ -106,8 +109,11 @@
 
 def first_kernel(early, me_ref, shifts, active, psi, left, right, mine, theirs, *refs):
     work = Work(refs, psi, left, right, shifts, active, me_ref[0])
-    work.start(QMAX, early)
+    work.start(QMAX, early + 1)
     work.inner(QMAX, early, mine, theirs)
+    shared = QMAX + early
+    work.source(shared + QMAX).wait()
+    work.sector(shared, early * work.nvec, mine, theirs, range(SHARE))
 
 
 def second_kernel(early, me_ref, shifts, active, psi, left, right, halo, other, earlier, mine, theirs, *refs):
@@ -130,6 +136,9 @@
             copy.start()
     for s in range(first - QMAX, first + QMAX):
         work.source(s).wait()
+    work.source(first + QMAX).wait()
+    work.sector(first, 0, mine, theirs, range(SHARE, nvec))
+    first, count = first + 1, count - 1
 
     def body(index, carry):
         inner = index < count
@@ -149,7 +158,7 @@
                     work.ext[:, at : at + QMAX] = jnp.zeros((nvec, QMAX) + psi.shape[2:], psi.dtype)
 
         t = jnp.where(inner, first + index, (index - count) * (sectors - QMAX))
-        work.sector(t, index * nvec, mine, theirs)
+        work.sector(t, index * nvec + nvec - SHARE, mine, theirs, range(nvec))
         return carry
 
     lax.fori_loop(0, count + 2 * QMAX, body, 0)
@@ -317,7 +326,6 @@
 
 def arrange_kernel(jobs, sectors, view, settled, out, acc, obuf, sem):
     size, _, share, half = view.shape
-    here = sorted({t for _, t in jobs})
     stores = []
     for vector in range(obuf.shape[0]):
 
@@ -331,6 +339,7 @@
         lax.fori_loop(0, size, body, 0, unroll=2)
         tiles = jnp.swapaxes(acc[vector, : out.shape[1]].reshape(size, share, sectors, half), 0, 1)
         before = settled[vector].astype(F32).reshape(tiles.shape)
+        here = sorted({t for v, t in jobs if v == vector})
         row = lax.broadcasted_iota(jnp.int32, tiles.shape, 2)
         direct = functools.reduce(jnp.logical_or, [row == t for t in here])
         obuf[vector] = jnp.where(direct, tiles, before).reshape(obuf.shape[1:]).astype(B16)
@@ -402,7 +411,8 @@
         return blocks(place, mine, swap(theirs), far, NEAR)
 
     def go_on(*operands):
-        mine, theirs = products(second_kernel, early, len(rest), *operands)
+        *state, halo, earlier = operands
+        mine, theirs = products(second_kernel, early, len(rest), *state, halo, swap(halo), earlier)
         return combine([(mine, swap(theirs))], size)
 
     def near_steps(*parts):
@@ -420,8 +430,7 @@
         steps = [(i, (i + a * NEAR) % size) for i in range(size)]
         parts[a] = lax.ppermute(parts[a], "sec", steps)
     block = jax.ShapeDtypeStruct((size, len(rest), share, half), B16)
-    halo = after(halo, own)
-    owned = after(fence(go_on, block, *state, halo, swap(halo), own), *parts[1:])
+    owned = after(fence(go_on, block, *state, halo, own), *parts[1:])
     view = lax.all_to_all(owned, "sec", split_axis=0, concat_axis=0, tiled=True)
     block = jax.ShapeDtypeStruct((far, len(first), share, half), B16)
     pieces = fence(near_steps, (block,) * NEAR, *parts)

time: 60.9 us -> 60.4 us (level)
  waiting for transfers between devices: 21.9 us -> 21.1 us
    all_to_all x1, waiting for transfers between devices: 4.83 us -> 2.42 us  [per_device(): view = lax.all_to_all(owned, 'sec', split_axis=0, concat_axis=0, tiled=True)]
    ppermute x3, waiting for transfers between devices: 4.55 us -> 6.14 us  [swap(): return lax.ppermute(value, 'op', [(0, 1), (1, 0)])]
    ppermute x3, waiting for transfers between devices: 11.8 us -> 12.6 us  [near_steps(): pieces[b] = lax.ppermute(pieces[b], 'sec', steps)]
    ppermute x1, waiting for transfers between devices: 0.79 us -> 0.01 us  [fetch(): return lax.ppermute(part, ('op', 'sec'), ahead + turns + back)]
  transfers between devices with their start and end apart: 11 -> 11, of which waited for: 6 -> 6; matrix products, arithmetic and copies ran while one was open for 0% -> 0% of each run, Pallas kernels for 28% -> 29%
where the time goes in v9:
time: 60.4 us; the launch traced here: 60.1 us
  waiting for transfers between devices  21.1 us (35%)
  Pallas kernels  19.1 us (32%)
  starting transfers between devices  18.6 us (31%)
  local copies, waits for them, and re-layouts  1.11 us (2%)
    pallas_call x2, Pallas kernels, products(): pl.pallas_call(functools.partial(kernel, early), out_shape=(out, out), in...  13.9 us
    ppermute x3, waiting for transfers between devices, near_steps(): pieces[b] = lax.ppermute(pieces[b], 'sec', steps)  12.6 us
    ppermute x3, waiting for transfers between devices, swap(): return lax.ppermute(value, 'op', [(0, 1), (1, 0)])  6.14 us
    ppermute x3, starting transfers between devices, per_device(): parts[a] = lax.ppermute(parts[a], 'sec', steps)  5.61 us
    ppermute x3, starting transfers between devices, near_steps(): pieces[b] = lax.ppermute(pieces[b], 'sec', steps)  4.89 us
    all_to_all x1, starting transfers between devices, per_device(): view = lax.all_to_all(owned, 'sec', split_axis=0, concat_axis=0, tiled=True)  4.84 us
    ppermute x1, starting transfers between devices, fetch(): return lax.ppermute(part, ('op', 'sec'), ahead + turns + back)  2.99 us
    all_to_all x1, waiting for transfers between devices, per_device(): view = lax.all_to_all(owned, 'sec', split_axis=0, concat_axis=0, tiled=True)  2.42 us
  transfers between devices with their start and end apart: 11, of which 6 were waited for; matrix products, arithmetic and copies ran while one was open for 0% of the time, Pallas kernels for 29%

profile of v9, /device:TPU:0, one launch (start us, length us, event | category | flops | bytes accessed | tf_op | source)
XLA Modules:
  0.0 60.1 jit_solution(17309847804892913837)
XLA Ops:
  0.0 1.0 %constant_dynamic-slice_fusion = bf16[3,1,256,256]{3,2,1,0:T(8,128)(2,1)S(1)} fusion(bf16[3,8,256,256]{3,2,1,0:T(8,128)(2,1)} %param.11, s32[]{:T(128)S(6)} %select_n.14), kind=kLoop, calls=%fused_computation | loop fusion | bytes 786436 | tf_op jit(solution)/shard_map/dynamic_slice | solution.py:30
  1.0 3.0 %collective-permute-start.6 = (bf16[3,1,256,256]{3,2,1,0:T(8,128)(2,1)S(1)}, bf16[3,1,256,256]{3,2,1,0:T(8,128)(2,1)S(1)}, u32[]{:S(2)}, u32[]{:S(2)}) collective-permute-start(bf16[3,1,256,256]{3,2,1,0:T(8,128)(2,1)S(1)} %constant_dynamic-slice_fusion), channel_id=1, source_target_pairs={{0,1},{1,2},{2,3},{3,4},{4,5},{5,6},{6,7},{7,8},{8,9},{9,10},{10,1... | collective-permute-start | bytes 1179656 | tf_op jit(solution)/shard_map/ppermute | solution.py:31
  4.0 0.1 stack.31.place
  4.1 9.4 %conditional.3 = ((bf16[4,10,16,128]{3,2,1,0:T(8,128)(2,1)S(1)}, bf16[4,10,16,128]{3,2,1,0:T(8,128)(2,1)S(1)}, bf16[4,10,16,128]{3,2,1,0:T(8,128)(2,1)S(1)}, bf16[4,10,16,128]{3,2,1,0:T(8,128)(2,1)S(1)})) conditional(s32[]{:T(128)} %convert_element_type.2, () %tuple.27, (s32[5]{0:T(128)S(1)}, s32[4]{0:T(128)}, s32[4,8]{1,0:T(4,128)}, ...), branch_computations={%region_0.1_spmd, %region_1.2_spmd} | conditional | flops 2684354560 | bytes 15204400 | solution.py:407
  4.1 6.3 %first_kernel.1 = (bf16[10,256,128]{2,1,0:T(8,128)(2,1)S(1)}, bf16[10,256,128]{2,1,0:T(8,128)(2,1)S(1)}) custom-call(s32[5]{0:T(128)S(1)} %get-tuple-element.44.me_ref.place, s32[4]{0:T(128)} %get-tuple-element.45.shifts, s32[4,8]{1,0:T(4,128)} %get-tuple-element.46.active, bf16[3,8,256,256]{3,2,1,0:T(8,128)(2,1)} %get-tuple-element.47.psi, ...), custom_call_target="tpu_custom_call" | custom-call | flops 2684354560 | bytes 12582912 | tf_op jit(solution)/shard_map/cond/branch_1_fun/first_kernel/pallas_call | solution.py:173
  10.4 0.1 collective-permute-start
  10.5 2.1 %collective-permute-done.other = bf16[10,256,128]{2,1,0:T(8,128)(2,1)S(1)} collective-permute-done((bf16[10,256,128]{2,1,0:T(8,128)(2,1)S(1)}, bf16[10,256,128]{2,1,0:T(8,128)(2,1)S(1)}, u32[]{:S(2)}, u32[]{:S(2)}) %collective-permute-start) | collective-permute-done | bytes 655392 | tf_op jit(solution)/shard_map/cond/branch_1_fun/ppermute | solution.py:35
  12.6 0.9 %blocks.1 = (bf16[4,10,16,128]{3,2,1,0:T(8,128)(2,1)S(1)}, bf16[4,10,16,128]{3,2,1,0:T(8,128)(2,1)S(1)}, bf16[4,10,16,128]{3,2,1,0:T(8,128)(2,1)S(1)}, bf16[4,10,16,128]{3,2,1,0:T(8,128)(2,1)S(1)}) custom-call(s32[5]{0:T(128)S(1)} %get-tuple-element.44.me_ref.place, bf16[10,256,128]{2,1,0:T(8,128)(2,1)S(1)} %get-tuple-element.50.mine, ...), custom_call_target="tpu_custom_call" | custom-call | tf_op jit(solution)/shard_map/cond/branch_1_fun/blocks/pallas_call | solution.py:266
  13.5 1.7 %collective-permute-start.7 = (bf16[4,10,16,128]{3,2,1,0:T(8,128)(2,1)S(1)}, bf16[4,10,16,128]{3,2,1,0:T(8,128)(2,1)S(1)}, u32[]{:S(2)}, u32[]{:S(2)}) collective-permute-start(bf16[4,10,16,128]{3,2,1,0:T(8,128)(2,1)S(1)} %get-tuple-element.79), channel_id=1, source_target_pairs={{0,4},{1,5},{2,6},{3,7},{4,8},{5,9},{6,10},{7,11},{8,12},{9,13},{1... | collective-permute-start | bytes 491528 | tf_op jit(solution)/shard_map/ppermute | solution.py:431
  15.1 2.6 %collective-permute-start.8 = (bf16[4,10,16,128]{3,2,1,0:T(8,128)(2,1)S(1)}, bf16[4,10,16,128]{3,2,1,0:T(8,128)(2,1)S(1)}, u32[]{:S(2)}, u32[]{:S(2)}) collective-permute-start(bf16[4,10,16,128]{3,2,1,0:T(8,128)(2,1)S(1)} %get-tuple-element.80), channel_id=1, source_target_pairs={{0,8},{1,9},{2,10},{3,11},{4,12},{5,13},{6,14},{7,15},{8,0},{9,1},... | collective-permute-start | bytes 491528 | tf_op jit(solution)/shard_map/ppermute | solution.py:431
  17.7 1.4 %collective-permute-start.9 = (bf16[4,10,16,128]{3,2,1,0:T(8,128)(2,1)S(1)}, bf16[4,10,16,128]{3,2,1,0:T(8,128)(2,1)S(1)}, u32[]{:S(2)}, u32[]{:S(2)}) collective-permute-start(bf16[4,10,16,128]{3,2,1,0:T(8,128)(2,1)S(1)} %get-tuple-element.81), channel_id=1, source_target_pairs={{0,12},{1,13},{2,14},{3,15},{4,0},{5,1},{6,2},{7,3},{8,4},{9,5},{1... | collective-permute-start | bytes 491528 | tf_op jit(solution)/shard_map/ppermute | solution.py:431
  19.1 0.0 collective-permute-done.6
  19.1 13.1 %conditional.4 = (bf16[16,14,16,128]{3,2,1,0:T(8,128)(2,1)}) conditional(s32[]{:T(128)} %convert_element_type.2, () %tuple.26, (bf16[3,1,256,256]{3,2,1,0:T(8,128)(2,1)S(1)}, s32[5]{0:T(128)S(1)}, s32[4]{0:T(128)}, s32[4,8]{1,0:T(4,128)}, bf16[3,8,256,256]{3,2,1,0:T(8,128)(2,1)}, /*index=5*/bf16[4,8,256,256]{3,2,1,0:T(8,128)(2,1)}, ...), branch_computations={%region_2.3_spmd, %region_3.4_spmd} | conditional | flops 3758096384 | bytes 17825880 | solution.py:407
  19.1 0.0 collective-permute-start.1
  19.1 1.7 %collective-permute-done.1.other = bf16[3,1,256,256]{3,2,1,0:T(8,128)(2,1)S(1)} collective-permute-done((bf16[3,1,256,256]{3,2,1,0:T(8,128)(2,1)S(1)}, bf16[3,1,256,256]{3,2,1,0:T(8,128)(2,1)S(1)}, u32[]{:S(2)}, u32[]{:S(2)}) %collective-permute-start.1) | collective-permute-done | bytes 393248 | tf_op jit(solution)/shard_map/cond/branch_1_fun/ppermute | solution.py:35
  20.8 7.6 %second_kernel.1 = (bf16[14,256,128]{2,1,0:T(8,128)(2,1)S(1)}, bf16[14,256,128]{2,1,0:T(8,128)(2,1)S(1)}) custom-call(s32[5]{0:T(128)S(1)} %get-tuple-element.52.me_ref, s32[4]{0:T(128)} %get-tuple-element.53.shifts, s32[4,8]{1,0:T(4,128)} %get-tuple-element.54.active, bf16[3,8,256,256]{3,2,1,0:T(8,128)(2,1)} %get-tuple-element.55.psi, ...), custom_call_target="tpu_custom_call" | custom-call | flops 3758096384 | bytes 12582912 | tf_op jit(solution)/shard_map/cond/branch_1_fun/second_kernel/pallas_call | solution.py:173
  28.4 0.2 collective-permute-start.2
  28.6 2.3 %collective-permute-done.2.refs_1_ = bf16[14,256,128]{2,1,0:T(8,128)(2,1)S(1)} collective-permute-done((bf16[14,256,128]{2,1,0:T(8,128)(2,1)S(1)}, bf16[14,256,128]{2,1,0:T(8,128)(2,1)S(1)}, u32[]{:S(2)}, u32[]{:S(2)}) %collective-permute-start.2) | collective-permute-done | bytes 917536 | tf_op jit(solution)/shard_map/cond/branch_1_fun/ppermute | solution.py:35
  31.0 1.2 %combine.1 = bf16[16,14,16,128]{3,2,1,0:T(8,128)(2,1)} custom-call(bf16[14,256,128]{2,1,0:T(8,128)(2,1)S(1)} %get-tuple-element.60.refs_0_, bf16[14,256,128]{2,1,0:T(8,128)(2,1)S(1)} %collective-permute-done.2.refs_1_), custom_call_target="tpu_custom_call" | custom-call | tf_op jit(solution)/shard_map/cond/branch_1_fun/combine/pallas_call | solution.py:235
  32.2 0.0 collective-permute-done.7.refs_0_
  32.2 0.0 collective-permute-done.9.refs_2_
  32.2 4.8 %all-to-all-start = ((bf16[16,14,16,128]{3,2,1,0:T(8,128)(2,1)}), bf16[16,14,16,128]{3,2,1,0:T(8,128)(2,1)S(1)}, u32[]{:S(2)}, u32[]{:S(2)}) async-start(bf16[16,14,16,128]{3,2,1,0:T(8,128)(2,1)} %after.1), calls=%async_computation | async-start | bytes 1835008 | tf_op jit(solution)/shard_map/all_to_all | solution.py:434
  37.1 17.5 %conditional.5 = (bf16[4,10,16,128]{3,2,1,0:T(8,128)(2,1)S(1)}, bf16[4,10,16,128]{3,2,1,0:T(8,128)(2,1)}, bf16[4,10,16,128]{3,2,1,0:T(8,128)(2,1)}, bf16[4,10,16,128]{3,2,1,0:T(8,128)(2,1)}) conditional(s32[]{:T(128)} %convert_element_type.2, () %tuple.30, (bf16[4,10,16,128]{3,2,1,0:T(8,128)(2,1)S(1)}, bf16[4,10,16,128]{3,2,1,0:T(8,128)(2,1)S(1)}, ...), branch_computations={%region_4.5_spmd, %region_5.6_spmd} | conditional | flops 16000000000 | bytes 1966232 | solution.py:407
  37.1 2.0 %collective-permute-start.3 = (bf16[4,10,16,128]{3,2,1,0:T(8,128)(2,1)S(1)}, bf16[4,10,16,128]{3,2,1,0:T(8,128)(2,1)}, u32[]{:S(2)}, u32[]{:S(2)}) collective-permute-start(bf16[4,10,16,128]{3,2,1,0:T(8,128)(2,1)S(1)} %get-tuple-element.67), channel_id=1, source_target_pairs={{0,1},{1,2},{2,3},{3,0},{4,5},{5,6},{6,7},{7,4},{8,9},{9,10},{10,1... | collective-permute-start | bytes 491528 | tf_op jit(solution)/shard_map/cond/branch_1_fun/ppermute | solution.py:422
  39.1 1.5 %collective-permute-start.4 = (bf16[4,10,16,128]{3,2,1,0:T(8,128)(2,1)S(1)}, bf16[4,10,16,128]{3,2,1,0:T(8,128)(2,1)}, u32[]{:S(2)}, u32[]{:S(2)}) collective-permute-start(bf16[4,10,16,128]{3,2,1,0:T(8,128)(2,1)S(1)} %get-tuple-element.68), channel_id=1, source_target_pairs={{0,2},{1,3},{2,0},{3,1},{4,6},{5,7},{6,4},{7,5},{8,10},{9,11},{10,... | collective-permute-start | bytes 491528 | tf_op jit(solution)/shard_map/cond/branch_1_fun/ppermute | solution.py:422
  40.6 1.5 %collective-permute-start.5 = (bf16[4,10,16,128]{3,2,1,0:T(8,128)(2,1)S(1)}, bf16[4,10,16,128]{3,2,1,0:T(8,128)(2,1)}, u32[]{:S(2)}, u32[]{:S(2)}) collective-permute-start(bf16[4,10,16,128]{3,2,1,0:T(8,128)(2,1)S(1)} %get-tuple-element.69), channel_id=1, source_target_pairs={{0,3},{1,0},{2,1},{3,2},{4,7},{5,4},{6,5},{7,6},{8,11},{9,8},{10,9... | collective-permute-start | bytes 491528 | tf_op jit(solution)/shard_map/cond/branch_1_fun/ppermute | solution.py:422
  42.0 11.8 %collective-permute-done.3 = bf16[4,10,16,128]{3,2,1,0:T(8,128)(2,1)} collective-permute-done((bf16[4,10,16,128]{3,2,1,0:T(8,128)(2,1)S(1)}, bf16[4,10,16,128]{3,2,1,0:T(8,128)(2,1)}, u32[]{:S(2)}, u32[]{:S(2)}) %collective-permute-start.3) | collective-permute-done | bytes 163872 | tf_op jit(solution)/shard_map/cond/branch_1_fun/ppermute | solution.py:422
  53.8 0.8 %collective-permute-done.4 = bf16[4,10,16,128]{3,2,1,0:T(8,128)(2,1)} collective-permute-done((bf16[4,10,16,128]{3,2,1,0:T(8,128)(2,1)S(1)}, bf16[4,10,16,128]{3,2,1,0:T(8,128)(2,1)}, u32[]{:S(2)}, u32[]{:S(2)}) %collective-permute-start.4) | collective-permute-done | bytes 163872 | tf_op jit(solution)/shard_map/cond/branch_1_fun/ppermute | solution.py:422
  54.6 0.0 collective-permute-done.5
  54.6 1.6 %settle.1.settled = bf16[3,2048,128]{2,1,0:T(8,128)(2,1)S(1)} custom-call(s32[5]{0:T(128)S(1)} %stack.31.place, bf16[4,10,16,128]{3,2,1,0:T(8,128)(2,1)S(1)} %get-tuple-element.82.refs_0_, bf16[4,10,16,128]{3,2,1,0:T(8,128)(2,1)} %get-tuple-element.83.refs_1_, bf16[4,10,16,128]{3,2,1,0:T(8,128)(2,1)} %get-tuple-element.84.refs_2_, ...), custom_call_target="tpu_custom_call" | custom-call | flops 1000000000 | tf_op jit(solution)/shard_map/settle/pallas_call | solution.py:315
  56.2 2.4 %all-to-all-done.view = bf16[16,14,16,128]{3,2,1,0:T(8,128)(2,1)S(1)} async-done(((bf16[16,14,16,128]{3,2,1,0:T(8,128)(2,1)}), bf16[16,14,16,128]{3,2,1,0:T(8,128)(2,1)S(1)}, u32[]{:S(2)}, u32[]{:S(2)}) %all-to-all-start) | async-done | bytes 917536 | tf_op jit(solution)/shard_map/all_to_all | solution.py:434
  58.6 1.5 %arrange.1 = bf16[3,2048,128]{2,1,0:T(8,128)(2,1)} custom-call(bf16[16,14,16,128]{3,2,1,0:T(8,128)(2,1)S(1)} %all-to-all-done.view, bf16[3,2048,128]{2,1,0:T(8,128)(2,1)S(1)} %settle.1.settled), custom_call_target="tpu_custom_call" | custom-call | tf_op jit(solution)/shard_map/arrange/pallas_call | solution.py:356
  (3 shorter events, 0.1 us)
Async XLA Ops:
  1.0 18.1 %collective-permute-start.6 = (bf16[3,1,256,256]{3,2,1,0:T(8,128)(2,1)S(1)}, bf16[3,1,256,256]{3,2,1,0:T(8,128)(2,1)S(1)}, u32[]{:S(2)}, u32[]{:S(2)}) collective-permute-start(bf16[3,1,256,256]{3,2,1,0:T(8,128)(2,1)S(1)} %constant_dynamic-slice_fusion), channel_id=1, source_target_pairs={{0,1},{1,2},{2,3},{3,4},{4,5},{5,6},{6,7},{7,8},{8,9},{9,10},{10,1... | collective-permute-start | bytes 1179656 | tf_op jit(solution)/shard_map/ppermute | solution.py:31
  10.4 2.2 %collective-permute-start = (bf16[10,256,128]{2,1,0:T(8,128)(2,1)S(1)}, bf16[10,256,128]{2,1,0:T(8,128)(2,1)S(1)}, u32[]{:S(2)}, u32[]{:S(2)}) collective-permute-start(bf16[10,256,128]{2,1,0:T(8,128)(2,1)S(1)} %get-tuple-element.51), channel_id=1, source_target_pairs={{0,16},{16,0},{1,17},{17,1},{2,18},{18,2},{3,19},{19,3},{4,20},{20... | collective-permute-start | bytes 1966088 | tf_op jit(solution)/shard_map/cond/branch_1_fun/ppermute | solution.py:35
  13.5 18.7 %collective-permute-start.7 = (bf16[4,10,16,128]{3,2,1,0:T(8,128)(2,1)S(1)}, bf16[4,10,16,128]{3,2,1,0:T(8,128)(2,1)S(1)}, u32[]{:S(2)}, u32[]{:S(2)}) collective-permute-start(bf16[4,10,16,128]{3,2,1,0:T(8,128)(2,1)S(1)} %get-tuple-element.79), channel_id=1, source_target_pairs={{0,4},{1,5},{2,6},{3,7},{4,8},{5,9},{6,10},{7,11},{8,12},{9,13},{1... | collective-permute-start | bytes 491528 | tf_op jit(solution)/shard_map/ppermute | solution.py:431
  15.1 17.0 %collective-permute-start.8 = (bf16[4,10,16,128]{3,2,1,0:T(8,128)(2,1)S(1)}, bf16[4,10,16,128]{3,2,1,0:T(8,128)(2,1)S(1)}, u32[]{:S(2)}, u32[]{:S(2)}) collective-permute-start(bf16[4,10,16,128]{3,2,1,0:T(8,128)(2,1)S(1)} %get-tuple-element.80), channel_id=1, source_target_pairs={{0,8},{1,9},{2,10},{3,11},{4,12},{5,13},{6,14},{7,15},{8,0},{9,1},... | collective-permute-start | bytes 491528 | tf_op jit(solution)/shard_map/ppermute | solution.py:431
  17.7 14.5 %collective-permute-start.9 = (bf16[4,10,16,128]{3,2,1,0:T(8,128)(2,1)S(1)}, bf16[4,10,16,128]{3,2,1,0:T(8,128)(2,1)S(1)}, u32[]{:S(2)}, u32[]{:S(2)}) collective-permute-start(bf16[4,10,16,128]{3,2,1,0:T(8,128)(2,1)S(1)} %get-tuple-element.81), channel_id=1, source_target_pairs={{0,12},{1,13},{2,14},{3,15},{4,0},{5,1},{6,2},{7,3},{8,4},{9,5},{1... | collective-permute-start | bytes 491528 | tf_op jit(solution)/shard_map/ppermute | solution.py:431
  19.1 1.7 %collective-permute-start.1 = (bf16[3,1,256,256]{3,2,1,0:T(8,128)(2,1)S(1)}, bf16[3,1,256,256]{3,2,1,0:T(8,128)(2,1)S(1)}, u32[]{:S(2)}, u32[]{:S(2)}) collective-permute-start(bf16[3,1,256,256]{3,2,1,0:T(8,128)(2,1)S(1)} %get-tuple-element.58.halo), channel_id=1, source_target_pairs={{0,16},{16,0},{1,17},{17,1},{2,18},{18,2},{3,19},{19,3},{4,20},{20... | collective-permute-start | bytes 1179656 | tf_op jit(solution)/shard_map/cond/branch_1_fun/ppermute | solution.py:35
  28.4 2.5 %collective-permute-start.2 = (bf16[14,256,128]{2,1,0:T(8,128)(2,1)S(1)}, bf16[14,256,128]{2,1,0:T(8,128)(2,1)S(1)}, u32[]{:S(2)}, u32[]{:S(2)}) collective-permute-start(bf16[14,256,128]{2,1,0:T(8,128)(2,1)S(1)} %get-tuple-element.61), channel_id=1, source_target_pairs={{0,16},{16,0},{1,17},{17,1},{2,18},{18,2},{3,19},{19,3},{4,20},{20... | collective-permute-start | bytes 2752520 | tf_op jit(solution)/shard_map/cond/branch_1_fun/ppermute | solution.py:35
  32.2 26.4 %all-to-all-start = ((bf16[16,14,16,128]{3,2,1,0:T(8,128)(2,1)}), bf16[16,14,16,128]{3,2,1,0:T(8,128)(2,1)S(1)}, u32[]{:S(2)}, u32[]{:S(2)}) async-start(bf16[16,14,16,128]{3,2,1,0:T(8,128)(2,1)} %after.1), calls=%async_computation | async-start | bytes 1835008 | tf_op jit(solution)/shard_map/all_to_all | solution.py:434
  37.1 16.7 %collective-permute-start.3 = (bf16[4,10,16,128]{3,2,1,0:T(8,128)(2,1)S(1)}, bf16[4,10,16,128]{3,2,1,0:T(8,128)(2,1)}, u32[]{:S(2)}, u32[]{:S(2)}) collective-permute-start(bf16[4,10,16,128]{3,2,1,0:T(8,128)(2,1)S(1)} %get-tuple-element.67), channel_id=1, source_target_pairs={{0,1},{1,2},{2,3},{3,0},{4,5},{5,6},{6,7},{7,4},{8,9},{9,10},{10,1... | collective-permute-start | bytes 491528 | tf_op jit(solution)/shard_map/cond/branch_1_fun/ppermute | solution.py:422
  39.1 15.5 %collective-permute-start.4 = (bf16[4,10,16,128]{3,2,1,0:T(8,128)(2,1)S(1)}, bf16[4,10,16,128]{3,2,1,0:T(8,128)(2,1)}, u32[]{:S(2)}, u32[]{:S(2)}) collective-permute-start(bf16[4,10,16,128]{3,2,1,0:T(8,128)(2,1)S(1)} %get-tuple-element.68), channel_id=1, source_target_pairs={{0,2},{1,3},{2,0},{3,1},{4,6},{5,7},{6,4},{7,5},{8,10},{9,11},{10,... | collective-permute-start | bytes 491528 | tf_op jit(solution)/shard_map/cond/branch_1_fun/ppermute | solution.py:422
  40.6 14.0 %collective-permute-start.5 = (bf16[4,10,16,128]{3,2,1,0:T(8,128)(2,1)S(1)}, bf16[4,10,16,128]{3,2,1,0:T(8,128)(2,1)}, u32[]{:S(2)}, u32[]{:S(2)}) collective-permute-start(bf16[4,10,16,128]{3,2,1,0:T(8,128)(2,1)S(1)} %get-tuple-element.69), channel_id=1, source_target_pairs={{0,3},{1,0},{2,1},{3,2},{4,7},{5,4},{6,5},{7,6},{8,11},{9,8},{10,9... | collective-permute-start | bytes 491528 | tf_op jit(solution)/shard_map/cond/branch_1_fun/ppermute | solution.py:422

commit v10 on v9

--- a/solution.py
+++ b/solution.py
@@ -250,13 +250,10 @@
     z, q = place[3], place[4]
     for a, out in enumerate(outs):
 
-        def body(b, carry, a=a, out=out):
+        for b in range(near):
             to = lax.rem(z + a, rows_of) * near + lax.rem(q + b, near)
             rows = pl.ds(pl.multiple_of(to * share, share), share)
             out[b] = (mine[:, rows, :].astype(F32) + other[:, rows, :].astype(F32)).astype(B16)
-            return carry
-
-        lax.fori_loop(0, near, body, 0)
 
 
 def blocks(place, mine, other, far, near):

time: 60.4 us -> 60.2 us (level)
  no operation moved by 1% of the time
where the time goes in v10:
time: 60.2 us; the launch traced here: 59.9 us
  waiting for transfers between devices  21.1 us (35%)
  Pallas kernels  18.9 us (31%)
  starting transfers between devices  18.6 us (31%)
  local copies, waits for them, and re-layouts  1.11 us (2%)
    pallas_call x2, Pallas kernels, products(): pl.pallas_call(functools.partial(kernel, early), out_shape=(out, out), in...  13.9 us
    ppermute x3, waiting for transfers between devices, near_steps(): pieces[b] = lax.ppermute(pieces[b], 'sec', steps)  12.6 us
    ppermute x3, waiting for transfers between devices, swap(): return lax.ppermute(value, 'op', [(0, 1), (1, 0)])  6.14 us
    ppermute x3, starting transfers between devices, per_device(): parts[a] = lax.ppermute(parts[a], 'sec', steps)  5.61 us
    ppermute x3, starting transfers between devices, near_steps(): pieces[b] = lax.ppermute(pieces[b], 'sec', steps)  4.89 us
    all_to_all x1, starting transfers between devices, per_device(): view = lax.all_to_all(owned, 'sec', split_axis=0, concat_axis=0, tiled=True)  4.84 us
    ppermute x1, starting transfers between devices, fetch(): return lax.ppermute(part, ('op', 'sec'), ahead + turns + back)  2.99 us
    all_to_all x1, waiting for transfers between devices, per_device(): view = lax.all_to_all(owned, 'sec', split_axis=0, concat_axis=0, tiled=True)  2.42 us
  transfers between devices with their start and end apart: 11, of which 6 were waited for; matrix products, arithmetic and copies ran while one was open for 0% of the time, Pallas kernels for 29%

profile of v10, /device:TPU:0, one launch (start us, length us, event | category | flops | bytes accessed | tf_op | source)
XLA Modules:
  0.0 59.9 jit_solution(3107017002335275297)
XLA Ops:
  0.0 1.0 %constant_dynamic-slice_fusion = bf16[3,1,256,256]{3,2,1,0:T(8,128)(2,1)S(1)} fusion(bf16[3,8,256,256]{3,2,1,0:T(8,128)(2,1)} %param.11, s32[]{:T(128)S(6)} %select_n.14), kind=kLoop, calls=%fused_computation | loop fusion | bytes 786436 | tf_op jit(solution)/shard_map/dynamic_slice | solution.py:30
  1.0 3.0 %collective-permute-start.6 = (bf16[3,1,256,256]{3,2,1,0:T(8,128)(2,1)S(1)}, bf16[3,1,256,256]{3,2,1,0:T(8,128)(2,1)S(1)}, u32[]{:S(2)}, u32[]{:S(2)}) collective-permute-start(bf16[3,1,256,256]{3,2,1,0:T(8,128)(2,1)S(1)} %constant_dynamic-slice_fusion), channel_id=1, source_target_pairs={{0,1},{1,2},{2,3},{3,4},{4,5},{5,6},{6,7},{7,8},{8,9},{9,10},{10,1... | collective-permute-start | bytes 1179656 | tf_op jit(solution)/shard_map/ppermute | solution.py:31
  4.0 0.1 stack.31.place
  4.1 9.2 %conditional.3 = ((bf16[4,10,16,128]{3,2,1,0:T(8,128)(2,1)S(1)}, bf16[4,10,16,128]{3,2,1,0:T(8,128)(2,1)S(1)}, bf16[4,10,16,128]{3,2,1,0:T(8,128)(2,1)S(1)}, bf16[4,10,16,128]{3,2,1,0:T(8,128)(2,1)S(1)})) conditional(s32[]{:T(128)} %convert_element_type.2, () %tuple.27, (s32[5]{0:T(128)S(1)}, s32[4]{0:T(128)}, s32[4,8]{1,0:T(4,128)}, ...), branch_computations={%region_0.1_spmd, %region_1.2_spmd} | conditional | flops 2684354560 | bytes 15204400 | solution.py:404
  4.1 6.3 %first_kernel.1 = (bf16[10,256,128]{2,1,0:T(8,128)(2,1)S(1)}, bf16[10,256,128]{2,1,0:T(8,128)(2,1)S(1)}) custom-call(s32[5]{0:T(128)S(1)} %get-tuple-element.44.me_ref.place, s32[4]{0:T(128)} %get-tuple-element.45.shifts, s32[4,8]{1,0:T(4,128)} %get-tuple-element.46.active, bf16[3,8,256,256]{3,2,1,0:T(8,128)(2,1)} %get-tuple-element.47.psi, ...), custom_call_target="tpu_custom_call" | custom-call | flops 2684354560 | bytes 12582912 | tf_op jit(solution)/shard_map/cond/branch_1_fun/first_kernel/pallas_call | solution.py:173
  10.4 0.1 collective-permute-start
  10.5 2.1 %collective-permute-done.other = bf16[10,256,128]{2,1,0:T(8,128)(2,1)S(1)} collective-permute-done((bf16[10,256,128]{2,1,0:T(8,128)(2,1)S(1)}, bf16[10,256,128]{2,1,0:T(8,128)(2,1)S(1)}, u32[]{:S(2)}, u32[]{:S(2)}) %collective-permute-start) | collective-permute-done | bytes 655392 | tf_op jit(solution)/shard_map/cond/branch_1_fun/ppermute | solution.py:35
  12.6 0.7 %blocks.1 = (bf16[4,10,16,128]{3,2,1,0:T(8,128)(2,1)S(1)}, bf16[4,10,16,128]{3,2,1,0:T(8,128)(2,1)S(1)}, bf16[4,10,16,128]{3,2,1,0:T(8,128)(2,1)S(1)}, bf16[4,10,16,128]{3,2,1,0:T(8,128)(2,1)S(1)}) custom-call(s32[5]{0:T(128)S(1)} %get-tuple-element.44.me_ref.place, bf16[10,256,128]{2,1,0:T(8,128)(2,1)S(1)} %get-tuple-element.50.mine, ...), custom_call_target="tpu_custom_call" | custom-call | tf_op jit(solution)/shard_map/cond/branch_1_fun/blocks/pallas_call | solution.py:263
  13.3 1.7 %collective-permute-start.7 = (bf16[4,10,16,128]{3,2,1,0:T(8,128)(2,1)S(1)}, bf16[4,10,16,128]{3,2,1,0:T(8,128)(2,1)S(1)}, u32[]{:S(2)}, u32[]{:S(2)}) collective-permute-start(bf16[4,10,16,128]{3,2,1,0:T(8,128)(2,1)S(1)} %get-tuple-element.79), channel_id=1, source_target_pairs={{0,4},{1,5},{2,6},{3,7},{4,8},{5,9},{6,10},{7,11},{8,12},{9,13},{1... | collective-permute-start | bytes 491528 | tf_op jit(solution)/shard_map/ppermute | solution.py:428
  15.0 2.6 %collective-permute-start.8 = (bf16[4,10,16,128]{3,2,1,0:T(8,128)(2,1)S(1)}, bf16[4,10,16,128]{3,2,1,0:T(8,128)(2,1)S(1)}, u32[]{:S(2)}, u32[]{:S(2)}) collective-permute-start(bf16[4,10,16,128]{3,2,1,0:T(8,128)(2,1)S(1)} %get-tuple-element.80), channel_id=1, source_target_pairs={{0,8},{1,9},{2,10},{3,11},{4,12},{5,13},{6,14},{7,15},{8,0},{9,1},... | collective-permute-start | bytes 491528 | tf_op jit(solution)/shard_map/ppermute | solution.py:428
  17.6 1.4 %collective-permute-start.9 = (bf16[4,10,16,128]{3,2,1,0:T(8,128)(2,1)S(1)}, bf16[4,10,16,128]{3,2,1,0:T(8,128)(2,1)S(1)}, u32[]{:S(2)}, u32[]{:S(2)}) collective-permute-start(bf16[4,10,16,128]{3,2,1,0:T(8,128)(2,1)S(1)} %get-tuple-element.81), channel_id=1, source_target_pairs={{0,12},{1,13},{2,14},{3,15},{4,0},{5,1},{6,2},{7,3},{8,4},{9,5},{1... | collective-permute-start | bytes 491528 | tf_op jit(solution)/shard_map/ppermute | solution.py:428
  18.9 0.0 collective-permute-done.6
  18.9 13.1 %conditional.4 = (bf16[16,14,16,128]{3,2,1,0:T(8,128)(2,1)}) conditional(s32[]{:T(128)} %convert_element_type.2, () %tuple.26, (bf16[3,1,256,256]{3,2,1,0:T(8,128)(2,1)S(1)}, s32[5]{0:T(128)S(1)}, s32[4]{0:T(128)}, s32[4,8]{1,0:T(4,128)}, bf16[3,8,256,256]{3,2,1,0:T(8,128)(2,1)}, /*index=5*/bf16[4,8,256,256]{3,2,1,0:T(8,128)(2,1)}, ...), branch_computations={%region_2.3_spmd, %region_3.4_spmd} | conditional | flops 3758096384 | bytes 17825880 | solution.py:404
  18.9 0.0 collective-permute-start.1
  18.9 1.7 %collective-permute-done.1.other = bf16[3,1,256,256]{3,2,1,0:T(8,128)(2,1)S(1)} collective-permute-done((bf16[3,1,256,256]{3,2,1,0:T(8,128)(2,1)S(1)}, bf16[3,1,256,256]{3,2,1,0:T(8,128)(2,1)S(1)}, u32[]{:S(2)}, u32[]{:S(2)}) %collective-permute-start.1) | collective-permute-done | bytes 393248 | tf_op jit(solution)/shard_map/cond/branch_1_fun/ppermute | solution.py:35
  20.6 7.6 %second_kernel.1 = (bf16[14,256,128]{2,1,0:T(8,128)(2,1)S(1)}, bf16[14,256,128]{2,1,0:T(8,128)(2,1)S(1)}) custom-call(s32[5]{0:T(128)S(1)} %get-tuple-element.52.me_ref, s32[4]{0:T(128)} %get-tuple-element.53.shifts, s32[4,8]{1,0:T(4,128)} %get-tuple-element.54.active, bf16[3,8,256,256]{3,2,1,0:T(8,128)(2,1)} %get-tuple-element.55.psi, ...), custom_call_target="tpu_custom_call" | custom-call | flops 3758096384 | bytes 12582912 | tf_op jit(solution)/shard_map/cond/branch_1_fun/second_kernel/pallas_call | solution.py:173
  28.3 0.2 collective-permute-start.2
  28.5 2.3 %collective-permute-done.2.refs_1_ = bf16[14,256,128]{2,1,0:T(8,128)(2,1)S(1)} collective-permute-done((bf16[14,256,128]{2,1,0:T(8,128)(2,1)S(1)}, bf16[14,256,128]{2,1,0:T(8,128)(2,1)S(1)}, u32[]{:S(2)}, u32[]{:S(2)}) %collective-permute-start.2) | collective-permute-done | bytes 917536 | tf_op jit(solution)/shard_map/cond/branch_1_fun/ppermute | solution.py:35
  30.8 1.2 %combine.1 = bf16[16,14,16,128]{3,2,1,0:T(8,128)(2,1)} custom-call(bf16[14,256,128]{2,1,0:T(8,128)(2,1)S(1)} %get-tuple-element.60.refs_0_, bf16[14,256,128]{2,1,0:T(8,128)(2,1)S(1)} %collective-permute-done.2.refs_1_), custom_call_target="tpu_custom_call" | custom-call | tf_op jit(solution)/shard_map/cond/branch_1_fun/combine/pallas_call | solution.py:235
  32.0 0.0 collective-permute-done.7.refs_0_
  32.0 0.0 collective-permute-done.8.refs_1_
  32.0 0.0 collective-permute-done.9.refs_2_
  32.0 4.8 %all-to-all-start = ((bf16[16,14,16,128]{3,2,1,0:T(8,128)(2,1)}), bf16[16,14,16,128]{3,2,1,0:T(8,128)(2,1)S(1)}, u32[]{:S(2)}, u32[]{:S(2)}) async-start(bf16[16,14,16,128]{3,2,1,0:T(8,128)(2,1)} %after.1), calls=%async_computation | async-start | bytes 1835008 | tf_op jit(solution)/shard_map/all_to_all | solution.py:431
  36.9 17.5 %conditional.5 = (bf16[4,10,16,128]{3,2,1,0:T(8,128)(2,1)S(1)}, bf16[4,10,16,128]{3,2,1,0:T(8,128)(2,1)}, bf16[4,10,16,128]{3,2,1,0:T(8,128)(2,1)}, bf16[4,10,16,128]{3,2,1,0:T(8,128)(2,1)}) conditional(s32[]{:T(128)} %convert_element_type.2, () %tuple.30, (bf16[4,10,16,128]{3,2,1,0:T(8,128)(2,1)S(1)}, bf16[4,10,16,128]{3,2,1,0:T(8,128)(2,1)S(1)}, ...), branch_computations={%region_4.5_spmd, %region_5.6_spmd} | conditional | flops 16000000000 | bytes 1966232 | solution.py:404
  37.0 2.0 %collective-permute-start.3 = (bf16[4,10,16,128]{3,2,1,0:T(8,128)(2,1)S(1)}, bf16[4,10,16,128]{3,2,1,0:T(8,128)(2,1)}, u32[]{:S(2)}, u32[]{:S(2)}) collective-permute-start(bf16[4,10,16,128]{3,2,1,0:T(8,128)(2,1)S(1)} %get-tuple-element.67), channel_id=1, source_target_pairs={{0,1},{1,2},{2,3},{3,0},{4,5},{5,6},{6,7},{7,4},{8,9},{9,10},{10,1... | collective-permute-start | bytes 491528 | tf_op jit(solution)/shard_map/cond/branch_1_fun/ppermute | solution.py:419
  38.9 1.5 %collective-permute-start.4 = (bf16[4,10,16,128]{3,2,1,0:T(8,128)(2,1)S(1)}, bf16[4,10,16,128]{3,2,1,0:T(8,128)(2,1)}, u32[]{:S(2)}, u32[]{:S(2)}) collective-permute-start(bf16[4,10,16,128]{3,2,1,0:T(8,128)(2,1)S(1)} %get-tuple-element.68), channel_id=1, source_target_pairs={{0,2},{1,3},{2,0},{3,1},{4,6},{5,7},{6,4},{7,5},{8,10},{9,11},{10,... | collective-permute-start | bytes 491528 | tf_op jit(solution)/shard_map/cond/branch_1_fun/ppermute | solution.py:419
  40.4 1.5 %collective-permute-start.5 = (bf16[4,10,16,128]{3,2,1,0:T(8,128)(2,1)S(1)}, bf16[4,10,16,128]{3,2,1,0:T(8,128)(2,1)}, u32[]{:S(2)}, u32[]{:S(2)}) collective-permute-start(bf16[4,10,16,128]{3,2,1,0:T(8,128)(2,1)S(1)} %get-tuple-element.69), channel_id=1, source_target_pairs={{0,3},{1,0},{2,1},{3,2},{4,7},{5,4},{6,5},{7,6},{8,11},{9,8},{10,9... | collective-permute-start | bytes 491528 | tf_op jit(solution)/shard_map/cond/branch_1_fun/ppermute | solution.py:419
  41.9 11.8 %collective-permute-done.3 = bf16[4,10,16,128]{3,2,1,0:T(8,128)(2,1)} collective-permute-done((bf16[4,10,16,128]{3,2,1,0:T(8,128)(2,1)S(1)}, bf16[4,10,16,128]{3,2,1,0:T(8,128)(2,1)}, u32[]{:S(2)}, u32[]{:S(2)}) %collective-permute-start.3) | collective-permute-done | bytes 163872 | tf_op jit(solution)/shard_map/cond/branch_1_fun/ppermute | solution.py:419
  53.7 0.8 %collective-permute-done.4 = bf16[4,10,16,128]{3,2,1,0:T(8,128)(2,1)} collective-permute-done((bf16[4,10,16,128]{3,2,1,0:T(8,128)(2,1)S(1)}, bf16[4,10,16,128]{3,2,1,0:T(8,128)(2,1)}, u32[]{:S(2)}, u32[]{:S(2)}) %collective-permute-start.4) | collective-permute-done | bytes 163872 | tf_op jit(solution)/shard_map/cond/branch_1_fun/ppermute | solution.py:419
  54.4 1.6 %settle.1.settled = bf16[3,2048,128]{2,1,0:T(8,128)(2,1)S(1)} custom-call(s32[5]{0:T(128)S(1)} %stack.31.place, bf16[4,10,16,128]{3,2,1,0:T(8,128)(2,1)S(1)} %get-tuple-element.82.refs_0_, bf16[4,10,16,128]{3,2,1,0:T(8,128)(2,1)} %get-tuple-element.83.refs_1_, bf16[4,10,16,128]{3,2,1,0:T(8,128)(2,1)} %get-tuple-element.84.refs_2_, ...), custom_call_target="tpu_custom_call" | custom-call | flops 1000000000 | tf_op jit(solution)/shard_map/settle/pallas_call | solution.py:312
  56.0 2.4 %all-to-all-done.view = bf16[16,14,16,128]{3,2,1,0:T(8,128)(2,1)S(1)} async-done(((bf16[16,14,16,128]{3,2,1,0:T(8,128)(2,1)}), bf16[16,14,16,128]{3,2,1,0:T(8,128)(2,1)S(1)}, u32[]{:S(2)}, u32[]{:S(2)}) %all-to-all-start) | async-done | bytes 917536 | tf_op jit(solution)/shard_map/all_to_all | solution.py:431
  58.4 1.5 %arrange.1 = bf16[3,2048,128]{2,1,0:T(8,128)(2,1)} custom-call(bf16[16,14,16,128]{3,2,1,0:T(8,128)(2,1)S(1)} %all-to-all-done.view, bf16[3,2048,128]{2,1,0:T(8,128)(2,1)S(1)} %settle.1.settled), custom_call_target="tpu_custom_call" | custom-call | tf_op jit(solution)/shard_map/arrange/pallas_call | solution.py:353
  (3 shorter events, 0.1 us)
Async XLA Ops:
  1.0 17.9 %collective-permute-start.6 = (bf16[3,1,256,256]{3,2,1,0:T(8,128)(2,1)S(1)}, bf16[3,1,256,256]{3,2,1,0:T(8,128)(2,1)S(1)}, u32[]{:S(2)}, u32[]{:S(2)}) collective-permute-start(bf16[3,1,256,256]{3,2,1,0:T(8,128)(2,1)S(1)} %constant_dynamic-slice_fusion), channel_id=1, source_target_pairs={{0,1},{1,2},{2,3},{3,4},{4,5},{5,6},{6,7},{7,8},{8,9},{9,10},{10,1... | collective-permute-start | bytes 1179656 | tf_op jit(solution)/shard_map/ppermute | solution.py:31
  10.4 2.2 %collective-permute-start = (bf16[10,256,128]{2,1,0:T(8,128)(2,1)S(1)}, bf16[10,256,128]{2,1,0:T(8,128)(2,1)S(1)}, u32[]{:S(2)}, u32[]{:S(2)}) collective-permute-start(bf16[10,256,128]{2,1,0:T(8,128)(2,1)S(1)} %get-tuple-element.51), channel_id=1, source_target_pairs={{0,16},{16,0},{1,17},{17,1},{2,18},{18,2},{3,19},{19,3},{4,20},{20... | collective-permute-start | bytes 1966088 | tf_op jit(solution)/shard_map/cond/branch_1_fun/ppermute | solution.py:35
  13.3 18.7 %collective-permute-start.7 = (bf16[4,10,16,128]{3,2,1,0:T(8,128)(2,1)S(1)}, bf16[4,10,16,128]{3,2,1,0:T(8,128)(2,1)S(1)}, u32[]{:S(2)}, u32[]{:S(2)}) collective-permute-start(bf16[4,10,16,128]{3,2,1,0:T(8,128)(2,1)S(1)} %get-tuple-element.79), channel_id=1, source_target_pairs={{0,4},{1,5},{2,6},{3,7},{4,8},{5,9},{6,10},{7,11},{8,12},{9,13},{1... | collective-permute-start | bytes 491528 | tf_op jit(solution)/shard_map/ppermute | solution.py:428
  15.0 17.0 %collective-permute-start.8 = (bf16[4,10,16,128]{3,2,1,0:T(8,128)(2,1)S(1)}, bf16[4,10,16,128]{3,2,1,0:T(8,128)(2,1)S(1)}, u32[]{:S(2)}, u32[]{:S(2)}) collective-permute-start(bf16[4,10,16,128]{3,2,1,0:T(8,128)(2,1)S(1)} %get-tuple-element.80), channel_id=1, source_target_pairs={{0,8},{1,9},{2,10},{3,11},{4,12},{5,13},{6,14},{7,15},{8,0},{9,1},... | collective-permute-start | bytes 491528 | tf_op jit(solution)/shard_map/ppermute | solution.py:428
  17.6 14.5 %collective-permute-start.9 = (bf16[4,10,16,128]{3,2,1,0:T(8,128)(2,1)S(1)}, bf16[4,10,16,128]{3,2,1,0:T(8,128)(2,1)S(1)}, u32[]{:S(2)}, u32[]{:S(2)}) collective-permute-start(bf16[4,10,16,128]{3,2,1,0:T(8,128)(2,1)S(1)} %get-tuple-element.81), channel_id=1, source_target_pairs={{0,12},{1,13},{2,14},{3,15},{4,0},{5,1},{6,2},{7,3},{8,4},{9,5},{1... | collective-permute-start | bytes 491528 | tf_op jit(solution)/shard_map/ppermute | solution.py:428
  18.9 1.7 %collective-permute-start.1 = (bf16[3,1,256,256]{3,2,1,0:T(8,128)(2,1)S(1)}, bf16[3,1,256,256]{3,2,1,0:T(8,128)(2,1)S(1)}, u32[]{:S(2)}, u32[]{:S(2)}) collective-permute-start(bf16[3,1,256,256]{3,2,1,0:T(8,128)(2,1)S(1)} %get-tuple-element.58.halo), channel_id=1, source_target_pairs={{0,16},{16,0},{1,17},{17,1},{2,18},{18,2},{3,19},{19,3},{4,20},{20... | collective-permute-start | bytes 1179656 | tf_op jit(solution)/shard_map/cond/branch_1_fun/ppermute | solution.py:35
  28.3 2.5 %collective-permute-start.2 = (bf16[14,256,128]{2,1,0:T(8,128)(2,1)S(1)}, bf16[14,256,128]{2,1,0:T(8,128)(2,1)S(1)}, u32[]{:S(2)}, u32[]{:S(2)}) collective-permute-start(bf16[14,256,128]{2,1,0:T(8,128)(2,1)S(1)} %get-tuple-element.61), channel_id=1, source_target_pairs={{0,16},{16,0},{1,17},{17,1},{2,18},{18,2},{3,19},{19,3},{4,20},{20... | collective-permute-start | bytes 2752520 | tf_op jit(solution)/shard_map/cond/branch_1_fun/ppermute | solution.py:35
  32.0 26.4 %all-to-all-start = ((bf16[16,14,16,128]{3,2,1,0:T(8,128)(2,1)}), bf16[16,14,16,128]{3,2,1,0:T(8,128)(2,1)S(1)}, u32[]{:S(2)}, u32[]{:S(2)}) async-start(bf16[16,14,16,128]{3,2,1,0:T(8,128)(2,1)} %after.1), calls=%async_computation | async-start | bytes 1835008 | tf_op jit(solution)/shard_map/all_to_all | solution.py:431
  37.0 16.7 %collective-permute-start.3 = (bf16[4,10,16,128]{3,2,1,0:T(8,128)(2,1)S(1)}, bf16[4,10,16,128]{3,2,1,0:T(8,128)(2,1)}, u32[]{:S(2)}, u32[]{:S(2)}) collective-permute-start(bf16[4,10,16,128]{3,2,1,0:T(8,128)(2,1)S(1)} %get-tuple-element.67), channel_id=1, source_target_pairs={{0,1},{1,2},{2,3},{3,0},{4,5},{5,6},{6,7},{7,4},{8,9},{9,10},{10,1... | collective-permute-start | bytes 491528 | tf_op jit(solution)/shard_map/cond/branch_1_fun/ppermute | solution.py:419
  38.9 15.5 %collective-permute-start.4 = (bf16[4,10,16,128]{3,2,1,0:T(8,128)(2,1)S(1)}, bf16[4,10,16,128]{3,2,1,0:T(8,128)(2,1)}, u32[]{:S(2)}, u32[]{:S(2)}) collective-permute-start(bf16[4,10,16,128]{3,2,1,0:T(8,128)(2,1)S(1)} %get-tuple-element.68), channel_id=1, source_target_pairs={{0,2},{1,3},{2,0},{3,1},{4,6},{5,7},{6,4},{7,5},{8,10},{9,11},{10,... | collective-permute-start | bytes 491528 | tf_op jit(solution)/shard_map/cond/branch_1_fun/ppermute | solution.py:419
  40.4 14.0 %collective-permute-start.5 = (bf16[4,10,16,128]{3,2,1,0:T(8,128)(2,1)S(1)}, bf16[4,10,16,128]{3,2,1,0:T(8,128)(2,1)}, u32[]{:S(2)}, u32[]{:S(2)}) collective-permute-start(bf16[4,10,16,128]{3,2,1,0:T(8,128)(2,1)S(1)} %get-tuple-element.69), channel_id=1, source_target_pairs={{0,3},{1,0},{2,1},{3,2},{4,7},{5,4},{6,5},{7,6},{8,11},{9,8},{10,9... | collective-permute-start | bytes 491528 | tf_op jit(solution)/shard_map/cond/branch_1_fun/ppermute | solution.py:419
